TPU v7x, 32 devices: a whole 2x2x4 slice. The times are simulated.
32 devices in a mesh: dp: 8 (over y, x, core), seq: 4 (over z).
Axes of the slice: x: 2, y: 2, z: 4, core: 2. Of those that a mesh axis runs over, the one named last changes fastest.
Arguments:
- queries: bfloat16 [4096, 2048], P(('dp', 'seq')), may hold values from -6 to 6
- keys: bfloat16 [4096, 2048], P(('dp', 'seq')), may hold values from -6 to 6
- values: bfloat16 [4096, 2048], P(('dp', 'seq')), may hold values from -6 to 6
- text_kv: bfloat16 [64, 256, 2, 2048], P('dp', None, None, 'seq'), may hold values from -6 to 6
- text_lengths: int32 [64], P('dp'), may hold values from 1 to 256
- clip_lengths: int32 [8, 8], P('dp'), may hold values from 1 to 128, 512 in all within a row
- timesteps: int32 [64], P('dp'), may hold values from 0 to 999
- mod_weight: bfloat16 [256, 4096], replicated, may hold values from -0.375 to 0.375
- final_weight: bfloat16 [2048, 64], replicated, may hold values from -0.125 to 0.125
- noise: float32 [4096, 64], P(('dp', 'seq')), may hold values from -6 to 6
- clean: float32 [4096, 64], P(('dp', 'seq')), may hold values from -12 to 12
- report_order: int32 [64], P('dp'), may hold values from 0 to 63, each once
Outputs:
- scores: float32 [64], P('dp')
Inputs may be any that keep to these rules, and one draw needn't show every extreme that they name: Each row of clip_lengths sums to 512, and its largest entry is exactly 128.
All inputs are finite; a program needn't handle non-finite values.
Results may differ from a plain program's by a relative error of at most 0.00055.
Values may be sent and summed in bfloat16 or wider, within the bound.
No kernel may reach another device: no remote copies, remote signals or barrier semaphores. Data moves between devices by JAX's collectives and lax.ppermute only.
A program may use at most 128 MiB of HBM per device.

v0:
```python
import math

import jax
import jax.numpy as jnp
from jax import lax
from jax.sharding import PartitionSpec as P

HEAD_DIM = 128
FREQ = 256


eps_norm = 1e-06


def step_embedding(timesteps):
    half_width = FREQ // 2
    frequency = jnp.exp(-math.log(10000.0) * jnp.arange(half_width, dtype=jnp.float32) / half_width)
    angles = timesteps.astype(jnp.float32)[:, None] * frequency[None, :]
    return jnp.concatenate([jnp.cos(angles), jnp.sin(angles)], axis=1)


def clip_index(lengths, row_total):
    clip_ends = jnp.cumsum(lengths)
    places = jnp.arange(row_total, dtype=jnp.int32)
    return jnp.sum((places[:, None] >= clip_ends[None, :]).astype(jnp.int32), axis=1)


def attend_block(query_block, key_rows, value_rows, live_mask):
    row_count = query_block.shape[0]
    heads_here = query_block.shape[1] // HEAD_DIM
    query_split = query_block.reshape(row_count, heads_here, HEAD_DIM)
    key_split = key_rows.reshape(key_rows.shape[0], heads_here, HEAD_DIM)
    value_split = value_rows.reshape(value_rows.shape[0], heads_here, HEAD_DIM)
    score_rows = jnp.einsum(
        "qhd,khd->hqk", query_split, key_split, preferred_element_type=jnp.float32
    ) * (1.0 / math.sqrt(HEAD_DIM))
    score_rows = jnp.where(live_mask[None], score_rows, -jnp.inf)
    row_top = jnp.max(score_rows, axis=2, keepdims=True)
    weights = jnp.exp(score_rows - row_top)
    weights = (weights / jnp.sum(weights, axis=2, keepdims=True)).astype(jnp.bfloat16)
    mixed_out = jnp.einsum("hqk,khd->qhd", weights, value_split, preferred_element_type=jnp.float32)
    return mixed_out.reshape(row_count, heads_here * HEAD_DIM).astype(jnp.bfloat16)


def per_device(
    queries,
    keys,
    values,
    text_kv,
    text_lengths,
    clip_lengths,
    timesteps,
    mod_weight,
    final_weight,
    noise,
    clean,
    report_order,
):
    tok_dev = queries.shape[0]
    feat_width = queries.shape[1]
    seq_count = lax.axis_size("seq")
    seq_rank = lax.axis_index("seq")
    query_heads, key_heads, value_heads = (
        lax.all_to_all(queries, "seq", split_axis=1, concat_axis=0, tiled=True),
        lax.all_to_all(keys, "seq", split_axis=1, concat_axis=0, tiled=True),
        lax.all_to_all(values, "seq", split_axis=1, concat_axis=0, tiled=True),
    )
    group_rows = tok_dev * seq_count
    local_width = query_heads.shape[1]
    block_rows = min(512, group_rows)
    lengths = clip_lengths[0]
    clips_here = lengths.shape[0]
    clip_of = clip_index(lengths, group_rows)
    clip_slots = jnp.arange(clips_here, dtype=jnp.int32)
    text_len = text_kv.shape[1]
    text_slots = jnp.arange(clips_here * text_len, dtype=jnp.int32)
    text_clip = text_slots // text_len
    text_live = text_slots % text_len < text_lengths[text_clip]
    text_keys = text_kv[:, :, 0, :].reshape(clips_here * text_len, local_width)
    text_values = text_kv[:, :, 1, :].reshape(clips_here * text_len, local_width)

    def one_block(block_index):
        first_row = block_index * block_rows
        query_block = lax.dynamic_slice_in_dim(query_heads, first_row, block_rows, 0)
        block_clip = lax.dynamic_slice_in_dim(clip_of, first_row, block_rows, 0)
        live_mask = jnp.concatenate(
            [
                block_clip[:, None] == clip_of[None, :],
                (block_clip[:, None] == text_clip[None, :]) & text_live[None, :],
            ],
            axis=1,
        )
        return attend_block(
            query_block,
            jnp.concatenate([key_heads, text_keys], axis=0),
            jnp.concatenate([value_heads, text_values], axis=0),
            live_mask,
        )

    attended = lax.map(one_block, jnp.arange(group_rows // block_rows, dtype=jnp.int32)).reshape(
        group_rows, local_width
    )
    activated = jax.nn.silu(step_embedding(timesteps)).astype(jnp.bfloat16)
    modulation = jnp.dot(activated, mod_weight, preferred_element_type=jnp.float32)
    tok_clip = lax.dynamic_slice_in_dim(clip_of, seq_rank * tok_dev, tok_dev, 0)
    token_picks = (tok_clip[:, None] == clip_slots[None, :]).astype(jnp.float32)
    gathered = lax.all_to_all(attended, "seq", split_axis=0, concat_axis=1, tiled=True)
    tok_mods = jnp.dot(token_picks, modulation, precision=lax.Precision.HIGHEST)
    values_full = gathered.astype(jnp.float32)
    center = jnp.mean(values_full, axis=1, keepdims=True)
    spread = jnp.mean(values_full * values_full, axis=1, keepdims=True) - center * center
    normed = (values_full - center) * lax.rsqrt(spread + eps_norm)
    modulated = normed * (1.0 + tok_mods[:, feat_width:]) + tok_mods[:, :feat_width]
    predicted = jnp.dot(
        modulated, final_weight.astype(jnp.float32), precision=lax.Precision.HIGHEST
    )
    difference = predicted - (noise - clean)
    error_rows = jnp.mean(difference * difference, axis=1)
    clip_partial = jnp.sum(token_picks * error_rows[:, None], axis=0)
    clip_sizes = lengths.astype(jnp.float32)
    clip_totals = lax.psum(clip_partial, "seq")
    all_losses = lax.all_gather(clip_totals / clip_sizes, "dp", axis=0, tiled=True)
    loss_slots = jnp.arange(all_losses.shape[0], dtype=jnp.int32)
    return jnp.sum(
        jnp.where(report_order[:, None] == loss_slots[None, :], all_losses[None, :], 0.0), axis=1
    )


def solution(mesh):
    in_specs = (
        P(("dp", "seq"), None),
        P(("dp", "seq"), None),
        P(("dp", "seq"), None),
        P("dp", None, None, "seq"),
        P("dp"),
        P("dp", None),
        P("dp"),
        P(),
        P(),
        P(("dp", "seq"), None),
        P(("dp", "seq"), None),
        P("dp"),
    )
    out_specs = P("dp")
    return jax.shard_map(
        per_device, mesh=mesh, in_specs=in_specs, out_specs=out_specs, check_vma=False
    )
```

profile of v0, /device:TPU:0, one launch (start us, length us, event | category | flops | bytes accessed | tf_op | source)
XLA Modules:
  0.0 179.5 jit_solution(1945307539956390578)
XLA Ops:
  0.0 2.1 %copy.63 = bf16[16,4,8,512]{3,2,0,1:T(8,128)(2,1)} copy(bf16[16,4,8,512]{3,2,1,0:T(8,128)(2,1)} %bitcast.54) | data formatting | bytes 1048576 | tf_op jit(solution)/shard_map/all_to_all | solution.py:65
  2.1 6.3 %all-to-all-start.1 = ((bf16[128,4,512]{2,0,1:T(8,128)(2,1)}), bf16[128,4,512]{2,0,1:T(8,128)(2,1)S(1)}, u32[]{:S(2)}, u32[]{:S(2)}) async-start(bf16[128,4,512]{2,0,1:T(8,128)(2,1)} %bitcast.50), calls=%async_computation.1 | async-start | bytes 1048576 | tf_op jit(solution)/shard_map/all_to_all | solution.py:65
  8.4 21.6 %slice_reduce_fusion.1 = (bf16[8,256,512]{2,1,0:T(8,128)(2,1)}, bf16[8,256,512]{2,1,0:T(8,128)(2,1)}) fusion(bf16[8,256,2,512]{3,2,1,0:T(2,128)(2,1)} %param.15), kind=kLoop, calls=%fused_computation.11 | loop fusion | bytes 8388608 | tf_op jit(solution)/shard_map/slice | solution.py:80
  30.0 4.0 %reshape.220 = bf16[2048,4,128]{2,1,0:T(4,128)(2,1)} reshape(bf16[8,256,512]{2,1,0:T(8,128)(2,1)} %get-tuple-element.24) | data formatting | bytes 4194304 | tf_op jit(solution)/shard_map/while/body/eval_jaxpr/concatenate | solution.py:95
  34.0 3.2 %copy.45 = bf16[2048,4,128]{2,0,1:T(8,128)(2,1)} copy(bf16[2048,4,128]{2,1,0:T(4,128)(2,1)} %reshape.220) | data formatting | bytes 4194304 | tf_op jit(solution)/shard_map/while/body/eval_jaxpr/concatenate | solution.py:95
  38.0 4.0 %reshape.219 = bf16[2048,4,128]{2,1,0:T(4,128)(2,1)} reshape(bf16[8,256,512]{2,1,0:T(8,128)(2,1)} %get-tuple-element.23) | data formatting | bytes 4194304 | tf_op jit(solution)/shard_map/while/body/eval_jaxpr/concatenate | solution.py:96
  42.1 4.4 %copy.52 = bf16[2048,4,128]{0,2,1:T(8,128)(2,1)} copy(bf16[2048,4,128]{2,1,0:T(4,128)(2,1)} %reshape.219) | data formatting | bytes 4194304 | tf_op jit(solution)/shard_map/while/body/eval_jaxpr/concatenate | solution.py:96
  46.5 1.0 copy.39
  48.5 5.1 %all-to-all-start.2 = ((bf16[128,4,512]{2,0,1:T(8,128)(2,1)}), bf16[128,4,512]{2,0,1:T(8,128)(2,1)S(1)}, u32[]{:S(2)}, u32[]{:S(2)}) async-start(bf16[128,4,512]{2,0,1:T(8,128)(2,1)} %bitcast.49), calls=%async_computation.2 | async-start | bytes 1048576 | tf_op jit(solution)/shard_map/all_to_all | solution.py:64
  53.6 4.5 %compare_select_fusion.1 = s32[2048,1]{0,1:T(1,128)S(1)} fusion(s32[]{:T(128)} %bitcast.5, s32[]{:T(128)} %bitcast.6, s32[]{:T(128)} %bitcast.7, s32[]{:T(128)} %bitcast.8, s32[]{:T(128)} %bitcast.9, s32[]{:T(128)} %bitcast.11, s32[]{:T(128)} %bitcast.10), kind=kLoop, calls=%fused_computation.41 | loop fusion | flops 47104 | bytes 8220 | tf_op jit(solution)/shard_map/gather | solution.py:78
  58.9 8.6 %all-to-all-done.2 = bf16[128,4,512]{2,0,1:T(8,128)(2,1)S(1)} async-done(((bf16[128,4,512]{2,0,1:T(8,128)(2,1)}), bf16[128,4,512]{2,0,1:T(8,128)(2,1)S(1)}, u32[]{:S(2)}, u32[]{:S(2)}) %all-to-all-start.2) | async-done | bytes 524320 | tf_op jit(solution)/shard_map/all_to_all | solution.py:64
  67.5 4.3 %all-to-all-start = ((bf16[128,4,512]{0,2,1:T(8,128)(2,1)}), bf16[128,4,512]{0,2,1:T(8,128)(2,1)}, u32[]{:S(2)}, u32[]{:S(2)}) async-start(bf16[128,4,512]{0,2,1:T(8,128)(2,1)} %bitcast.2), calls=%async_computation | async-start | bytes 1048576 | tf_op jit(solution)/shard_map/all_to_all | solution.py:66
  71.8 1.5 compare_and_fusion
  73.4 1.5 pad_add_fusion
  74.9 0.9 concatenate.29
  75.8 1.1 copy.44
  77.0 1.2 reshape.168
  78.1 7.5 %all-to-all-done = bf16[128,4,512]{0,2,1:T(8,128)(2,1)} async-done(((bf16[128,4,512]{0,2,1:T(8,128)(2,1)}), bf16[128,4,512]{0,2,1:T(8,128)(2,1)}, u32[]{:S(2)}, u32[]{:S(2)}) %all-to-all-start) | async-done | bytes 524320 | tf_op jit(solution)/shard_map/all_to_all | solution.py:66
  85.7 2.2 %copy.40 = bf16[4,128,512]{1,0,2:T(4,128)(2,1)} copy(bf16[4,128,512]{1,2,0:T(8,128)(2,1)} %bitcast.3) | data formatting | bytes 1048576 | tf_op jit(solution)/shard_map/all_to_all | solution.py:66
  87.9 2.0 %concatenate.25 = bf16[512,4,128]{0,2,1:T(8,128)(2,1)} reshape(bf16[4,128,512]{1,0,2:T(4,128)(2,1)} %copy.40) | data formatting | bytes 1048576 | tf_op jit(solution)/shard_map/while/body/eval_jaxpr/concatenate | solution.py:96
  89.9 10.4 %fusion.9 = f32[4,2560,512]{2,1,0:T(8,128)} fusion(bf16[2048,4,128]{2,0,1:T(8,128)(2,1)} %copy.45, bf16[512,4,128]{2,0,1:T(8,128)(2,1)S(1)} %copy.44, bf16[512,4,128]{2,1,0:T(4,128)(2,1)S(1)} %reshape.168), kind=kOutput, calls=%fused_computation.16 | convolution fusion | flops 1347420160 | bytes 24117248 | tf_op jit(solution)/shard_map/while/body/eval_jaxpr/qhd,khd->hqk/dot_general | solution.py:34
  100.4 22.6 %fusion.50 = (f32[4,512]{1,0:T(4,128)S(1)}, f32[4,512,2560]{1,2,0:T(8,128)}) fusion(f32[4,2560,512]{2,1,0:T(8,128)} %fusion.9, pred[512,2560]{0,1:T(8,128)(4,1)S(1)} %copy-done.3), kind=kOutput, calls=%fused_computation.91 | output fusion | flops 31459840 | bytes 43261952 | tf_op jit(solution)/shard_map/while/body/eval_jaxpr/sub | solution.py:39
  123.0 8.1 %fusion.16 = bf16[512,4,128]{0,2,1:T(8,128)(2,1)S(1)} fusion(f32[4,512,2560]{1,2,0:T(8,128)} %get-tuple-element.52, f32[4,512]{1,0:T(4,128)S(1)} %get-tuple-element.51, bf16[2048,4,128]{0,2,1:T(8,128)(2,1)S(1)} %copy-done.1, bf16[512,4,128]{0,2,1:T(8,128)(2,1)S(1)} %copy-done.6), kind=kOutput, calls=%fused_computation.21 | convolution fusion | flops 1358168064 | bytes 24125440 | tf_op jit(solution)/shard_map/while/body/eval_jaxpr/hqk,khd->qhd/dot_general | solution.py:41
  131.3 0.9 copy.49
  132.1 3.5 %all-to-all-start.3 = ((bf16[4,128,512]{1,2,0:T(8,128)(2,1)}), bf16[4,128,512]{1,2,0:T(8,128)(2,1)S(1)}, u32[]{:S(2)}, u32[]{:S(2)}) async-start(bf16[4,128,512]{1,2,0:T(8,128)(2,1)} %copy.49), calls=%async_computation.3 | async-start | bytes 1048576 | tf_op jit(solution)/shard_map/all_to_all | solution.py:107
  136.8 2.4 %fusion.39 = f32[128,4096]{1,0:T(8,128)} fusion(f32[8,4096]{1,0:T(8,128)S(1)} %fusion.37, s32[128]{0:T(128)S(1)} %dynamic_slice.10), kind=kOutput, calls=%fused_computation.74 | convolution fusion | flops 50332672 | bytes 2228736 | tf_op jit(solution)/shard_map/dot_general | solution.py:108
  139.2 10.3 %all-to-all-done.3 = bf16[4,128,512]{1,2,0:T(8,128)(2,1)S(1)} async-done(((bf16[4,128,512]{1,2,0:T(8,128)(2,1)}), bf16[4,128,512]{1,2,0:T(8,128)(2,1)S(1)}, u32[]{:S(2)}, u32[]{:S(2)}) %all-to-all-start.3) | async-done | bytes 524320 | tf_op jit(solution)/shard_map/all_to_all | solution.py:107
  149.6 1.1 convert_element_type.61
  150.6 2.5 %copy.55 = f32[128,2048]{1,0:T(8,128)} copy(f32[128,2048]{0,1:T(8,128)} %bitcast.51) | data formatting | bytes 2097152 | tf_op jit(solution)/shard_map/convert_element_type | solution.py:109
  153.5 2.8 %fusion.20 = f32[128]{0:T(128)S(1)} fusion(bf16[2048,64]{0,1:T(8,128)(2,1)S(1)} %copy-done.7, f32[128,4096]{1,0:T(8,128)} %fusion.39, f32[128,2048]{1,0:T(8,128)} %copy.55, f32[128]{0:T(128)S(1)} %get-tuple-element.40, f32[128]{0:T(128)S(1)} %get-tuple-element.29, f32[128,64]{0,1:T(8,128)S(1)} %copy-done.8, f32[128,64]{0,1:T(8,128)S(1)} %copy-done.9), kind=kOutput, calls=%fused_computation.24 | convolution fusion | flops 202669952 | bytes 3474944 | tf_op jit(solution)/shard_map/dot_general | solution.py:114
  157.1 9.8 %psum.7 = f32[8]{0:T(128)S(1)} all-reduce(f32[8]{0:T(128)S(1)} %select_reduce_fusion.1), channel_id=1, replica_groups=mesh['dp'=8,'seq'=4] {'seq'}, use_global_device_ids=true, to_apply=%region_8.9 | all-reduce | flops 8 | bytes 64 | tf_op jit(solution)/shard_map/psum | solution.py:121
  167.0 11.8 %all-reduce = f32[64]{0:T(128)S(1)} all-reduce(f32[64]{0:T(128)S(1)} %fusion.41), channel_id=1, replica_groups=mesh['dp'=8,'seq'=4] {'dp'}, use_global_device_ids=true, to_apply=%add | all-reduce | flops 64 | bytes 512
  (53 shorter events, 5.3 us)
Async XLA Ops:
  0.0 136.4 %copy-start = (bf16[256,4096]{1,0:T(8,128)(2,1)S(1)}, bf16[256,4096]{1,0:T(8,128)(2,1)}, u32[]{:S(2)}) copy-start(bf16[256,4096]{1,0:T(8,128)(2,1)} %param.19) | copy-start | bytes 6291460
  2.1 46.4 %all-to-all-start.1 = ((bf16[128,4,512]{2,0,1:T(8,128)(2,1)}), bf16[128,4,512]{2,0,1:T(8,128)(2,1)S(1)}, u32[]{:S(2)}, u32[]{:S(2)}) async-start(bf16[128,4,512]{2,0,1:T(8,128)(2,1)} %bitcast.50), calls=%async_computation.1 | async-start | bytes 1048576 | tf_op jit(solution)/shard_map/all_to_all | solution.py:65
  30.0 7.2 %copy-start.4 = (bf16[128,2048]{1,0:T(8,128)(2,1)S(1)}, bf16[128,2048]{1,0:T(8,128)(2,1)}, u32[]{:S(2)}) copy-start(bf16[128,2048]{1,0:T(8,128)(2,1)} %param.12) | copy-start | bytes 1572868
  38.0 8.4 %copy-start.5 = (bf16[128,2048]{1,0:T(8,128)(2,1)S(1)}, bf16[128,2048]{1,0:T(8,128)(2,1)}, u32[]{:S(2)}) copy-start(bf16[128,2048]{1,0:T(8,128)(2,1)} %param.14) | copy-start | bytes 1572868
  38.0 9.4 %copy-start.11 = (s32[1,8]{1,0:T(1,128)S(1)}, s32[1,8]{1,0:T(1,128)}, u32[]{:S(2)}) copy-start(s32[1,8]{1,0:T(1,128)} %param.17) | copy-start | bytes 100
  38.0 9.6 %copy-start.10 = (s32[8]{0:T(128)S(1)}, s32[8]{0:T(128)}, u32[]{:S(2)}) copy-start(s32[8]{0:T(128)} %param.16) | copy-start | bytes 100
  48.5 19.0 %all-to-all-start.2 = ((bf16[128,4,512]{2,0,1:T(8,128)(2,1)}), bf16[128,4,512]{2,0,1:T(8,128)(2,1)S(1)}, u32[]{:S(2)}, u32[]{:S(2)}) async-start(bf16[128,4,512]{2,0,1:T(8,128)(2,1)} %bitcast.49), calls=%async_computation.2 | async-start | bytes 1048576 | tf_op jit(solution)/shard_map/all_to_all | solution.py:64
  67.5 9.5 %copy-start.2 = (bf16[128,4,512]{2,0,1:T(8,128)(2,1)}, bf16[128,4,512]{2,0,1:T(8,128)(2,1)S(1)}, u32[]{:S(2)}) copy-start(bf16[128,4,512]{2,0,1:T(8,128)(2,1)S(1)} %all-to-all-done.2) | copy-start | bytes 1572868
  67.5 18.2 %all-to-all-start = ((bf16[128,4,512]{0,2,1:T(8,128)(2,1)}), bf16[128,4,512]{0,2,1:T(8,128)(2,1)}, u32[]{:S(2)}, u32[]{:S(2)}) async-start(bf16[128,4,512]{0,2,1:T(8,128)(2,1)} %bitcast.2), calls=%async_computation | async-start | bytes 1048576 | tf_op jit(solution)/shard_map/all_to_all | solution.py:66
  89.9 10.4 %copy-start.3 = (pred[512,2560]{0,1:T(8,128)(4,1)S(1)}, pred[512,2560]{0,1:T(8,128)(4,1)}, u32[]{:S(2)}) copy-start(pred[512,2560]{0,1:T(8,128)(4,1)} %pad_add_fusion) | copy-start | bytes 3932164
  100.4 22.6 %copy-start.1 = (bf16[2048,4,128]{0,2,1:T(8,128)(2,1)S(1)}, bf16[2048,4,128]{0,2,1:T(8,128)(2,1)}, u32[]{:S(2)}) copy-start(bf16[2048,4,128]{0,2,1:T(8,128)(2,1)} %copy.52) | copy-start | bytes 6291460
  100.4 22.6 %copy-start.6 = (bf16[512,4,128]{0,2,1:T(8,128)(2,1)S(1)}, bf16[512,4,128]{0,2,1:T(8,128)(2,1)}, u32[]{:S(2)}) copy-start(bf16[512,4,128]{0,2,1:T(8,128)(2,1)} %concatenate.25) | copy-start | bytes 1572868
  123.0 12.7 %copy-start.12 = (s32[8]{0:T(128)S(1)}, s32[8]{0:T(128)}, u32[]{:S(2)}) copy-start(s32[8]{0:T(128)} %param.18) | copy-start | bytes 100
  123.0 12.7 %copy-start.14 = (u32[32]{0:T(128)S(1)}, u32[32]{0:T(128)}, u32[]{:S(2)}) copy-start(u32[32]{0:T(128)} %constant.99) | copy-start | bytes 388
  132.1 17.4 %all-to-all-start.3 = ((bf16[4,128,512]{1,2,0:T(8,128)(2,1)}), bf16[4,128,512]{1,2,0:T(8,128)(2,1)S(1)}, u32[]{:S(2)}, u32[]{:S(2)}) async-start(bf16[4,128,512]{1,2,0:T(8,128)(2,1)} %copy.49), calls=%async_computation.3 | async-start | bytes 1048576 | tf_op jit(solution)/shard_map/all_to_all | solution.py:107
  136.4 17.0 %copy-start.7 = (bf16[2048,64]{0,1:T(8,128)(2,1)S(1)}, bf16[2048,64]{0,1:T(8,128)(2,1)}, u32[]{:S(2)}) copy-start(bf16[2048,64]{0,1:T(8,128)(2,1)} %param.20) | copy-start | bytes 786436
  136.4 17.0 %copy-start.8 = (f32[128,64]{0,1:T(8,128)S(1)}, f32[128,64]{0,1:T(8,128)}, u32[]{:S(2)}) copy-start(f32[128,64]{0,1:T(8,128)} %param.21) | copy-start | bytes 98308
  136.4 17.0 %copy-start.9 = (f32[128,64]{0,1:T(8,128)S(1)}, f32[128,64]{0,1:T(8,128)}, u32[]{:S(2)}) copy-start(f32[128,64]{0,1:T(8,128)} %param.22) | copy-start | bytes 98308
  136.8 42.0 %copy-start.13 = (s32[8]{0:T(128)S(1)}, s32[8]{0:T(128)}, u32[]{:S(2)}) copy-start(s32[8]{0:T(128)} %param.23) | copy-start | bytes 100
where the time goes:
time: 180 us; the launch traced here: 179 us
  local copies, waits for them, and re-layouts  53.6 us (30%)
  other arithmetic  33.7 us (19%)
  waiting for transfers between devices  26.5 us (15%)
  matrix products  24.1 us (13%)
  blocking collectives  21.6 us (12%)
  starting transfers between devices  19.2 us (11%)
    sub x1, other arithmetic, attend_block(): weights = jnp.exp(score_rows - row_top)  22.6 us
    slice x1, local copies, waits for them, and re-layouts, per_device(): text_kv[:, :, 1, :].reshape(clips_here * text_len, local_width)  21.6 us
    unnamed x1, blocking collectives  11.8 us
    concatenate x3, local copies, waits for them, and re-layouts, one_block(): jnp.concatenate([value_heads, text_values], axis=0)  10.4 us
    dot_general x1, matrix products, attend_block(): jnp.einsum('qhd,khd->hqk', query_split, key_split, preferred_element_type...  10.4 us
    all_to_all x1, waiting for transfers between devices, per_device(): lax.all_to_all(attended, 'seq', split_axis=0, concat_axis=1, tiled=True)  10.3 us
    psum x1, blocking collectives, per_device(): clip_totals = lax.psum(clip_partial, 'seq')  9.83 us
    concatenate x4, local copies, waits for them, and re-layouts, one_block(): jnp.concatenate([key_heads, text_keys], axis=0)  9.27 us
  transfers between devices with their start and end apart: 4, of which 3 were waited for; matrix products, arithmetic and copies ran while one was open for 31% of the time, Pallas kernels for 0%

commit v1 on v0

v1 whole, which is shorter than its diff:
```python
import functools
import math

import jax
import jax.numpy as jnp
from jax import lax
from jax.experimental import pallas as pl
from jax.experimental.pallas import tpu as pltpu
from jax.sharding import PartitionSpec as P

HEAD_DIM = 128
FREQ = 256
EPS = 1e-06
NEG = -1e30
STAT_ROWS = 8
ALIGN = 16
F32 = jnp.float32
BF16 = jnp.bfloat16
EXACT = lax.Precision.HIGHEST
VMEM_LIMIT = 32 * 1024 * 1024
SCORE_SCALE = math.log2(math.e) / math.sqrt(HEAD_DIM)


def nt_dot(a, b, precision=None):
    return lax.dot_general(a, b, (((1,), (1,)), ((), ())), precision=precision, preferred_element_type=F32)


def two_parts(x):
    high = x.astype(BF16)
    return high, (x - high.astype(F32)).astype(BF16)


def head_cols(h):
    return slice(h * HEAD_DIM, (h + 1) * HEAD_DIM)


def step_embedding(timesteps):
    half_width = FREQ // 2
    frequency = jnp.exp(-math.log(10000.0) * jnp.arange(half_width, dtype=F32) / half_width)
    angles = timesteps.astype(F32)[:, None] * frequency[None, :]
    return jnp.concatenate([jnp.cos(angles), jnp.sin(angles)], axis=1)


def clip_index(info_ref, clips, shape, axis, first):
    places = lax.broadcasted_iota(jnp.int32, shape, axis) + first
    end = jnp.int32(0)
    index = jnp.zeros(shape, jnp.int32)
    for c in range(clips):
        end = end + info_ref[c]
        index = index + (places >= end).astype(jnp.int32)
    return index


def source_rows(sources, k, tok_dev):
    source = lax.rem(lax.axis_index("seq") + sources - k, sources)
    return pl.ds(pl.multiple_of(source * tok_dev, tok_dev), tok_dev)


def cut_kernel(sources, count, *refs):
    wholes, pieces, sems = refs[:count], refs[count:-1], refs[-1]
    local = pieces[0].shape[2]
    copies = []
    for k in [*range(1, sources), 0]:
        target = lax.rem(lax.axis_index("seq") + k, sources)
        for i in range(count):
            copies.append(
                pltpu.make_async_copy(
                    wholes[i].at[:, pl.ds(pl.multiple_of(target * local, HEAD_DIM), local)],
                    pieces[k].at[i],
                    sems.at[k * count + i],
                )
            )
            copies[-1].start()
    for copy in copies:
        copy.wait()


def prep_kernel(
    clips, info_ref, act_ref, mod_hbm, wt_hbm, noise_hbm, clean_hbm, kv_hbm,
    scale_ref, slope_ref, offset_ref, share_ref, weight_ref, keys_ref, values_ref,
    mods, mod_buf, wt_buf, noise_buf, clean_buf, kv_buf, sems,
):
    width = wt_buf.shape[1]
    group_rows, local = scale_ref.shape
    tok_dev = noise_buf.shape[1]
    rank = lax.axis_index("seq")
    pairs = [(mod_hbm, mod_buf), (wt_hbm, wt_buf), (noise_hbm, noise_buf), (clean_hbm, clean_buf)]
    pairs += [(kv_hbm.at[c], kv_buf.at[c]) for c in range(clips)]
    copies = [pltpu.make_async_copy(a, b, sems.at[i]) for i, (a, b) in enumerate(pairs)]
    for copy in copies:
        copy.start()
    for copy in copies[:4]:
        copy.wait()
    mods[...] = jnp.dot(act_ref[...], mod_buf[...], preferred_element_type=F32)
    scales = 1.0 + mods[:, width:]
    weight = wt_buf[...].astype(F32)
    slopes = nt_dot(weight, scales, EXACT)
    shifts = nt_dot(weight, mods[:, :width], EXACT)
    tok_clip = clip_index(info_ref, clips, (clips, tok_dev), 1, rank * tok_dev)
    picks = (tok_clip == lax.broadcasted_iota(jnp.int32, (clips, tok_dev), 0)).astype(F32)
    slot = lax.broadcasted_iota(jnp.int32, (clips, 1), 0)
    sizes = jnp.zeros((clips, 1), F32)
    for c in range(clips):
        sizes = jnp.where(slot == c, info_ref[c].astype(F32), sizes)
    share_ref[...] = picks / sizes
    slope_ref[...] = jnp.dot(slopes, picks, precision=EXACT, preferred_element_type=F32)
    offset_ref[...] = jnp.dot(shifts, picks, precision=EXACT, preferred_element_type=F32) - (
        noise_buf[...] - clean_buf[...]
    )
    row_clip = clip_index(info_ref, clips, (group_rows, clips), 0, 0)
    row_picks = (row_clip == lax.broadcasted_iota(jnp.int32, (group_rows, clips), 1)).astype(F32)
    mine = 1.0 + mods[:, pl.ds(pl.multiple_of(width + rank * local, HEAD_DIM), local)]
    scale_ref[...] = jnp.dot(row_picks, mine, precision=EXACT, preferred_element_type=F32)
    weight_ref[...] = wt_buf[:, pl.ds(pl.multiple_of(rank * local, HEAD_DIM), local)]
    for c in range(clips):
        copies[4 + c].wait()
        keys_ref[c] = kv_buf[c, :, 0, :]
        values_ref[c] = kv_buf[c, :, 1, :]


def text_kernel(sources, clips, window, info_ref, *refs):
    qk_refs = refs[:sources]
    keys_ref, values_ref, out_ref, level_ref, q_all = refs[sources:]
    tok_dev, local = qk_refs[0].shape[1:]
    heads = local // HEAD_DIM
    text_len = keys_ref.shape[1]
    for k, qk_ref in enumerate(qk_refs):
        q_all[source_rows(sources, k, tok_dev), :] = qk_ref[0]
    slots = lax.broadcasted_iota(jnp.int32, (1, text_len), 1)
    ones = jnp.ones((text_len, HEAD_DIM), BF16)

    def one_clip(clip, start):
        first = pl.multiple_of(start // ALIGN * ALIGN, ALIGN)
        rows = pl.ds(first, window)
        edge = pl.ds(first, ALIGN)
        live = slots < info_ref[clips + clip]
        before = lax.broadcasted_iota(jnp.int32, (ALIGN, 1), 0) + first < start
        kept = [(out_ref[edge, head_cols(h)], level_ref[h, edge, :]) for h in range(heads)]
        scores = [nt_dot(q_all[rows, head_cols(h)], keys_ref[clip, :, head_cols(h)]) for h in range(heads)]
        weights, tops = [], []
        for score in scores:
            score = jnp.where(live, score, NEG)
            top = jnp.max(score, axis=1, keepdims=True)
            weights.append(jnp.exp2((score - top) * SCORE_SCALE).astype(BF16))
            tops.append(top)
        results = []
        for h in range(heads):
            beside = jnp.concatenate([values_ref[clip, :, head_cols(h)], ones], axis=1)
            mixed = jnp.dot(weights[h], beside, preferred_element_type=F32)
            total = mixed[:, HEAD_DIM:]
            results.append((mixed[:, :HEAD_DIM] / total, tops[h] * SCORE_SCALE + jnp.log2(total)))
        for h in range(heads):
            out_ref[rows, head_cols(h)] = results[h][0]
            level_ref[h, rows, :] = results[h][1]
            out_ref[edge, head_cols(h)] = jnp.where(before, kept[h][0], results[h][0][:ALIGN])
            level_ref[h, edge, :] = jnp.where(before, kept[h][1], results[h][1][:ALIGN])
        return start + info_ref[clip]

    lax.fori_loop(0, clips, one_clip, jnp.int32(0))


def reach_of(first, reach, group_rows):
    span = group_rows - reach[1]
    return jnp.clip(first - reach[0], 0, span) if span else jnp.int32(0)


def weigh_kernel(sources, clips, reach, info_ref, *refs):
    qk_refs = refs[:sources]
    text_ref, level_ref, weight_ref, base_ref, q_all, k_all = refs[sources:]
    tok_dev, local = qk_refs[0].shape[1:]
    group_rows = q_all.shape[0]
    heads = local // HEAD_DIM
    for k in range(sources):
        rows = source_rows(sources, k, tok_dev)
        q_all[rows, :] = qk_refs[k][0]
        k_all[rows, :] = qk_refs[k][1]
    for first in range(0, group_rows, tok_dev):
        low = min(max(first - reach[0], 0), group_rows - reach[1])
        rows, span = slice(first, first + tok_dev), slice(low, low + reach[1])
        row_clip = clip_index(info_ref, clips, (tok_dev, 1), 0, first)
        live = row_clip == clip_index(info_ref, clips, (1, reach[1]), 1, low)
        scores = [nt_dot(q_all[rows, head_cols(h)], k_all[span, head_cols(h)]) for h in range(heads)]
        for h in range(heads):
            score = jnp.where(live, scores[h] * SCORE_SCALE, NEG)
            level = level_ref[h, rows, :]
            top = jnp.maximum(jnp.max(score, axis=1, keepdims=True), level)
            chunks = [slice(part, part + HEAD_DIM) for part in range(0, reach[1], HEAD_DIM)]
            weights = [jnp.exp2(score[:, cols] - top) for cols in chunks]
            fade = jnp.exp2(level - top)
            share = 1.0 / (jnp.sum(sum(weights[1:], weights[0]), axis=1, keepdims=True) + fade)
            for cols, weight in zip(chunks, weights):
                weight_ref[h, rows, cols] = (weight * share).astype(BF16)
            base_ref[rows, head_cols(h)] = (fade * share) * text_ref[rows, head_cols(h)]


def mix_kernel(sources, reach, ahead, *refs):
    v_refs = refs[:sources]
    weight_ref, base_ref, scale_ref, wt_ref, out_ref, v_all = refs[sources:]
    tok_dev, local = v_refs[0].shape[1:]
    group_rows = scale_ref.shape[0]
    heads = local // HEAD_DIM
    channels = wt_ref.shape[0]
    for k in range(sources):
        v_all[source_rows(sources, k, tok_dev), :] = v_refs[k][0]
    first = pl.multiple_of(lax.rem(lax.axis_index("seq") + ahead, sources) * tok_dev, tok_dev)
    rows = pl.ds(first, tok_dev)
    span = pl.ds(pl.multiple_of(reach_of(first, reach, group_rows), HEAD_DIM), reach[1])
    mixed = [
        jnp.dot(weight_ref[h, rows, :], v_all[span, head_cols(h)], preferred_element_type=F32) for h in range(heads)
    ]
    attended = jnp.concatenate([(mixed[h] + base_ref[rows, head_cols(h)]).astype(BF16) for h in range(heads)], axis=1)
    attended_full = attended.astype(F32)
    y_high, y_low = two_parts(attended_full * scale_ref[rows, :])
    s_high, s_low = two_parts(attended_full * attended_full)
    weight = wt_ref[...]
    every = jnp.ones((STAT_ROWS, local), BF16)
    out_ref[:channels, :] = nt_dot(weight, y_high) + nt_dot(weight, y_low)
    is_sum = lax.broadcasted_iota(jnp.int32, (STAT_ROWS, tok_dev), 0) == 0
    squares = nt_dot(every, s_high) + nt_dot(every, s_low)
    out_ref[channels:, :] = jnp.where(is_sum, nt_dot(every, attended), squares)


def loss_kernel(sources, width, *refs):
    part_refs = refs[:sources]
    slope_ref, offset_ref, share_ref, out_ref = refs[sources:]
    channels = slope_ref.shape[0]
    clips = share_ref.shape[0]
    total = part_refs[0][...]
    for part in part_refs[1:]:
        total = total + part[...]
    center = total[channels : channels + 1, :] * (1.0 / width)
    spread = total[channels + 1 : channels + 2, :] * (1.0 / width) - center * center
    diff = (total[:channels, :] - center * slope_ref[...]) * lax.rsqrt(spread + EPS) + offset_ref[...]
    error = jnp.sum(diff * diff, axis=0, keepdims=True) * (1.0 / channels)
    sums = jnp.sum(share_ref[...] * error, axis=1, keepdims=True)
    lanes = lax.broadcasted_iota(jnp.int32, (clips, out_ref.shape[2]), 1)
    mine = lanes == lax.broadcasted_iota(jnp.int32, lanes.shape, 0)
    row = jnp.sum(jnp.where(mine, sums, 0.0), axis=0, keepdims=True)
    out_ref[...] = jnp.broadcast_to(row[None], out_ref.shape)


def smem():
    return pl.BlockSpec(memory_space=pltpu.SMEM)


def vmem():
    return pl.BlockSpec(memory_space=pltpu.VMEM)


def hbm():
    return pl.BlockSpec(memory_space=pltpu.HBM)


def call(kernel, name, operands, results, scratch=(), scalars=(), in_hbm=(), limit=VMEM_LIMIT, flops=0, traffic=0, exps=0):
    return pl.pallas_call(
        kernel,
        in_specs=[smem()] * len(scalars) + [hbm() if i in in_hbm else vmem() for i in range(len(operands))],
        out_specs=[vmem()] * len(results),
        out_shape=[pltpu.VMEM(*r) for r in results],
        scratch_shapes=list(scratch),
        compiler_params=pltpu.CompilerParams(vmem_limit_bytes=limit),
        cost_estimate=pl.CostEstimate(flops=flops, bytes_accessed=traffic, transcendentals=exps),
        name=name,
    )(*scalars, *(pltpu.with_memory_space_constraint(x, pltpu.HBM) if i in in_hbm else x for i, x in enumerate(operands)))


def per_device(
    queries, keys, values, text_kv, text_lengths, clip_lengths, timesteps, mod_weight, final_weight, noise, clean,
    report_order,
):
    tok_dev, width = queries.shape
    sources = lax.axis_size("seq")
    groups = lax.axis_size("dp")
    local = width // sources
    heads = local // HEAD_DIM
    group_rows = tok_dev * sources
    clips = clip_lengths.shape[1]
    text_len = text_kv.shape[1]
    clip_most = 2 * group_rows // clips
    window = clip_most + ALIGN
    padded = group_rows + window
    reach = (clip_most, min(group_rows, tok_dev + 2 * clip_most))
    channels = final_weight.shape[1]
    info = jnp.concatenate([clip_lengths[0], text_lengths])

    def cut(arrays, name):
        return call(
            functools.partial(cut_kernel, sources, len(arrays)), name, arrays,
            [((len(arrays), tok_dev, local), BF16)] * sources,
            [pltpu.SemaphoreType.DMA((sources * len(arrays),))], in_hbm=range(len(arrays)),
            traffic=4 * tok_dev * width * len(arrays),
        )

    def onward(x, k):
        return lax.ppermute(x, "seq", [(i, (i + k) % sources) for i in range(sources)]) if k else x

    qk_pieces = list(cut([queries, keys], "cut_queries_keys"))
    qk_pieces[0], values = lax.optimization_barrier((qk_pieces[0], values))
    qk_blocks = [onward(piece, k) for k, piece in enumerate(qk_pieces)]
    v_pieces = cut([values], "cut_values")

    weight_t = final_weight.T
    activated = jax.nn.silu(step_embedding(timesteps)).astype(BF16)
    scale_tok, slope, offset, share, weight_local, text_keys, text_values = call(
        functools.partial(prep_kernel, clips), "prep",
        [activated, mod_weight, weight_t, noise.T, clean.T, text_kv],
        [
            ((group_rows, local), F32), ((channels, tok_dev), F32), ((channels, tok_dev), F32), ((clips, tok_dev), F32),
            ((channels, local), BF16), ((clips, text_len, local), BF16), ((clips, text_len, local), BF16),
        ],
        [
            pltpu.VMEM((clips, 2 * width), F32), pltpu.VMEM(mod_weight.shape, BF16),
            pltpu.VMEM(weight_t.shape, BF16), pltpu.VMEM((channels, tok_dev), F32),
            pltpu.VMEM((channels, tok_dev), F32), pltpu.VMEM(text_kv.shape, BF16),
            pltpu.SemaphoreType.DMA((4 + clips,)),
        ],
        scalars=[info], in_hbm=range(1, 6),
    )

    v_pieces, scale_tok = lax.optimization_barrier((v_pieces, scale_tok))
    v_blocks = [onward(piece, k) for k, piece in enumerate(v_pieces)]

    text_out, level = call(
        functools.partial(text_kernel, sources, clips, window), "text", [*qk_blocks, text_keys, text_values],
        [((padded, local), F32), ((heads, padded, HEAD_DIM), F32)],
        [pltpu.VMEM((padded, local), BF16)], scalars=[info],
    )

    weights, base = call(
        functools.partial(weigh_kernel, sources, clips, reach), "weigh", [*qk_blocks, text_out, level],
        [((heads, group_rows, reach[1]), BF16), ((group_rows, local), F32)],
        [pltpu.VMEM((group_rows, local), BF16)] * 2, scalars=[info],
    )

    parts = [None] * sources
    for k in [*range(1, sources), 0]:
        (part,) = call(
            functools.partial(mix_kernel, sources, reach, k), "mix",
            [*v_blocks, weights, base, scale_tok, weight_local], [((channels + STAT_ROWS, tok_dev), F32)],
            [pltpu.VMEM((group_rows, local), BF16)], flops=4 * tok_dev * reach[1] * local, traffic=2**20,
        )
        parts[k] = onward(part, k)

    (shares,) = call(
        functools.partial(loss_kernel, sources, width), "loss", [*parts, slope, offset, share],
        [((groups * sources, 1, HEAD_DIM), F32)],
    )
    everyone = lax.all_to_all(shares, ("dp", "seq"), split_axis=0, concat_axis=0, tiled=True)
    losses = jnp.sum(everyone.reshape(groups, sources, HEAD_DIM), axis=1)[:, :clips].reshape(1, -1)
    slots = jnp.arange(groups * clips, dtype=jnp.int32)
    return jnp.sum(jnp.where(report_order[:, None] == slots[None, :], losses, 0.0), axis=1)


def solution(mesh):
    in_specs = (
        P(("dp", "seq"), None),
        P(("dp", "seq"), None),
        P(("dp", "seq"), None),
        P("dp", None, None, "seq"),
        P("dp"),
        P("dp", None),
        P("dp"),
        P(),
        P(),
        P(("dp", "seq"), None),
        P(("dp", "seq"), None),
        P("dp"),
    )
    return jax.shard_map(per_device, mesh=mesh, in_specs=in_specs, out_specs=P("dp"), check_vma=False)
```

time: 180 us -> 64 us (0.36)
  local copies, waits for them, and re-layouts: 53.6 us -> 0.08 us
  other arithmetic: 33.7 us -> 2.25 us
  Pallas kernels: 0 us -> 25 us
  matrix products: 24.1 us -> 0 us
  waiting for transfers between devices: 26.5 us -> 7.74 us
  blocking collectives: 21.6 us -> 10.3 us
    all_to_all x4 -> x0, waiting for transfers between devices: 26.5 us -> none  [the longest x1 10.3 us: per_device(): lax.all_to_all(attended, 'seq', split_axis=0, concat_axis=1, tiled=True)]
    pallas_call x0 -> x10, Pallas kernels: none -> 25 us  [call(): pl.pallas_call(kernel, in_specs=[smem()] * len(scalars) + [hbm() if i in...]
    dot_general x5 -> x0, matrix products: 24.1 us -> none  [the longest x1 10.4 us: attend_block(): jnp.einsum('qhd,khd->hqk', query_split, key_split, preferred_element_type...]
    sub x1 -> x0, other arithmetic: 22.6 us -> none  [attend_block(): weights = jnp.exp(score_rows - row_top)]
    slice x1 -> x0, local copies, waits for them, and re-layouts: 21.6 us -> none  [per_device(): text_kv[:, :, 1, :].reshape(clips_here * text_len, local_width)]
    concatenate x7 -> x0, local copies, waits for them, and re-layouts: 19.7 us -> none  [the longest x3 10.4 us: one_block(): jnp.concatenate([value_heads, text_values], axis=0)]
    all_to_all x4 -> x0, starting transfers between devices: 19.2 us -> none  [the longest x1 6.32 us: per_device(): lax.all_to_all(keys, 'seq', split_axis=1, concat_axis=0, tiled=True)]
    ppermute x0 -> x9, starting transfers between devices: none -> 18.3 us  [onward(): lax.ppermute(x, 'seq', [(i, (i + k) % sources) for i in range(sources)])]
  transfers between devices with their start and end apart: 4 -> 9, of which waited for: 3 -> 3; matrix products, arithmetic and copies ran while one was open for 31% -> 2% of each run, Pallas kernels for 0% -> 36%
where the time goes in v1:
time: 64 us; the launch traced here: 63.9 us
  Pallas kernels  25 us (39%)
  starting transfers between devices  18.3 us (29%)
  blocking collectives  10.3 us (16%)
  waiting for transfers between devices  7.74 us (12%)
  other arithmetic  2.25 us (4%)
    pallas_call x10, Pallas kernels, call(): pl.pallas_call(kernel, in_specs=[smem()] * len(scalars) + [hbm() if i in...  25 us
    ppermute x9, starting transfers between devices, onward(): lax.ppermute(x, 'seq', [(i, (i + k) % sources) for i in range(sources)])  18.3 us
    all_to_all x1, blocking collectives, per_device(): lax.all_to_all(shares, ('dp', 'seq'), split_axis=0, concat_axis=0, tiled=...  10.3 us
    ppermute x9, waiting for transfers between devices, onward(): lax.ppermute(x, 'seq', [(i, (i + k) % sources) for i in range(sources)])  7.74 us
  transfers between devices with their start and end apart: 9, of which 3 were waited for; matrix products, arithmetic and copies ran while one was open for 2% of the time, Pallas kernels for 36%

profile of v1, /device:TPU:0, one launch (start us, length us, event | category | flops | bytes accessed | tf_op | source)
XLA Modules:
  0.0 63.9 jit_solution(4262428662220952755)
XLA Ops:
  0.0 1.4 %cut_queries_keys.1 = (bf16[2,128,512]{2,1,0:T(8,128)(2,1)S(1)}, bf16[2,128,512]{2,1,0:T(8,128)(2,1)S(1)}, bf16[2,128,512]{2,1,0:T(8,128)(2,1)S(1)}, bf16[2,128,512]{2,1,0:T(8,128)(2,1)S(1)}) custom-call(bf16[128,2048]{1,0:T(8,128)(2,1)} %refs_0_.1, bf16[128,2048]{1,0:T(8,128)(2,1)} %refs_1_.1), custom_call_target="tpu_custom_call" | custom-call | bytes 2097152 | tf_op jit(solution)/shard_map/cut_queries_keys/pallas_call | solution.py:255
  1.4 3.1 %collective-permute-start.3 = (bf16[2,128,512]{2,1,0:T(8,128)(2,1)S(1)}, bf16[2,128,512]{2,1,0:T(8,128)(2,1)S(1)}, u32[]{:S(2)}, u32[]{:S(2)}) collective-permute-start(bf16[2,128,512]{2,1,0:T(8,128)(2,1)S(1)} %get-tuple-element.43), channel_id=1, source_target_pairs={{0,1},{1,2},{2,3},{3,0},{4,5},{5,6},{6,7},{7,4},{8,9},{9,10},{10,1... | collective-permute-start | bytes 786440 | tf_op jit(solution)/shard_map/ppermute | solution.py:295
  4.4 2.6 %collective-permute-start.4 = (bf16[2,128,512]{2,1,0:T(8,128)(2,1)S(1)}, bf16[2,128,512]{2,1,0:T(8,128)(2,1)S(1)}, u32[]{:S(2)}, u32[]{:S(2)}) collective-permute-start(bf16[2,128,512]{2,1,0:T(8,128)(2,1)S(1)} %get-tuple-element.44), channel_id=1, source_target_pairs={{0,2},{1,3},{2,0},{3,1},{4,6},{5,7},{6,4},{7,5},{8,10},{9,11},{10,... | collective-permute-start | bytes 786440 | tf_op jit(solution)/shard_map/ppermute | solution.py:295
  7.0 1.3 %collective-permute-start.5 = (bf16[2,128,512]{2,1,0:T(8,128)(2,1)S(1)}, bf16[2,128,512]{2,1,0:T(8,128)(2,1)S(1)}, u32[]{:S(2)}, u32[]{:S(2)}) collective-permute-start(bf16[2,128,512]{2,1,0:T(8,128)(2,1)S(1)} %get-tuple-element.45), channel_id=1, source_target_pairs={{0,3},{1,0},{2,1},{3,2},{4,7},{5,4},{6,5},{7,6},{8,11},{9,8},{10,9... | collective-permute-start | bytes 786440 | tf_op jit(solution)/shard_map/ppermute | solution.py:295
  8.4 0.7 %convert_element_type.6 = f32[8]{0:T(128)S(1)} convert(s32[8]{0:T(128)} %param.18) | non-fusion elementwise | flops 8 | bytes 64 | tf_op jit(solution)/shard_map/convert_element_type | solution.py:40
  9.1 0.1 multiply_cosine_fusion
  9.2 0.8 %pad_add_fusion.info_ref = s32[16]{0:T(128)S(1)} fusion(s32[8]{0:T(128)} %param.16, s32[8]{0:T(128)} %bitcast.11), kind=kLoop, calls=%fused_computation.6 | loop fusion | flops 16 | bytes 128 | tf_op jit(solution)/shard_map/concatenate | solution.py:284
  9.9 1.1 %cut_values.1 = (bf16[1,128,512]{2,1,0:T(8,128)(2,1)S(1)}, bf16[1,128,512]{2,1,0:T(8,128)(2,1)S(1)}, bf16[1,128,512]{2,1,0:T(8,128)(2,1)S(1)}, bf16[1,128,512]{2,1,0:T(8,128)(2,1)S(1)}) custom-call(bf16[128,2048]{1,0:T(8,128)(2,1)} %refs_0_.2), custom_call_target="tpu_custom_call" | custom-call | bytes 1048576 | tf_op jit(solution)/shard_map/cut_values/pallas_call | solution.py:255
  11.1 13.3 %prep.1 = (f32[512,512]{1,0:T(8,128)S(1)}, f32[64,128]{1,0:T(8,128)S(1)}, f32[64,128]{1,0:T(8,128)S(1)}, f32[8,128]{1,0:T(8,128)S(1)}, bf16[64,512]{1,0:T(8,128)...) custom-call(s32[16]{0:T(128)S(1)} %pad_add_fusion.info_ref, ...), custom_call_target="tpu_custom_call" | custom-call | tf_op jit(solution)/shard_map/prep/pallas_call | solution.py:255
  24.3 0.7 %collective-permute-start = (bf16[1,128,512]{2,1,0:T(8,128)(2,1)S(1)}, bf16[1,128,512]{2,1,0:T(8,128)(2,1)S(1)}, u32[]{:S(2)}, u32[]{:S(2)}) collective-permute-start(bf16[1,128,512]{2,1,0:T(8,128)(2,1)S(1)} %get-tuple-element.39), channel_id=1, source_target_pairs={{0,1},{1,2},{2,3},{3,0},{4,5},{5,6},{6,7},{7,4},{8,9},{9,10},{10,1... | collective-permute-start | bytes 393224 | tf_op jit(solution)/shard_map/ppermute | solution.py:295
  25.1 0.3 collective-permute-start.1
  25.4 0.0 collective-permute-done.3.refs_1_
  25.4 2.8 %collective-permute-start.2 = (bf16[1,128,512]{2,1,0:T(8,128)(2,1)S(1)}, bf16[1,128,512]{2,1,0:T(8,128)(2,1)S(1)}, u32[]{:S(2)}, u32[]{:S(2)}) collective-permute-start(bf16[1,128,512]{2,1,0:T(8,128)(2,1)S(1)} %get-tuple-element.41), channel_id=1, source_target_pairs={{0,3},{1,0},{2,1},{3,2},{4,7},{5,4},{6,5},{7,6},{8,11},{9,8},{10,9... | collective-permute-start | bytes 393224 | tf_op jit(solution)/shard_map/ppermute | solution.py:295
  28.2 0.0 collective-permute-done.4.refs_2_
  28.2 0.0 collective-permute-done.5.refs_3_
  28.2 4.5 %text.1 = (f32[656,512]{1,0:T(8,128)S(1)}, f32[4,656,128]{2,1,0:T(8,128)S(1)}) custom-call(s32[16]{0:T(128)S(1)} %pad_add_fusion.info_ref, bf16[2,128,512]{2,1,0:T(8,128)(2,1)S(1)} %get-tuple-element.42.refs_0_, bf16[2,128,512]{2,1,0:T(8,128)(2,1)S(1)} %collective-permute-done.3.refs_1_, bf16[2,128,512]{2,1,0:T(8,128)(2,1)S(1)} %collective-permute-done.4.refs_2_, ...), custom_call_target="tpu_custom_call" | custom-call | tf_op jit(solution)/shard_map/text/pallas_call | solution.py:255
  32.7 2.3 %weigh.1 = (bf16[4,512,384]{2,1,0:T(8,128)(2,1)S(1)}, f32[512,512]{1,0:T(8,128)S(1)}) custom-call(s32[16]{0:T(128)S(1)} %pad_add_fusion.info_ref, bf16[2,128,512]{2,1,0:T(8,128)(2,1)S(1)} %get-tuple-element.42.refs_0_, bf16[2,128,512]{2,1,0:T(8,128)(2,1)S(1)} %collective-permute-done.3.refs_1_, bf16[2,128,512]{2,1,0:T(8,128)(2,1)S(1)} %collective-permute-done.4.refs_2_, ...), custom_call_target="tpu_custom_call" | custom-call | tf_op jit(solution)/shard_map/weigh/pallas_call | solution.py:255
  35.1 0.0 collective-permute-done.refs_1_
  35.1 3.1 %collective-permute-done.1.refs_2_ = bf16[1,128,512]{2,1,0:T(8,128)(2,1)S(1)} collective-permute-done((bf16[1,128,512]{2,1,0:T(8,128)(2,1)S(1)}, bf16[1,128,512]{2,1,0:T(8,128)(2,1)S(1)}, u32[]{:S(2)}, u32[]{:S(2)}) %collective-permute-start.1) | collective-permute-done | bytes 131104 | tf_op jit(solution)/shard_map/ppermute | solution.py:295
  38.2 0.6 mix.7
  38.8 6.8 %collective-permute-start.8 = (f32[72,128]{1,0:T(8,128)S(1)}, f32[72,128]{1,0:T(8,128)S(1)}, u32[]{:S(2)}, u32[]{:S(2)}) collective-permute-start(f32[72,128]{1,0:T(8,128)S(1)} %mix.7), channel_id=1, source_target_pairs={{0,3},{1,0},{2,1},{3,2},{4,7},{5,4},{6,5},{7,6},{8,11},{9,8},{10,9... | collective-permute-start | bytes 110600 | tf_op jit(solution)/shard_map/ppermute | solution.py:295
  45.5 0.6 mix.6
  46.1 0.0 collective-permute-start.7
  46.2 0.6 mix.5
  46.8 0.6 collective-permute-start.6
  47.4 0.6 mix.4.refs_0_
  48.0 3.1 %collective-permute-done.7.refs_2_ = f32[72,128]{1,0:T(8,128)S(1)} collective-permute-done((f32[72,128]{1,0:T(8,128)S(1)}, f32[72,128]{1,0:T(8,128)S(1)}, u32[]{:S(2)}, u32[]{:S(2)}) %collective-permute-start.7) | collective-permute-done | bytes 36896 | tf_op jit(solution)/shard_map/ppermute | solution.py:295
  51.0 1.5 %collective-permute-done.6.refs_1_ = f32[72,128]{1,0:T(8,128)S(1)} collective-permute-done((f32[72,128]{1,0:T(8,128)S(1)}, f32[72,128]{1,0:T(8,128)S(1)}, u32[]{:S(2)}, u32[]{:S(2)}) %collective-permute-start.6) | collective-permute-done | bytes 36896 | tf_op jit(solution)/shard_map/ppermute | solution.py:295
  52.6 0.1 loss.1
  52.7 10.3 %all_to_all.5 = f32[32,1,128]{2,1,0:T(1,128)S(1)} all-to-all(f32[32,1,128]{2,1,0:T(1,128)S(1)} %loss.1), channel_id=1, replica_groups=mesh['dp'=8,'seq'=4] {'dp','seq'}, dimensions={0} | all-to-all | bytes 32768 | tf_op jit(solution)/shard_map/all_to_all | solution.py:348
  63.1 0.1 broadcast_in_dim.18
  63.2 0.7 %select_reduce_fusion = f32[8]{0:T(128)} fusion(f32[64]{0:T(128)S(1)} %broadcast_in_dim.18, s32[8]{0:T(128)S(1)} %copy-done), kind=kLoop, calls=%fused_computation.4 | loop fusion | flops 1528 | bytes 320 | tf_op jit(solution)/shard_map/reduce_sum | solution.py:351
  (7 shorter events, 0.0 us)
Async XLA Ops:
  1.4 24.0 %collective-permute-start.3 = (bf16[2,128,512]{2,1,0:T(8,128)(2,1)S(1)}, bf16[2,128,512]{2,1,0:T(8,128)(2,1)S(1)}, u32[]{:S(2)}, u32[]{:S(2)}) collective-permute-start(bf16[2,128,512]{2,1,0:T(8,128)(2,1)S(1)} %get-tuple-element.43), channel_id=1, source_target_pairs={{0,1},{1,2},{2,3},{3,0},{4,5},{5,6},{6,7},{7,4},{8,9},{9,10},{10,1... | collective-permute-start | bytes 786440 | tf_op jit(solution)/shard_map/ppermute | solution.py:295
  4.4 23.8 %collective-permute-start.4 = (bf16[2,128,512]{2,1,0:T(8,128)(2,1)S(1)}, bf16[2,128,512]{2,1,0:T(8,128)(2,1)S(1)}, u32[]{:S(2)}, u32[]{:S(2)}) collective-permute-start(bf16[2,128,512]{2,1,0:T(8,128)(2,1)S(1)} %get-tuple-element.44), channel_id=1, source_target_pairs={{0,2},{1,3},{2,0},{3,1},{4,6},{5,7},{6,4},{7,5},{8,10},{9,11},{10,... | collective-permute-start | bytes 786440 | tf_op jit(solution)/shard_map/ppermute | solution.py:295
  7.0 21.2 %collective-permute-start.5 = (bf16[2,128,512]{2,1,0:T(8,128)(2,1)S(1)}, bf16[2,128,512]{2,1,0:T(8,128)(2,1)S(1)}, u32[]{:S(2)}, u32[]{:S(2)}) collective-permute-start(bf16[2,128,512]{2,1,0:T(8,128)(2,1)S(1)} %get-tuple-element.45), channel_id=1, source_target_pairs={{0,3},{1,0},{2,1},{3,2},{4,7},{5,4},{6,5},{7,6},{8,11},{9,8},{10,9... | collective-permute-start | bytes 786440 | tf_op jit(solution)/shard_map/ppermute | solution.py:295
  24.3 10.7 %collective-permute-start = (bf16[1,128,512]{2,1,0:T(8,128)(2,1)S(1)}, bf16[1,128,512]{2,1,0:T(8,128)(2,1)S(1)}, u32[]{:S(2)}, u32[]{:S(2)}) collective-permute-start(bf16[1,128,512]{2,1,0:T(8,128)(2,1)S(1)} %get-tuple-element.39), channel_id=1, source_target_pairs={{0,1},{1,2},{2,3},{3,0},{4,5},{5,6},{6,7},{7,4},{8,9},{9,10},{10,1... | collective-permute-start | bytes 393224 | tf_op jit(solution)/shard_map/ppermute | solution.py:295
  25.1 13.1 %collective-permute-start.1 = (bf16[1,128,512]{2,1,0:T(8,128)(2,1)S(1)}, bf16[1,128,512]{2,1,0:T(8,128)(2,1)S(1)}, u32[]{:S(2)}, u32[]{:S(2)}) collective-permute-start(bf16[1,128,512]{2,1,0:T(8,128)(2,1)S(1)} %get-tuple-element.40), channel_id=1, source_target_pairs={{0,2},{1,3},{2,0},{3,1},{4,6},{5,7},{6,4},{7,5},{8,10},{9,11},{10,... | collective-permute-start | bytes 393224 | tf_op jit(solution)/shard_map/ppermute | solution.py:295
  25.4 12.8 %collective-permute-start.2 = (bf16[1,128,512]{2,1,0:T(8,128)(2,1)S(1)}, bf16[1,128,512]{2,1,0:T(8,128)(2,1)S(1)}, u32[]{:S(2)}, u32[]{:S(2)}) collective-permute-start(bf16[1,128,512]{2,1,0:T(8,128)(2,1)S(1)} %get-tuple-element.41), channel_id=1, source_target_pairs={{0,3},{1,0},{2,1},{3,2},{4,7},{5,4},{6,5},{7,6},{8,11},{9,8},{10,9... | collective-permute-start | bytes 393224 | tf_op jit(solution)/shard_map/ppermute | solution.py:295
  38.8 9.2 %collective-permute-start.8 = (f32[72,128]{1,0:T(8,128)S(1)}, f32[72,128]{1,0:T(8,128)S(1)}, u32[]{:S(2)}, u32[]{:S(2)}) collective-permute-start(f32[72,128]{1,0:T(8,128)S(1)} %mix.7), channel_id=1, source_target_pairs={{0,3},{1,0},{2,1},{3,2},{4,7},{5,4},{6,5},{7,6},{8,11},{9,8},{10,9... | collective-permute-start | bytes 110600 | tf_op jit(solution)/shard_map/ppermute | solution.py:295
  46.1 4.9 %collective-permute-start.7 = (f32[72,128]{1,0:T(8,128)S(1)}, f32[72,128]{1,0:T(8,128)S(1)}, u32[]{:S(2)}, u32[]{:S(2)}) collective-permute-start(f32[72,128]{1,0:T(8,128)S(1)} %mix.6), channel_id=1, source_target_pairs={{0,2},{1,3},{2,0},{3,1},{4,6},{5,7},{6,4},{7,5},{8,10},{9,11},{10,... | collective-permute-start | bytes 110600 | tf_op jit(solution)/shard_map/ppermute | solution.py:295
  46.8 16.4 %copy-start = (s32[8]{0:T(128)S(1)}, s32[8]{0:T(128)}, u32[]{:S(2)}) copy-start(s32[8]{0:T(128)} %param.23) | copy-start | bytes 100
  46.8 5.8 %collective-permute-start.6 = (f32[72,128]{1,0:T(8,128)S(1)}, f32[72,128]{1,0:T(8,128)S(1)}, u32[]{:S(2)}, u32[]{:S(2)}) collective-permute-start(f32[72,128]{1,0:T(8,128)S(1)} %mix.5), channel_id=1, source_target_pairs={{0,1},{1,2},{2,3},{3,0},{4,5},{5,6},{6,7},{7,4},{8,9},{9,10},{10,1... | collective-permute-start | bytes 110600 | tf_op jit(solution)/shard_map/ppermute | solution.py:295

commit v2 on v1

--- a/solution.py
+++ b/solution.py
@@ -14,6 +14,7 @@
 NEG = -1e30
 STAT_ROWS = 8
 ALIGN = 16
+NEAR = 2
 F32 = jnp.float32
 BF16 = jnp.bfloat16
 EXACT = lax.Precision.HIGHEST
@@ -51,33 +52,40 @@
     return index
 
 
+def partner(rank, k, size):
+    return rank ^ k if size & (size - 1) == 0 else (rank + k) % size
+
+
 def source_rows(sources, k, tok_dev):
-    source = lax.rem(lax.axis_index("seq") + sources - k, sources)
+    rank = lax.axis_index("seq")
+    source = partner(rank, k if sources & (sources - 1) == 0 else sources - k, sources)
     return pl.ds(pl.multiple_of(source * tok_dev, tok_dev), tok_dev)
 
 
-def cut_kernel(sources, count, *refs):
+def summed_here(rank, sources, tok_dev):
+    if sources != 4:
+        return rank * tok_dev, tok_dev, True
+    return rank // 2 * 2 * tok_dev, 2 * tok_dev, (rank == 1) | (rank == 2)
+
+
+def cut_kernel(sources, plan, *refs):
+    count = len(refs) - 1 - len(plan)
     wholes, pieces, sems = refs[:count], refs[count:-1], refs[-1]
     local = pieces[0].shape[2]
     copies = []
-    for k in [*range(1, sources), 0]:
-        target = lax.rem(lax.axis_index("seq") + k, sources)
-        for i in range(count):
-            copies.append(
-                pltpu.make_async_copy(
-                    wholes[i].at[:, pl.ds(pl.multiple_of(target * local, HEAD_DIM), local)],
-                    pieces[k].at[i],
-                    sems.at[k * count + i],
-                )
-            )
+    for (k, which), piece in zip(plan, pieces):
+        target = partner(lax.axis_index("seq"), k, sources)
+        for place, i in enumerate(which):
+            columns = pl.ds(pl.multiple_of(target * local, HEAD_DIM), local)
+            copies.append(pltpu.make_async_copy(wholes[i].at[:, columns], piece.at[place], sems.at[len(copies)]))
             copies[-1].start()
     for copy in copies:
         copy.wait()
 
 
 def prep_kernel(
-    clips, info_ref, act_ref, mod_hbm, wt_hbm, noise_hbm, clean_hbm, kv_hbm,
-    scale_ref, slope_ref, offset_ref, share_ref, weight_ref, keys_ref, values_ref,
+    sources, clips, info_ref, act_ref, mod_hbm, wt_hbm, noise_hbm, clean_hbm, kv_hbm,
+    scale_ref, slope_ref, shift_ref, share_ref, target_ref, weight_ref, keys_ref, values_ref,
     mods, mod_buf, wt_buf, noise_buf, clean_buf, kv_buf, sems,
 ):
     width = wt_buf.shape[1]
@@ -96,17 +104,17 @@
     weight = wt_buf[...].astype(F32)
     slopes = nt_dot(weight, scales, EXACT)
     shifts = nt_dot(weight, mods[:, :width], EXACT)
-    tok_clip = clip_index(info_ref, clips, (clips, tok_dev), 1, rank * tok_dev)
-    picks = (tok_clip == lax.broadcasted_iota(jnp.int32, (clips, tok_dev), 0)).astype(F32)
+    first, count, active = summed_here(rank, sources, tok_dev)
+    tok_clip = clip_index(info_ref, clips, (clips, count), 1, first)
+    picks = (tok_clip == lax.broadcasted_iota(jnp.int32, (clips, count), 0)).astype(F32)
     slot = lax.broadcasted_iota(jnp.int32, (clips, 1), 0)
     sizes = jnp.zeros((clips, 1), F32)
     for c in range(clips):
         sizes = jnp.where(slot == c, info_ref[c].astype(F32), sizes)
-    share_ref[...] = picks / sizes
+    share_ref[...] = jnp.where(active, picks / sizes, 0.0)
     slope_ref[...] = jnp.dot(slopes, picks, precision=EXACT, preferred_element_type=F32)
-    offset_ref[...] = jnp.dot(shifts, picks, precision=EXACT, preferred_element_type=F32) - (
-        noise_buf[...] - clean_buf[...]
-    )
+    shift_ref[...] = jnp.dot(shifts, picks, precision=EXACT, preferred_element_type=F32)
+    target_ref[...] = noise_buf[...] - clean_buf[...]
     row_clip = clip_index(info_ref, clips, (group_rows, clips), 0, 0)
     row_picks = (row_clip == lax.broadcasted_iota(jnp.int32, (group_rows, clips), 1)).astype(F32)
     mine = 1.0 + mods[:, pl.ds(pl.multiple_of(width + rank * local, HEAD_DIM), local)]
@@ -119,13 +127,13 @@
 
 
 def text_kernel(sources, clips, window, info_ref, *refs):
-    qk_refs = refs[:sources]
+    q_refs = refs[:sources]
     keys_ref, values_ref, out_ref, level_ref, q_all = refs[sources:]
-    tok_dev, local = qk_refs[0].shape[1:]
+    tok_dev, local = q_refs[0].shape[1:]
     heads = local // HEAD_DIM
     text_len = keys_ref.shape[1]
-    for k, qk_ref in enumerate(qk_refs):
-        q_all[source_rows(sources, k, tok_dev), :] = qk_ref[0]
+    for k, q_ref in enumerate(q_refs):
+        q_all[source_rows(sources, k, tok_dev), :] = q_ref[0]
     slots = lax.broadcasted_iota(jnp.int32, (1, text_len), 1)
     ones = jnp.ones((text_len, HEAD_DIM), BF16)
 
@@ -165,15 +173,15 @@
 
 
 def weigh_kernel(sources, clips, reach, info_ref, *refs):
-    qk_refs = refs[:sources]
-    text_ref, level_ref, weight_ref, base_ref, q_all, k_all = refs[sources:]
-    tok_dev, local = qk_refs[0].shape[1:]
+    q_refs, kv_refs = refs[:sources], refs[sources : 2 * sources - NEAR]
+    text_ref, level_ref, weight_ref, base_ref, q_all, k_all = refs[2 * sources - NEAR :]
+    tok_dev, local = q_refs[0].shape[1:]
     group_rows = q_all.shape[0]
     heads = local // HEAD_DIM
     for k in range(sources):
         rows = source_rows(sources, k, tok_dev)
-        q_all[rows, :] = qk_refs[k][0]
-        k_all[rows, :] = qk_refs[k][1]
+        q_all[rows, :] = q_refs[k][0]
+        k_all[rows, :] = q_refs[k][1] if k < NEAR else kv_refs[k - NEAR][0]
     for first in range(0, group_rows, tok_dev):
         low = min(max(first - reach[0], 0), group_rows - reach[1])
         rows, span = slice(first, first + tok_dev), slice(low, low + reach[1])
@@ -193,7 +201,7 @@
             base_ref[rows, head_cols(h)] = (fade * share) * text_ref[rows, head_cols(h)]
 
 
-def mix_kernel(sources, reach, ahead, *refs):
+def mix_kernel(sources, reach, place, *refs):
     v_refs = refs[:sources]
     weight_ref, base_ref, scale_ref, wt_ref, out_ref, v_all = refs[sources:]
     tok_dev, local = v_refs[0].shape[1:]
@@ -201,9 +209,10 @@
     heads = local // HEAD_DIM
     channels = wt_ref.shape[0]
     for k in range(sources):
-        v_all[source_rows(sources, k, tok_dev), :] = v_refs[k][0]
-    first = pl.multiple_of(lax.rem(lax.axis_index("seq") + ahead, sources) * tok_dev, tok_dev)
-    rows = pl.ds(first, tok_dev)
+        v_all[source_rows(sources, k, tok_dev), :] = v_refs[k][2 if k < NEAR else 1]
+    count = out_ref.shape[1]
+    first = pl.multiple_of(place(lax.axis_index("seq")) * tok_dev, tok_dev)
+    rows = pl.ds(first, count)
     span = pl.ds(pl.multiple_of(reach_of(first, reach, group_rows), HEAD_DIM), reach[1])
     mixed = [
         jnp.dot(weight_ref[h, rows, :], v_all[span, head_cols(h)], preferred_element_type=F32) for h in range(heads)
@@ -215,24 +224,30 @@
     weight = wt_ref[...]
     every = jnp.ones((STAT_ROWS, local), BF16)
     out_ref[:channels, :] = nt_dot(weight, y_high) + nt_dot(weight, y_low)
-    is_sum = lax.broadcasted_iota(jnp.int32, (STAT_ROWS, tok_dev), 0) == 0
+    is_sum = lax.broadcasted_iota(jnp.int32, (STAT_ROWS, count), 0) == 0
     squares = nt_dot(every, s_high) + nt_dot(every, s_low)
     out_ref[channels:, :] = jnp.where(is_sum, nt_dot(every, attended), squares)
 
 
-def loss_kernel(sources, width, *refs):
-    part_refs = refs[:sources]
-    slope_ref, offset_ref, share_ref, out_ref = refs[sources:]
+def loss_kernel(count, width, *refs):
+    part_refs = refs[:count]
+    slope_ref, shift_ref, share_ref, *target_refs, out_ref = refs[count:]
     channels = slope_ref.shape[0]
     clips = share_ref.shape[0]
     total = part_refs[0][...]
     for part in part_refs[1:]:
         total = total + part[...]
+    targets = [target[...] for target in target_refs]
+    if len(targets) == 2:
+        swap = lax.axis_index("seq") == 1
+        targets = [jnp.where(swap, *targets[::-1]), jnp.where(swap, *targets)]
+    offset = shift_ref[...] - jnp.concatenate(targets, axis=1)
     center = total[channels : channels + 1, :] * (1.0 / width)
     spread = total[channels + 1 : channels + 2, :] * (1.0 / width) - center * center
-    diff = (total[:channels, :] - center * slope_ref[...]) * lax.rsqrt(spread + EPS) + offset_ref[...]
+    diff = (total[:channels, :] - center * slope_ref[...]) * lax.rsqrt(spread + EPS) + offset
     error = jnp.sum(diff * diff, axis=0, keepdims=True) * (1.0 / channels)
-    sums = jnp.sum(share_ref[...] * error, axis=1, keepdims=True)
+    share = share_ref[...]
+    sums = jnp.sum(jnp.where(share > 0.0, share * error, 0.0), axis=1, keepdims=True)
     lanes = lax.broadcasted_iota(jnp.int32, (clips, out_ref.shape[2]), 1)
     mine = lanes == lax.broadcasted_iota(jnp.int32, lanes.shape, 0)
     row = jnp.sum(jnp.where(mine, sums, 0.0), axis=0, keepdims=True)
@@ -283,29 +298,41 @@
     channels = final_weight.shape[1]
     info = jnp.concatenate([clip_lengths[0], text_lengths])
 
-    def cut(arrays, name):
-        return call(
-            functools.partial(cut_kernel, sources, len(arrays)), name, arrays,
-            [((len(arrays), tok_dev, local), BF16)] * sources,
-            [pltpu.SemaphoreType.DMA((sources * len(arrays),))], in_hbm=range(len(arrays)),
-            traffic=4 * tok_dev * width * len(arrays),
+    def cut(arrays, plan, name):
+        count = sum(len(which) for _, which in plan)
+        return list(
+            call(
+                functools.partial(cut_kernel, sources, plan), name, arrays,
+                [((len(which), tok_dev, local), BF16) for _, which in plan],
+                [pltpu.SemaphoreType.DMA((count,))], in_hbm=range(len(arrays)), traffic=4 * tok_dev * local * count,
+            )
         )
 
     def onward(x, k):
-        return lax.ppermute(x, "seq", [(i, (i + k) % sources) for i in range(sources)]) if k else x
-
-    qk_pieces = list(cut([queries, keys], "cut_queries_keys"))
-    qk_pieces[0], values = lax.optimization_barrier((qk_pieces[0], values))
-    qk_blocks = [onward(piece, k) for k, piece in enumerate(qk_pieces)]
-    v_pieces = cut([values], "cut_values")
+        return lax.ppermute(x, "seq", [(i, partner(i, k, sources)) for i in range(sources)]) if k else x
+
+    far = [*range(NEAR, sources)]
+    pieces = cut(
+        [queries, keys, values],
+        [(k, (0,)) for k in far] + [(k, (0, 1, 2)) for k in reversed(range(NEAR))],
+        "cut_first",
+    )
+    pieces[-1], keys = lax.optimization_barrier((pieces[-1], keys))
+    kv_pieces = cut([keys, values], [(k, (0, 1)) for k in far], "cut_far")
+    q_blocks = [onward(piece, k) for k, piece in zip(far, pieces)]
+    near_blocks = [onward(pieces[-1 - k], k) for k in range(NEAR)]
+    q_blocks = near_blocks + q_blocks
+    kv_blocks = [onward(piece, k) for k, piece in zip(far, kv_pieces)]
 
     weight_t = final_weight.T
     activated = jax.nn.silu(step_embedding(timesteps)).astype(BF16)
-    scale_tok, slope, offset, share, weight_local, text_keys, text_values = call(
-        functools.partial(prep_kernel, clips), "prep",
+    _, summed, _ = summed_here(0, sources, tok_dev)
+    scale_tok, slope, shift, share, target, weight_local, text_keys, text_values = call(
+        functools.partial(prep_kernel, sources, clips), "prep",
         [activated, mod_weight, weight_t, noise.T, clean.T, text_kv],
         [
-            ((group_rows, local), F32), ((channels, tok_dev), F32), ((channels, tok_dev), F32), ((clips, tok_dev), F32),
+            ((group_rows, local), F32), ((channels, summed), F32), ((channels, summed), F32), ((clips, summed), F32),
+            ((channels, tok_dev), F32),
             ((channels, local), BF16), ((clips, text_len, local), BF16), ((clips, text_len, local), BF16),
         ],
         [
@@ -317,32 +344,41 @@
         scalars=[info], in_hbm=range(1, 6),
     )
 
-    v_pieces, scale_tok = lax.optimization_barrier((v_pieces, scale_tok))
-    v_blocks = [onward(piece, k) for k, piece in enumerate(v_pieces)]
-
     text_out, level = call(
-        functools.partial(text_kernel, sources, clips, window), "text", [*qk_blocks, text_keys, text_values],
+        functools.partial(text_kernel, sources, clips, window), "text", [*q_blocks, text_keys, text_values],
         [((padded, local), F32), ((heads, padded, HEAD_DIM), F32)],
         [pltpu.VMEM((padded, local), BF16)], scalars=[info],
     )
 
+    targets = [target]
+    if sources == 4:
+        text_out, moved = lax.optimization_barrier((text_out, lax.ppermute(target, "seq", [(0, 1), (3, 2)])))
+        targets.append(moved)
+
     weights, base = call(
-        functools.partial(weigh_kernel, sources, clips, reach), "weigh", [*qk_blocks, text_out, level],
+        functools.partial(weigh_kernel, sources, clips, reach), "weigh", [*q_blocks, *kv_blocks, text_out, level],
         [((heads, group_rows, reach[1]), BF16), ((group_rows, local), F32)],
         [pltpu.VMEM((group_rows, local), BF16)] * 2, scalars=[info],
     )
 
-    parts = [None] * sources
-    for k in [*range(1, sources), 0]:
-        (part,) = call(
-            functools.partial(mix_kernel, sources, reach, k), "mix",
-            [*v_blocks, weights, base, scale_tok, weight_local], [((channels + STAT_ROWS, tok_dev), F32)],
-            [pltpu.VMEM((group_rows, local), BF16)], flops=4 * tok_dev * reach[1] * local, traffic=2**20,
-        )
-        parts[k] = onward(part, k)
+    def mix(place):
+        return call(
+            functools.partial(mix_kernel, sources, reach, place), "mix",
+            [*near_blocks, *kv_blocks, weights, base, scale_tok, weight_local],
+            [((channels + STAT_ROWS, summed), F32)],
+            [pltpu.VMEM((group_rows, local), BF16)], flops=4 * summed * reach[1] * local, traffic=2**20,
+        )[0]
+
+    if sources == 4:
+        here = mix(lambda rank: rank // 2 * 2)
+        parts = [here, lax.ppermute(here, "seq", [(0, 1), (3, 2)])]
+        there = mix(lambda rank: 2 - rank // 2 * 2)
+        parts += [lax.ppermute(there, "seq", pairs) for pairs in ([(0, 2), (3, 1)], [(1, 2), (2, 1)])]
+    else:
+        parts = [onward(mix(lambda rank, k=k: partner(rank, k, sources)), k) for k in reversed(range(sources))]
 
     (shares,) = call(
-        functools.partial(loss_kernel, sources, width), "loss", [*parts, slope, offset, share],
+        functools.partial(loss_kernel, len(parts), width), "loss", [*parts, slope, shift, share, *targets],
         [((groups * sources, 1, HEAD_DIM), F32)],
     )
     everyone = lax.all_to_all(shares, ("dp", "seq"), split_axis=0, concat_axis=0, tiled=True)

time: 64 us -> 67.5 us (1.055)
  starting transfers between devices: 18.3 us -> 23.8 us
  waiting for transfers between devices: 7.74 us -> 6.2 us
  other arithmetic: 2.25 us -> 0.92 us
  blocking collectives: 10.3 us -> 11.6 us
    ppermute x9, starting transfers between devices: 18.3 us -> 23.8 us  [the longest x5 9.65 us: onward(): lax.ppermute(x, 'seq', [(i, partner(i, k, sources)) for i in range(source...]
    ppermute x9, waiting for transfers between devices: 7.74 us -> 6.2 us  [the longest x5 4.26 us: onward(): lax.ppermute(x, 'seq', [(i, partner(i, k, sources)) for i in range(source...]
    all_to_all x1, blocking collectives: 10.3 us -> 11.6 us  [per_device(): lax.all_to_all(shares, ('dp', 'seq'), split_axis=0, concat_axis=0, tiled=...]
    pallas_call x10 -> x8, Pallas kernels: 25 us -> 24.5 us  [call(): pl.pallas_call(kernel, in_specs=[smem()] * len(scalars) + [hbm() if i in...]
  transfers between devices with their start and end apart: 9 -> 9, of which waited for: 3 -> 2; matrix products, arithmetic and copies ran while one was open for 2% -> 0% of each run, Pallas kernels for 36% -> 29%
where the time goes in v2:
time: 67.5 us; the launch traced here: 67.3 us
  Pallas kernels  24.5 us (36%)
  starting transfers between devices  23.8 us (35%)
  blocking collectives  11.6 us (17%)
  waiting for transfers between devices  6.2 us (9%)
  other arithmetic  0.92 us (1%)
    pallas_call x8, Pallas kernels, call(): pl.pallas_call(kernel, in_specs=[smem()] * len(scalars) + [hbm() if i in...  24.5 us
    all_to_all x1, blocking collectives, per_device(): lax.all_to_all(shares, ('dp', 'seq'), split_axis=0, concat_axis=0, tiled=...  11.6 us
    ppermute x5, starting transfers between devices, onward(): lax.ppermute(x, 'seq', [(i, partner(i, k, sources)) for i in range(source...  9.65 us
    ppermute x2, starting transfers between devices, per_device(): lax.ppermute(there, 'seq', pairs)  8.47 us
    ppermute x5, waiting for transfers between devices, onward(): lax.ppermute(x, 'seq', [(i, partner(i, k, sources)) for i in range(source...  4.26 us
    ppermute x1, starting transfers between devices, per_device(): parts = [here, lax.ppermute(here, 'seq', [(0, 1), (3, 2)])]  3.1 us
    ppermute x1, starting transfers between devices, per_device(): lax.ppermute(target, 'seq', [(0, 1), (3, 2)])  2.58 us
    ppermute x1, waiting for transfers between devices, per_device(): parts = [here, lax.ppermute(here, 'seq', [(0, 1), (3, 2)])]  1.94 us
  transfers between devices with their start and end apart: 9, of which 2 were waited for; matrix products, arithmetic and copies ran while one was open for 0% of the time, Pallas kernels for 29%

profile of v2, /device:TPU:0, one launch (start us, length us, event | category | flops | bytes accessed | tf_op | source)
XLA Modules:
  0.0 67.3 jit_solution(14588288359494800598)
XLA Ops:
  0.0 1.4 %cut_first.1 = (bf16[1,128,512]{2,1,0:T(8,128)(2,1)S(1)}, bf16[1,128,512]{2,1,0:T(8,128)(2,1)S(1)}, bf16[3,128,512]{2,1,0:T(8,128)(2,1)S(1)}, bf16[3,128,512]{2,1,0:T(8,128)(2,1)S(1)}) custom-call(bf16[128,2048]{1,0:T(8,128)(2,1)} %refs_0_.1, bf16[128,2048]{1,0:T(8,128)(2,1)} %refs_0_.2, bf16[128,2048]{1,0:T(8,128)(2,1)} %refs_1_.3), custom_call_target="tpu_custom_call" | custom-call | bytes 2097152 | tf_op jit(solution)/shard_map/cut_first/pallas_call | solution.py:270
  1.4 3.1 %collective-permute-start = (bf16[3,128,512]{2,1,0:T(8,128)(2,1)S(1)}, bf16[3,128,512]{2,1,0:T(8,128)(2,1)S(1)}, u32[]{:S(2)}, u32[]{:S(2)}) collective-permute-start(bf16[3,128,512]{2,1,0:T(8,128)(2,1)S(1)} %get-tuple-element.29), channel_id=1, source_target_pairs={{0,1},{1,0},{2,3},{3,2},{4,5},{5,4},{6,7},{7,6},{8,9},{9,8},{10,11... | collective-permute-start | bytes 1179656 | tf_op jit(solution)/shard_map/ppermute | solution.py:312
  4.5 2.6 %collective-permute-start.3 = (bf16[1,128,512]{2,1,0:T(8,128)(2,1)S(1)}, bf16[1,128,512]{2,1,0:T(8,128)(2,1)S(1)}, u32[]{:S(2)}, u32[]{:S(2)}) collective-permute-start(bf16[1,128,512]{2,1,0:T(8,128)(2,1)S(1)} %get-tuple-element.33), channel_id=1, source_target_pairs={{0,2},{1,3},{2,0},{3,1},{4,6},{5,7},{6,4},{7,5},{8,10},{9,11},{10,... | collective-permute-start | bytes 393224 | tf_op jit(solution)/shard_map/ppermute | solution.py:312
  7.1 0.0 collective-permute-start.4
  7.1 1.1 %cut_far.1 = (bf16[2,128,512]{2,1,0:T(8,128)(2,1)S(1)}, bf16[2,128,512]{2,1,0:T(8,128)(2,1)S(1)}) custom-call(bf16[128,2048]{1,0:T(8,128)(2,1)} %refs_0_.2, bf16[128,2048]{1,0:T(8,128)(2,1)} %refs_1_.3), custom_call_target="tpu_custom_call" | custom-call | bytes 1048576 | tf_op jit(solution)/shard_map/cut_far/pallas_call | solution.py:270
  8.2 2.0 %collective-permute-start.1 = (bf16[2,128,512]{2,1,0:T(8,128)(2,1)S(1)}, bf16[2,128,512]{2,1,0:T(8,128)(2,1)S(1)}, u32[]{:S(2)}, u32[]{:S(2)}) collective-permute-start(bf16[2,128,512]{2,1,0:T(8,128)(2,1)S(1)} %get-tuple-element.31), channel_id=1, source_target_pairs={{0,2},{1,3},{2,0},{3,1},{4,6},{5,7},{6,4},{7,5},{8,10},{9,11},{10,... | collective-permute-start | bytes 786440 | tf_op jit(solution)/shard_map/ppermute | solution.py:312
  10.2 2.0 %collective-permute-start.2 = (bf16[2,128,512]{2,1,0:T(8,128)(2,1)S(1)}, bf16[2,128,512]{2,1,0:T(8,128)(2,1)S(1)}, u32[]{:S(2)}, u32[]{:S(2)}) collective-permute-start(bf16[2,128,512]{2,1,0:T(8,128)(2,1)S(1)} %get-tuple-element.32), channel_id=1, source_target_pairs={{0,3},{1,2},{2,1},{3,0},{4,7},{5,6},{6,5},{7,4},{8,11},{9,10},{10,... | collective-permute-start | bytes 786440 | tf_op jit(solution)/shard_map/ppermute | solution.py:312
  12.2 0.1 multiply_cosine_fusion
  12.3 0.0 copy-done.2
  12.4 0.1 pad_add_fusion.info_ref
  12.4 13.3 %prep.1 = (f32[512,512]{1,0:T(8,128)S(1)}, f32[64,256]{1,0:T(8,128)S(1)}, f32[64,256]{1,0:T(8,128)S(1)}, f32[8,256]{1,0:T(8,128)S(1)}, f32[64,128]{1,0:T(8,128)S...) custom-call(s32[16]{0:T(128)S(1)} %pad_add_fusion.info_ref, ...), custom_call_target="tpu_custom_call" | custom-call | tf_op jit(solution)/shard_map/prep/pallas_call | solution.py:270
  25.7 0.0 collective-permute-done.3.refs_2_
  25.8 2.6 %collective-permute-start.5 = (f32[64,128]{1,0:T(8,128)S(1)}, f32[64,128]{1,0:T(8,128)S(1)}, u32[]{:S(2)}, u32[]{:S(2)}) collective-permute-start(f32[64,128]{1,0:T(8,128)S(1)} %get-tuple-element.38.refs_7_), channel_id=1, source_target_pairs={{0,1},{3,2},{4,5},{7,6},{8,9},{11,10},{12,13},{15,14},{16,17},{19,... | collective-permute-start | bytes 98312 | tf_op jit(solution)/shard_map/ppermute | solution.py:355
  28.3 0.0 collective-permute-done.4.refs_3_
  28.4 0.0 collective-permute-done.refs_1_
  28.4 4.5 %text.1 = (f32[656,512]{1,0:T(8,128)S(1)}, f32[4,656,128]{2,1,0:T(8,128)S(1)}) custom-call(s32[16]{0:T(128)S(1)} %pad_add_fusion.info_ref, bf16[3,128,512]{2,1,0:T(8,128)(2,1)S(1)} %get-tuple-element.28.refs_0_, bf16[3,128,512]{2,1,0:T(8,128)(2,1)S(1)} %collective-permute-done.refs_1_, bf16[1,128,512]{2,1,0:T(8,128)(2,1)S(1)} %collective-permute-done.3.refs_2_, ...), custom_call_target="tpu_custom_call" | custom-call | tf_op jit(solution)/shard_map/text/pallas_call | solution.py:270
  32.8 0.0 collective-permute-done.5.refs_8_
  32.9 4.2 %collective-permute-done.1.refs_4_.refs_2_ = bf16[2,128,512]{2,1,0:T(8,128)(2,1)S(1)} collective-permute-done((bf16[2,128,512]{2,1,0:T(8,128)(2,1)S(1)}, bf16[2,128,512]{2,1,0:T(8,128)(2,1)S(1)}, u32[]{:S(2)}, u32[]{:S(2)}) %collective-permute-start.1) | collective-permute-done | bytes 262176 | tf_op jit(solution)/shard_map/ppermute | solution.py:312
  37.1 0.0 collective-permute-done.2.refs_5_.refs_3_
  37.1 2.2 %weigh.1 = (bf16[4,512,384]{2,1,0:T(8,128)(2,1)S(1)}, f32[512,512]{1,0:T(8,128)S(1)}) custom-call(s32[16]{0:T(128)S(1)} %pad_add_fusion.info_ref, bf16[3,128,512]{2,1,0:T(8,128)(2,1)S(1)} %get-tuple-element.28.refs_0_, bf16[3,128,512]{2,1,0:T(8,128)(2,1)S(1)} %collective-permute-done.refs_1_, bf16[1,128,512]{2,1,0:T(8,128)(2,1)S(1)} %collective-permute-done.3.refs_2_, ...), custom_call_target="tpu_custom_call" | custom-call | tf_op jit(solution)/shard_map/weigh/pallas_call | solution.py:270
  39.4 0.9 %mix.3 = f32[72,256]{1,0:T(8,128)S(1)} custom-call(bf16[3,128,512]{2,1,0:T(8,128)(2,1)S(1)} %get-tuple-element.28.refs_0_, bf16[3,128,512]{2,1,0:T(8,128)(2,1)S(1)} %collective-permute-done.refs_1_, bf16[2,128,512]{2,1,0:T(8,128)(2,1)S(1)} %collective-permute-done.1.refs_4_.refs_2_, bf16[2,128,512]{2,1,0:T(8,128)(2,1)S(1)} %collective-permute-done.2.refs_5_.refs_3_, ...), custom_call_target="tpu_custom_call" | custom-call | flops 201326592 | bytes 1048576 | tf_op jit(solution)/shard_map/mix/pallas_call | solution.py:270
  40.3 7.8 %collective-permute-start.7 = (f32[72,256]{1,0:T(8,128)S(1)}, f32[72,256]{1,0:T(8,128)S(1)}, u32[]{:S(2)}, u32[]{:S(2)}) collective-permute-start(f32[72,256]{1,0:T(8,128)S(1)} %mix.3), channel_id=1, source_target_pairs={{0,2},{3,1},{4,6},{7,5},{8,10},{11,9},{12,14},{15,13},{16,18},{19,... | collective-permute-start | bytes 221192 | tf_op jit(solution)/shard_map/ppermute | solution.py:376
  48.1 0.7 collective-permute-start.8
  48.8 0.9 %mix.2.refs_0_ = f32[72,256]{1,0:T(8,128)S(1)} custom-call(bf16[3,128,512]{2,1,0:T(8,128)(2,1)S(1)} %get-tuple-element.28.refs_0_, bf16[3,128,512]{2,1,0:T(8,128)(2,1)S(1)} %collective-permute-done.refs_1_, bf16[2,128,512]{2,1,0:T(8,128)(2,1)S(1)} %collective-permute-done.1.refs_4_.refs_2_, bf16[2,128,512]{2,1,0:T(8,128)(2,1)S(1)} %collective-permute-done.2.refs_5_.refs_3_, ...), custom_call_target="tpu_custom_call" | custom-call | flops 201326592 | bytes 1048576 | tf_op jit(solution)/shard_map/mix/pallas_call | solution.py:270
  49.7 3.1 %collective-permute-start.6 = (f32[72,256]{1,0:T(8,128)S(1)}, f32[72,256]{1,0:T(8,128)S(1)}, u32[]{:S(2)}, u32[]{:S(2)}) collective-permute-start(f32[72,256]{1,0:T(8,128)S(1)} %mix.2.refs_0_), channel_id=1, source_target_pairs={{0,1},{3,2},{4,5},{7,6},{8,9},{11,10},{12,13},{15,14},{16,17},{19,... | collective-permute-start | bytes 221192 | tf_op jit(solution)/shard_map/ppermute | solution.py:374
  52.8 0.0 collective-permute-done.7.refs_2_
  52.8 0.0 collective-permute-done.8.refs_3_
  52.8 1.9 %collective-permute-done.6.refs_1_ = f32[72,256]{1,0:T(8,128)S(1)} collective-permute-done((f32[72,256]{1,0:T(8,128)S(1)}, f32[72,256]{1,0:T(8,128)S(1)}, u32[]{:S(2)}, u32[]{:S(2)}) %collective-permute-start.6) | collective-permute-done | bytes 73760 | tf_op jit(solution)/shard_map/ppermute | solution.py:374
  54.7 0.1 loss.1
  54.9 11.6 %all_to_all.5 = f32[32,1,128]{2,1,0:T(1,128)S(1)} all-to-all(f32[32,1,128]{2,1,0:T(1,128)S(1)} %loss.1), channel_id=1, replica_groups=mesh['dp'=8,'seq'=4] {'dp','seq'}, dimensions={0} | all-to-all | bytes 32768 | tf_op jit(solution)/shard_map/all_to_all | solution.py:384
  66.5 0.1 broadcast_in_dim.18
  66.6 0.7 %select_reduce_fusion = f32[8]{0:T(128)} fusion(f32[64]{0:T(128)S(1)} %broadcast_in_dim.18, s32[8]{0:T(128)S(1)} %copy-done.3), kind=kLoop, calls=%fused_computation.4 | loop fusion | flops 1528 | bytes 320 | tf_op jit(solution)/shard_map/reduce_sum | solution.py:387
  (11 shorter events, 0.1 us)
Async XLA Ops:
  0.0 12.2 %copy-start = (s32[8]{0:T(128)S(1)}, s32[8]{0:T(128)}, u32[]{:S(2)}) copy-start(s32[8]{0:T(128)} %param.18) | copy-start | bytes 100
  0.0 12.3 %copy-start.2 = (s32[1,8]{1,0:T(1,128)S(1)}, s32[1,8]{1,0:T(1,128)}, u32[]{:S(2)}) copy-start(s32[1,8]{1,0:T(1,128)} %param.17) | copy-start | bytes 100
  0.0 12.3 %copy-start.1 = (s32[8]{0:T(128)S(1)}, s32[8]{0:T(128)}, u32[]{:S(2)}) copy-start(s32[8]{0:T(128)} %param.16) | copy-start | bytes 100
  1.4 27.0 %collective-permute-start = (bf16[3,128,512]{2,1,0:T(8,128)(2,1)S(1)}, bf16[3,128,512]{2,1,0:T(8,128)(2,1)S(1)}, u32[]{:S(2)}, u32[]{:S(2)}) collective-permute-start(bf16[3,128,512]{2,1,0:T(8,128)(2,1)S(1)} %get-tuple-element.29), channel_id=1, source_target_pairs={{0,1},{1,0},{2,3},{3,2},{4,5},{5,4},{6,7},{7,6},{8,9},{9,8},{10,11... | collective-permute-start | bytes 1179656 | tf_op jit(solution)/shard_map/ppermute | solution.py:312
  4.5 21.3 %collective-permute-start.3 = (bf16[1,128,512]{2,1,0:T(8,128)(2,1)S(1)}, bf16[1,128,512]{2,1,0:T(8,128)(2,1)S(1)}, u32[]{:S(2)}, u32[]{:S(2)}) collective-permute-start(bf16[1,128,512]{2,1,0:T(8,128)(2,1)S(1)} %get-tuple-element.33), channel_id=1, source_target_pairs={{0,2},{1,3},{2,0},{3,1},{4,6},{5,7},{6,4},{7,5},{8,10},{9,11},{10,... | collective-permute-start | bytes 393224 | tf_op jit(solution)/shard_map/ppermute | solution.py:312
  7.1 21.3 %collective-permute-start.4 = (bf16[1,128,512]{2,1,0:T(8,128)(2,1)S(1)}, bf16[1,128,512]{2,1,0:T(8,128)(2,1)S(1)}, u32[]{:S(2)}, u32[]{:S(2)}) collective-permute-start(bf16[1,128,512]{2,1,0:T(8,128)(2,1)S(1)} %get-tuple-element.34), channel_id=1, source_target_pairs={{0,3},{1,2},{2,1},{3,0},{4,7},{5,6},{6,5},{7,4},{8,11},{9,10},{10,... | collective-permute-start | bytes 393224 | tf_op jit(solution)/shard_map/ppermute | solution.py:312
  8.2 28.9 %collective-permute-start.1 = (bf16[2,128,512]{2,1,0:T(8,128)(2,1)S(1)}, bf16[2,128,512]{2,1,0:T(8,128)(2,1)S(1)}, u32[]{:S(2)}, u32[]{:S(2)}) collective-permute-start(bf16[2,128,512]{2,1,0:T(8,128)(2,1)S(1)} %get-tuple-element.31), channel_id=1, source_target_pairs={{0,2},{1,3},{2,0},{3,1},{4,6},{5,7},{6,4},{7,5},{8,10},{9,11},{10,... | collective-permute-start | bytes 786440 | tf_op jit(solution)/shard_map/ppermute | solution.py:312
  10.2 26.9 %collective-permute-start.2 = (bf16[2,128,512]{2,1,0:T(8,128)(2,1)S(1)}, bf16[2,128,512]{2,1,0:T(8,128)(2,1)S(1)}, u32[]{:S(2)}, u32[]{:S(2)}) collective-permute-start(bf16[2,128,512]{2,1,0:T(8,128)(2,1)S(1)} %get-tuple-element.32), channel_id=1, source_target_pairs={{0,3},{1,2},{2,1},{3,0},{4,7},{5,6},{6,5},{7,4},{8,11},{9,10},{10,... | collective-permute-start | bytes 786440 | tf_op jit(solution)/shard_map/ppermute | solution.py:312
  25.8 7.1 %collective-permute-start.5 = (f32[64,128]{1,0:T(8,128)S(1)}, f32[64,128]{1,0:T(8,128)S(1)}, u32[]{:S(2)}, u32[]{:S(2)}) collective-permute-start(f32[64,128]{1,0:T(8,128)S(1)} %get-tuple-element.38.refs_7_), channel_id=1, source_target_pairs={{0,1},{3,2},{4,5},{7,6},{8,9},{11,10},{12,13},{15,14},{16,17},{19,... | collective-permute-start | bytes 98312 | tf_op jit(solution)/shard_map/ppermute | solution.py:355
  40.3 26.3 %copy-start.3 = (s32[8]{0:T(128)S(1)}, s32[8]{0:T(128)}, u32[]{:S(2)}) copy-start(s32[8]{0:T(128)} %param.23) | copy-start | bytes 100
  40.3 12.5 %collective-permute-start.7 = (f32[72,256]{1,0:T(8,128)S(1)}, f32[72,256]{1,0:T(8,128)S(1)}, u32[]{:S(2)}, u32[]{:S(2)}) collective-permute-start(f32[72,256]{1,0:T(8,128)S(1)} %mix.3), channel_id=1, source_target_pairs={{0,2},{3,1},{4,6},{7,5},{8,10},{11,9},{12,14},{15,13},{16,18},{19,... | collective-permute-start | bytes 221192 | tf_op jit(solution)/shard_map/ppermute | solution.py:376
  48.1 4.7 %collective-permute-start.8 = (f32[72,256]{1,0:T(8,128)S(1)}, f32[72,256]{1,0:T(8,128)S(1)}, u32[]{:S(2)}, u32[]{:S(2)}) collective-permute-start(f32[72,256]{1,0:T(8,128)S(1)} %mix.3), channel_id=1, source_target_pairs={{1,2},{2,1},{5,6},{6,5},{9,10},{10,9},{13,14},{14,13},{17,18},{18,... | collective-permute-start | bytes 221192 | tf_op jit(solution)/shard_map/ppermute | solution.py:376
  49.7 5.1 %collective-permute-start.6 = (f32[72,256]{1,0:T(8,128)S(1)}, f32[72,256]{1,0:T(8,128)S(1)}, u32[]{:S(2)}, u32[]{:S(2)}) collective-permute-start(f32[72,256]{1,0:T(8,128)S(1)} %mix.2.refs_0_), channel_id=1, source_target_pairs={{0,1},{3,2},{4,5},{7,6},{8,9},{11,10},{12,13},{15,14},{16,17},{19,... | collective-permute-start | bytes 221192 | tf_op jit(solution)/shard_map/ppermute | solution.py:374

commit v3 on v2

--- a/solution.py
+++ b/solution.py
@@ -173,7 +173,7 @@
 
 
 def weigh_kernel(sources, clips, reach, info_ref, *refs):
-    q_refs, kv_refs = refs[:sources], refs[sources : 2 * sources - NEAR]
+    q_refs, k_refs = refs[:sources], refs[sources : 2 * sources - NEAR]
     text_ref, level_ref, weight_ref, base_ref, q_all, k_all = refs[2 * sources - NEAR :]
     tok_dev, local = q_refs[0].shape[1:]
     group_rows = q_all.shape[0]
@@ -181,7 +181,7 @@
     for k in range(sources):
         rows = source_rows(sources, k, tok_dev)
         q_all[rows, :] = q_refs[k][0]
-        k_all[rows, :] = q_refs[k][1] if k < NEAR else kv_refs[k - NEAR][0]
+        k_all[rows, :] = q_refs[k][1] if k < NEAR else k_refs[k - NEAR][0]
     for first in range(0, group_rows, tok_dev):
         low = min(max(first - reach[0], 0), group_rows - reach[1])
         rows, span = slice(first, first + tok_dev), slice(low, low + reach[1])
@@ -209,7 +209,7 @@
     heads = local // HEAD_DIM
     channels = wt_ref.shape[0]
     for k in range(sources):
-        v_all[source_rows(sources, k, tok_dev), :] = v_refs[k][2 if k < NEAR else 1]
+        v_all[source_rows(sources, k, tok_dev), :] = v_refs[k][2 if k < NEAR else 0]
     count = out_ref.shape[1]
     first = pl.multiple_of(place(lax.axis_index("seq")) * tok_dev, tok_dev)
     rows = pl.ds(first, count)
@@ -266,15 +266,15 @@
     return pl.BlockSpec(memory_space=pltpu.HBM)
 
 
-def call(kernel, name, operands, results, scratch=(), scalars=(), in_hbm=(), limit=VMEM_LIMIT, flops=0, traffic=0, exps=0):
+def call(kernel, name, operands, results, scratch=(), scalars=(), in_hbm=(), pinned=True, flops=0, traffic=0):
     return pl.pallas_call(
         kernel,
         in_specs=[smem()] * len(scalars) + [hbm() if i in in_hbm else vmem() for i in range(len(operands))],
         out_specs=[vmem()] * len(results),
-        out_shape=[pltpu.VMEM(*r) for r in results],
+        out_shape=[pltpu.VMEM(*r) if pinned else jax.ShapeDtypeStruct(*r) for r in results],
         scratch_shapes=list(scratch),
-        compiler_params=pltpu.CompilerParams(vmem_limit_bytes=limit),
-        cost_estimate=pl.CostEstimate(flops=flops, bytes_accessed=traffic, transcendentals=exps),
+        compiler_params=pltpu.CompilerParams(vmem_limit_bytes=VMEM_LIMIT),
+        cost_estimate=pl.CostEstimate(flops=flops, bytes_accessed=traffic, transcendentals=0),
         name=name,
     )(*scalars, *(pltpu.with_memory_space_constraint(x, pltpu.HBM) if i in in_hbm else x for i, x in enumerate(operands)))
 
@@ -312,17 +312,17 @@
         return lax.ppermute(x, "seq", [(i, partner(i, k, sources)) for i in range(sources)]) if k else x
 
     far = [*range(NEAR, sources)]
+    q_pieces = cut([queries], [(k, (0,)) for k in far], "cut_first")
+    q_blocks = [onward(piece, k) for k, piece in zip(far, q_pieces)]
+    q_pieces[0], keys = lax.optimization_barrier((q_pieces[0], keys))
     pieces = cut(
         [queries, keys, values],
-        [(k, (0,)) for k in far] + [(k, (0, 1, 2)) for k in reversed(range(NEAR))],
-        "cut_first",
-    )
-    pieces[-1], keys = lax.optimization_barrier((pieces[-1], keys))
-    kv_pieces = cut([keys, values], [(k, (0, 1)) for k in far], "cut_far")
-    q_blocks = [onward(piece, k) for k, piece in zip(far, pieces)]
-    near_blocks = [onward(pieces[-1 - k], k) for k in range(NEAR)]
+        [(k, (0, 1, 2)) for k in reversed(range(NEAR))] + [(k, (i,)) for i in (1, 2) for k in far],
+        "cut_rest",
+    )
+    near_blocks = [onward(pieces[NEAR - 1 - k], k) for k in range(NEAR)]
     q_blocks = near_blocks + q_blocks
-    kv_blocks = [onward(piece, k) for k, piece in zip(far, kv_pieces)]
+    k_blocks = [onward(piece, k) for k, piece in zip(far, pieces[NEAR:])]
 
     weight_t = final_weight.T
     activated = jax.nn.silu(step_embedding(timesteps)).astype(BF16)
@@ -344,19 +344,23 @@
         scalars=[info], in_hbm=range(1, 6),
     )
 
+    v_pieces, scale_tok = lax.optimization_barrier((pieces[NEAR + len(far) :], scale_tok))
+    v_blocks = [onward(piece, k) for k, piece in zip(far, v_pieces)]
+
     text_out, level = call(
         functools.partial(text_kernel, sources, clips, window), "text", [*q_blocks, text_keys, text_values],
         [((padded, local), F32), ((heads, padded, HEAD_DIM), F32)],
         [pltpu.VMEM((padded, local), BF16)], scalars=[info],
     )
 
+    swap = [(0, 1), (1, 0), (2, 3), (3, 2)]
     targets = [target]
     if sources == 4:
-        text_out, moved = lax.optimization_barrier((text_out, lax.ppermute(target, "seq", [(0, 1), (3, 2)])))
+        text_out, moved = lax.optimization_barrier((text_out, lax.ppermute(target, "seq", swap)))
         targets.append(moved)
 
     weights, base = call(
-        functools.partial(weigh_kernel, sources, clips, reach), "weigh", [*q_blocks, *kv_blocks, text_out, level],
+        functools.partial(weigh_kernel, sources, clips, reach), "weigh", [*q_blocks, *k_blocks, text_out, level],
         [((heads, group_rows, reach[1]), BF16), ((group_rows, local), F32)],
         [pltpu.VMEM((group_rows, local), BF16)] * 2, scalars=[info],
     )
@@ -364,16 +368,17 @@
     def mix(place):
         return call(
             functools.partial(mix_kernel, sources, reach, place), "mix",
-            [*near_blocks, *kv_blocks, weights, base, scale_tok, weight_local],
+            [*near_blocks, *v_blocks, weights, base, scale_tok, weight_local],
             [((channels + STAT_ROWS, summed), F32)],
             [pltpu.VMEM((group_rows, local), BF16)], flops=4 * summed * reach[1] * local, traffic=2**20,
         )[0]
 
     if sources == 4:
         here = mix(lambda rank: rank // 2 * 2)
-        parts = [here, lax.ppermute(here, "seq", [(0, 1), (3, 2)])]
+        parts = [here, lax.ppermute(here, "seq", swap)]
         there = mix(lambda rank: 2 - rank // 2 * 2)
-        parts += [lax.ppermute(there, "seq", pairs) for pairs in ([(0, 2), (3, 1)], [(1, 2), (2, 1)])]
+        for pairs in ([(1, 2), (2, 1), (0, 0), (3, 3)], [(0, 2), (2, 3), (3, 1), (1, 0)]):
+            parts.append(lax.ppermute(there, "seq", pairs))
     else:
         parts = [onward(mix(lambda rank, k=k: partner(rank, k, sources)), k) for k in reversed(range(sources))]
 

time: 67.5 us -> 61.4 us (0.910)
  starting transfers between devices: 23.8 us -> 20.8 us
  waiting for transfers between devices: 6.2 us -> 3.5 us
    ppermute x4, starting transfers between devices: 14.2 us -> 8.19 us  [the longest x2 5.67 us: per_device(): parts.append(lax.ppermute(there, 'seq', pairs))]
    ppermute x5 -> x7, waiting for transfers between devices: 4.26 us -> 1.09 us  [onward(): lax.ppermute(x, 'seq', [(i, partner(i, k, sources)) for i in range(source...]
    ppermute x5 -> x7, starting transfers between devices: 9.65 us -> 12.6 us  [onward(): lax.ppermute(x, 'seq', [(i, partner(i, k, sources)) for i in range(source...]
  transfers between devices with their start and end apart: 9 -> 11, of which waited for: 2 -> 2; matrix products, arithmetic and copies ran while one was open for 0% -> 0% of each run, Pallas kernels for 29% -> 37%
where the time goes in v3:
time: 61.4 us; the launch traced here: 61.2 us
  Pallas kernels  24.7 us (40%)
  starting transfers between devices  20.8 us (34%)
  blocking collectives  11.2 us (18%)
  waiting for transfers between devices  3.5 us (6%)
  other arithmetic  0.92 us (1%)
    pallas_call x8, Pallas kernels, call(): pl.pallas_call(kernel, in_specs=[smem()] * len(scalars) + [hbm() if i in...  24.7 us
    ppermute x7, starting transfers between devices, onward(): lax.ppermute(x, 'seq', [(i, partner(i, k, sources)) for i in range(source...  12.6 us
    all_to_all x1, blocking collectives, per_device(): lax.all_to_all(shares, ('dp', 'seq'), split_axis=0, concat_axis=0, tiled=...  11.2 us
    ppermute x2, starting transfers between devices, per_device(): parts.append(lax.ppermute(there, 'seq', pairs))  5.67 us
    ppermute x1, waiting for transfers between devices, per_device(): parts = [here, lax.ppermute(here, 'seq', swap)]  2.4 us
    ppermute x1, starting transfers between devices, per_device(): parts = [here, lax.ppermute(here, 'seq', swap)]  1.96 us
  transfers between devices with their start and end apart: 11, of which 2 were waited for; matrix products, arithmetic and copies ran while one was open for 0% of the time, Pallas kernels for 37%

profile of v3, /device:TPU:0, one launch (start us, length us, event | category | flops | bytes accessed | tf_op | source)
XLA Modules:
  0.0 61.2 jit_solution(16833145252924425250)
XLA Ops:
  0.0 1.0 %cut_first.1 = (bf16[1,128,512]{2,1,0:T(8,128)(2,1)S(1)}, bf16[1,128,512]{2,1,0:T(8,128)(2,1)S(1)}) custom-call(bf16[128,2048]{1,0:T(8,128)(2,1)} %refs_0_.3), custom_call_target="tpu_custom_call" | custom-call | bytes 524288 | tf_op jit(solution)/shard_map/cut_first/pallas_call | solution.py:270
  1.0 4.1 %collective-permute-start.3 = (bf16[1,128,512]{2,1,0:T(8,128)(2,1)S(1)}, bf16[1,128,512]{2,1,0:T(8,128)(2,1)S(1)}, u32[]{:S(2)}, u32[]{:S(2)}) collective-permute-start(bf16[1,128,512]{2,1,0:T(8,128)(2,1)S(1)} %get-tuple-element.31), channel_id=1, source_target_pairs={{0,2},{1,3},{2,0},{3,1},{4,6},{5,7},{6,4},{7,5},{8,10},{9,11},{10,... | collective-permute-start | bytes 393224 | tf_op jit(solution)/shard_map/ppermute | solution.py:312
  5.1 1.5 %cut_rest.1 = (bf16[3,128,512]{2,1,0:T(8,128)(2,1)S(1)}, bf16[3,128,512]{2,1,0:T(8,128)(2,1)S(1)}, bf16[1,128,512]{2,1,0:T(8,128)(2,1)S(1)}, bf16[1,128,512]{2,1...) custom-call(bf16[128,2048]{1,0:T(8,128)(2,1)} %refs_0_.3, ...), custom_call_target="tpu_custom_call" | custom-call | bytes 2621440 | tf_op jit(solution)/shard_map/cut_rest/pallas_call | solution.py:270
  6.6 1.6 %collective-permute-start = (bf16[3,128,512]{2,1,0:T(8,128)(2,1)S(1)}, bf16[3,128,512]{2,1,0:T(8,128)(2,1)S(1)}, u32[]{:S(2)}, u32[]{:S(2)}) collective-permute-start(bf16[3,128,512]{2,1,0:T(8,128)(2,1)S(1)} %get-tuple-element.34), channel_id=1, source_target_pairs={{0,1},{1,0},{2,3},{3,2},{4,5},{5,4},{6,7},{7,6},{8,9},{9,8},{10,11... | collective-permute-start | bytes 1179656 | tf_op jit(solution)/shard_map/ppermute | solution.py:312
  8.2 0.0 collective-permute-start.4
  8.2 1.9 %collective-permute-start.5 = (bf16[1,128,512]{2,1,0:T(8,128)(2,1)S(1)}, bf16[1,128,512]{2,1,0:T(8,128)(2,1)S(1)}, u32[]{:S(2)}, u32[]{:S(2)}) collective-permute-start(bf16[1,128,512]{2,1,0:T(8,128)(2,1)S(1)} %get-tuple-element.41), channel_id=1, source_target_pairs={{0,2},{1,3},{2,0},{3,1},{4,6},{5,7},{6,4},{7,5},{8,10},{9,11},{10,... | collective-permute-start | bytes 393224 | tf_op jit(solution)/shard_map/ppermute | solution.py:312
  10.2 1.9 %collective-permute-start.6 = (bf16[1,128,512]{2,1,0:T(8,128)(2,1)S(1)}, bf16[1,128,512]{2,1,0:T(8,128)(2,1)S(1)}, u32[]{:S(2)}, u32[]{:S(2)}) collective-permute-start(bf16[1,128,512]{2,1,0:T(8,128)(2,1)S(1)} %get-tuple-element.42), channel_id=1, source_target_pairs={{0,3},{1,2},{2,1},{3,0},{4,7},{5,6},{6,5},{7,4},{8,11},{9,10},{10,... | collective-permute-start | bytes 393224 | tf_op jit(solution)/shard_map/ppermute | solution.py:312
  12.1 0.1 multiply_cosine_fusion
  12.2 0.1 pad_add_fusion.info_ref
  12.3 13.3 %prep.1 = (f32[512,512]{1,0:T(8,128)S(1)}, f32[64,256]{1,0:T(8,128)S(1)}, f32[64,256]{1,0:T(8,128)S(1)}, f32[8,256]{1,0:T(8,128)S(1)}, f32[64,128]{1,0:T(8,128)S...) custom-call(s32[16]{0:T(128)S(1)} %pad_add_fusion.info_ref, ...), custom_call_target="tpu_custom_call" | custom-call | tf_op jit(solution)/shard_map/prep/pallas_call | solution.py:270
  25.6 2.1 %collective-permute-start.1 = (bf16[1,128,512]{2,1,0:T(8,128)(2,1)S(1)}, bf16[1,128,512]{2,1,0:T(8,128)(2,1)S(1)}, u32[]{:S(2)}, u32[]{:S(2)}) collective-permute-start(bf16[1,128,512]{2,1,0:T(8,128)(2,1)S(1)} %get-tuple-element.38), channel_id=1, source_target_pairs={{0,2},{1,3},{2,0},{3,1},{4,6},{5,7},{6,4},{7,5},{8,10},{9,11},{10,... | collective-permute-start | bytes 393224 | tf_op jit(solution)/shard_map/ppermute | solution.py:312
  27.7 0.0 collective-permute-done.4.refs_3_
  27.7 0.9 %collective-permute-start.2 = (bf16[1,128,512]{2,1,0:T(8,128)(2,1)S(1)}, bf16[1,128,512]{2,1,0:T(8,128)(2,1)S(1)}, u32[]{:S(2)}, u32[]{:S(2)}) collective-permute-start(bf16[1,128,512]{2,1,0:T(8,128)(2,1)S(1)} %get-tuple-element.39), channel_id=1, source_target_pairs={{0,3},{1,2},{2,1},{3,0},{4,7},{5,6},{6,5},{7,4},{8,11},{9,10},{10,... | collective-permute-start | bytes 393224 | tf_op jit(solution)/shard_map/ppermute | solution.py:312
  28.6 0.6 collective-permute-start.7
  29.2 4.6 %text.1 = (f32[656,512]{1,0:T(8,128)S(1)}, f32[4,656,128]{2,1,0:T(8,128)S(1)}) custom-call(s32[16]{0:T(128)S(1)} %pad_add_fusion.info_ref, bf16[3,128,512]{2,1,0:T(8,128)(2,1)S(1)} %get-tuple-element.33.refs_0_, bf16[3,128,512]{2,1,0:T(8,128)(2,1)S(1)} %collective-permute-done.refs_1_, bf16[1,128,512]{2,1,0:T(8,128)(2,1)S(1)} %collective-permute-done.3.refs_2_, ...), custom_call_target="tpu_custom_call" | custom-call | tf_op jit(solution)/shard_map/text/pallas_call | solution.py:270
  33.9 0.0 collective-permute-done.7.refs_8_
  33.9 0.0 collective-permute-done.5.refs_4_
  33.9 2.3 %weigh.1 = (bf16[4,512,384]{2,1,0:T(8,128)(2,1)S(1)}, f32[512,512]{1,0:T(8,128)S(1)}) custom-call(s32[16]{0:T(128)S(1)} %pad_add_fusion.info_ref, bf16[3,128,512]{2,1,0:T(8,128)(2,1)S(1)} %get-tuple-element.33.refs_0_, bf16[3,128,512]{2,1,0:T(8,128)(2,1)S(1)} %collective-permute-done.refs_1_, bf16[1,128,512]{2,1,0:T(8,128)(2,1)S(1)} %collective-permute-done.3.refs_2_, ...), custom_call_target="tpu_custom_call" | custom-call | tf_op jit(solution)/shard_map/weigh/pallas_call | solution.py:270
  36.2 1.1 %collective-permute-done.1.refs_2_ = bf16[1,128,512]{2,1,0:T(8,128)(2,1)S(1)} collective-permute-done((bf16[1,128,512]{2,1,0:T(8,128)(2,1)S(1)}, bf16[1,128,512]{2,1,0:T(8,128)(2,1)S(1)}, u32[]{:S(2)}, u32[]{:S(2)}) %collective-permute-start.1) | collective-permute-done | bytes 131104 | tf_op jit(solution)/shard_map/ppermute | solution.py:312
  37.3 0.0 collective-permute-done.2.refs_3_
  37.3 0.9 %mix.3 = f32[72,256]{1,0:T(8,128)S(1)} custom-call(bf16[3,128,512]{2,1,0:T(8,128)(2,1)S(1)} %get-tuple-element.33.refs_0_, bf16[3,128,512]{2,1,0:T(8,128)(2,1)S(1)} %collective-permute-done.refs_1_, bf16[1,128,512]{2,1,0:T(8,128)(2,1)S(1)} %collective-permute-done.1.refs_2_, bf16[1,128,512]{2,1,0:T(8,128)(2,1)S(1)} %collective-permute-done.2.refs_3_, ...), custom_call_target="tpu_custom_call" | custom-call | flops 201326592 | bytes 1048576 | tf_op jit(solution)/shard_map/mix/pallas_call | solution.py:270
  38.2 5.0 %collective-permute-start.10 = (f32[72,256]{1,0:T(8,128)S(1)}, f32[72,256]{1,0:T(8,128)S(1)}, u32[]{:S(2)}, u32[]{:S(2)}) collective-permute-start(f32[72,256]{1,0:T(8,128)S(1)} %mix.3), channel_id=1, source_target_pairs={{0,2},{2,3},{3,1},{1,0},{4,6},{6,7},{7,5},{5,4},{8,10},{10,11},{11... | collective-permute-start | bytes 221192 | tf_op jit(solution)/shard_map/ppermute | solution.py:381
  43.2 0.7 %collective-permute-start.9 = (f32[72,256]{1,0:T(8,128)S(1)}, f32[72,256]{1,0:T(8,128)S(1)}, u32[]{:S(2)}, u32[]{:S(2)}) collective-permute-start(f32[72,256]{1,0:T(8,128)S(1)} %mix.3), channel_id=1, source_target_pairs={{1,2},{2,1},{0,0},{3,3},{5,6},{6,5},{4,4},{7,7},{9,10},{10,9},{8,8... | collective-permute-start | bytes 221192 | tf_op jit(solution)/shard_map/ppermute | solution.py:381
  43.8 0.9 %mix.2.refs_0_ = f32[72,256]{1,0:T(8,128)S(1)} custom-call(bf16[3,128,512]{2,1,0:T(8,128)(2,1)S(1)} %get-tuple-element.33.refs_0_, bf16[3,128,512]{2,1,0:T(8,128)(2,1)S(1)} %collective-permute-done.refs_1_, bf16[1,128,512]{2,1,0:T(8,128)(2,1)S(1)} %collective-permute-done.1.refs_2_, bf16[1,128,512]{2,1,0:T(8,128)(2,1)S(1)} %collective-permute-done.2.refs_3_, ...), custom_call_target="tpu_custom_call" | custom-call | flops 201326592 | bytes 1048576 | tf_op jit(solution)/shard_map/mix/pallas_call | solution.py:270
  44.8 2.0 %collective-permute-start.8 = (f32[72,256]{1,0:T(8,128)S(1)}, f32[72,256]{1,0:T(8,128)S(1)}, u32[]{:S(2)}, u32[]{:S(2)}) collective-permute-start(f32[72,256]{1,0:T(8,128)S(1)} %mix.2.refs_0_), channel_id=1, source_target_pairs={{0,1},{1,0},{2,3},{3,2},{4,5},{5,4},{6,7},{7,6},{8,9},{9,8},{10,11... | collective-permute-start | bytes 221192 | tf_op jit(solution)/shard_map/ppermute | solution.py:378
  46.7 0.0 collective-permute-done.10.refs_3_
  46.7 0.0 collective-permute-done.9.refs_2_
  46.7 2.4 %collective-permute-done.8.refs_1_ = f32[72,256]{1,0:T(8,128)S(1)} collective-permute-done((f32[72,256]{1,0:T(8,128)S(1)}, f32[72,256]{1,0:T(8,128)S(1)}, u32[]{:S(2)}, u32[]{:S(2)}) %collective-permute-start.8) | collective-permute-done | bytes 73760 | tf_op jit(solution)/shard_map/ppermute | solution.py:378
  49.1 0.1 loss.1
  49.3 11.2 %all_to_all.5 = f32[32,1,128]{2,1,0:T(1,128)S(1)} all-to-all(f32[32,1,128]{2,1,0:T(1,128)S(1)} %loss.1), channel_id=1, replica_groups=mesh['dp'=8,'seq'=4] {'dp','seq'}, dimensions={0} | all-to-all | bytes 32768 | tf_op jit(solution)/shard_map/all_to_all | solution.py:389
  60.5 0.1 broadcast_in_dim.18
  60.5 0.7 %select_reduce_fusion = f32[8]{0:T(128)} fusion(f32[64]{0:T(128)S(1)} %broadcast_in_dim.18, s32[8]{0:T(128)S(1)} %copy-done.3), kind=kLoop, calls=%fused_computation.4 | loop fusion | flops 1528 | bytes 320 | tf_op jit(solution)/shard_map/reduce_sum | solution.py:392
  (15 shorter events, 0.1 us)
Async XLA Ops:
  0.0 12.1 %copy-start = (s32[8]{0:T(128)S(1)}, s32[8]{0:T(128)}, u32[]{:S(2)}) copy-start(s32[8]{0:T(128)} %param.18) | copy-start | bytes 100
  0.0 12.2 %copy-start.2 = (s32[1,8]{1,0:T(1,128)S(1)}, s32[1,8]{1,0:T(1,128)}, u32[]{:S(2)}) copy-start(s32[1,8]{1,0:T(1,128)} %param.17) | copy-start | bytes 100
  0.0 12.2 %copy-start.1 = (s32[8]{0:T(128)S(1)}, s32[8]{0:T(128)}, u32[]{:S(2)}) copy-start(s32[8]{0:T(128)} %param.16) | copy-start | bytes 100
  1.0 24.6 %collective-permute-start.3 = (bf16[1,128,512]{2,1,0:T(8,128)(2,1)S(1)}, bf16[1,128,512]{2,1,0:T(8,128)(2,1)S(1)}, u32[]{:S(2)}, u32[]{:S(2)}) collective-permute-start(bf16[1,128,512]{2,1,0:T(8,128)(2,1)S(1)} %get-tuple-element.31), channel_id=1, source_target_pairs={{0,2},{1,3},{2,0},{3,1},{4,6},{5,7},{6,4},{7,5},{8,10},{9,11},{10,... | collective-permute-start | bytes 393224 | tf_op jit(solution)/shard_map/ppermute | solution.py:312
  6.6 22.0 %collective-permute-start = (bf16[3,128,512]{2,1,0:T(8,128)(2,1)S(1)}, bf16[3,128,512]{2,1,0:T(8,128)(2,1)S(1)}, u32[]{:S(2)}, u32[]{:S(2)}) collective-permute-start(bf16[3,128,512]{2,1,0:T(8,128)(2,1)S(1)} %get-tuple-element.34), channel_id=1, source_target_pairs={{0,1},{1,0},{2,3},{3,2},{4,5},{5,4},{6,7},{7,6},{8,9},{9,8},{10,11... | collective-permute-start | bytes 1179656 | tf_op jit(solution)/shard_map/ppermute | solution.py:312
  8.2 19.5 %collective-permute-start.4 = (bf16[1,128,512]{2,1,0:T(8,128)(2,1)S(1)}, bf16[1,128,512]{2,1,0:T(8,128)(2,1)S(1)}, u32[]{:S(2)}, u32[]{:S(2)}) collective-permute-start(bf16[1,128,512]{2,1,0:T(8,128)(2,1)S(1)} %get-tuple-element.40), channel_id=1, source_target_pairs={{0,3},{1,2},{2,1},{3,0},{4,7},{5,6},{6,5},{7,4},{8,11},{9,10},{10,... | collective-permute-start | bytes 393224 | tf_op jit(solution)/shard_map/ppermute | solution.py:312
  8.2 25.6 %collective-permute-start.5 = (bf16[1,128,512]{2,1,0:T(8,128)(2,1)S(1)}, bf16[1,128,512]{2,1,0:T(8,128)(2,1)S(1)}, u32[]{:S(2)}, u32[]{:S(2)}) collective-permute-start(bf16[1,128,512]{2,1,0:T(8,128)(2,1)S(1)} %get-tuple-element.41), channel_id=1, source_target_pairs={{0,2},{1,3},{2,0},{3,1},{4,6},{5,7},{6,4},{7,5},{8,10},{9,11},{10,... | collective-permute-start | bytes 393224 | tf_op jit(solution)/shard_map/ppermute | solution.py:312
  10.2 23.7 %collective-permute-start.6 = (bf16[1,128,512]{2,1,0:T(8,128)(2,1)S(1)}, bf16[1,128,512]{2,1,0:T(8,128)(2,1)S(1)}, u32[]{:S(2)}, u32[]{:S(2)}) collective-permute-start(bf16[1,128,512]{2,1,0:T(8,128)(2,1)S(1)} %get-tuple-element.42), channel_id=1, source_target_pairs={{0,3},{1,2},{2,1},{3,0},{4,7},{5,6},{6,5},{7,4},{8,11},{9,10},{10,... | collective-permute-start | bytes 393224 | tf_op jit(solution)/shard_map/ppermute | solution.py:312
  25.6 11.6 %collective-permute-start.1 = (bf16[1,128,512]{2,1,0:T(8,128)(2,1)S(1)}, bf16[1,128,512]{2,1,0:T(8,128)(2,1)S(1)}, u32[]{:S(2)}, u32[]{:S(2)}) collective-permute-start(bf16[1,128,512]{2,1,0:T(8,128)(2,1)S(1)} %get-tuple-element.38), channel_id=1, source_target_pairs={{0,2},{1,3},{2,0},{3,1},{4,6},{5,7},{6,4},{7,5},{8,10},{9,11},{10,... | collective-permute-start | bytes 393224 | tf_op jit(solution)/shard_map/ppermute | solution.py:312
  27.7 9.5 %collective-permute-start.2 = (bf16[1,128,512]{2,1,0:T(8,128)(2,1)S(1)}, bf16[1,128,512]{2,1,0:T(8,128)(2,1)S(1)}, u32[]{:S(2)}, u32[]{:S(2)}) collective-permute-start(bf16[1,128,512]{2,1,0:T(8,128)(2,1)S(1)} %get-tuple-element.39), channel_id=1, source_target_pairs={{0,3},{1,2},{2,1},{3,0},{4,7},{5,6},{6,5},{7,4},{8,11},{9,10},{10,... | collective-permute-start | bytes 393224 | tf_op jit(solution)/shard_map/ppermute | solution.py:312
  28.6 5.2 %collective-permute-start.7 = (f32[64,128]{1,0:T(8,128)S(1)}, f32[64,128]{1,0:T(8,128)S(1)}, u32[]{:S(2)}, u32[]{:S(2)}) collective-permute-start(f32[64,128]{1,0:T(8,128)S(1)} %get-tuple-element.46.refs_7_), channel_id=1, source_target_pairs={{0,1},{1,0},{2,3},{3,2},{4,5},{5,4},{6,7},{7,6},{8,9},{9,8},{10,11... | collective-permute-start | bytes 98312 | tf_op jit(solution)/shard_map/ppermute | solution.py:359
  38.2 22.4 %copy-start.3 = (s32[8]{0:T(128)S(1)}, s32[8]{0:T(128)}, u32[]{:S(2)}) copy-start(s32[8]{0:T(128)} %param.23) | copy-start | bytes 100
  38.2 8.5 %collective-permute-start.10 = (f32[72,256]{1,0:T(8,128)S(1)}, f32[72,256]{1,0:T(8,128)S(1)}, u32[]{:S(2)}, u32[]{:S(2)}) collective-permute-start(f32[72,256]{1,0:T(8,128)S(1)} %mix.3), channel_id=1, source_target_pairs={{0,2},{2,3},{3,1},{1,0},{4,6},{6,7},{7,5},{5,4},{8,10},{10,11},{11... | collective-permute-start | bytes 221192 | tf_op jit(solution)/shard_map/ppermute | solution.py:381
  43.2 3.5 %collective-permute-start.9 = (f32[72,256]{1,0:T(8,128)S(1)}, f32[72,256]{1,0:T(8,128)S(1)}, u32[]{:S(2)}, u32[]{:S(2)}) collective-permute-start(f32[72,256]{1,0:T(8,128)S(1)} %mix.3), channel_id=1, source_target_pairs={{1,2},{2,1},{0,0},{3,3},{5,6},{6,5},{4,4},{7,7},{9,10},{10,9},{8,8... | collective-permute-start | bytes 221192 | tf_op jit(solution)/shard_map/ppermute | solution.py:381
  44.8 4.4 %collective-permute-start.8 = (f32[72,256]{1,0:T(8,128)S(1)}, f32[72,256]{1,0:T(8,128)S(1)}, u32[]{:S(2)}, u32[]{:S(2)}) collective-permute-start(f32[72,256]{1,0:T(8,128)S(1)} %mix.2.refs_0_), channel_id=1, source_target_pairs={{0,1},{1,0},{2,3},{3,2},{4,5},{5,4},{6,7},{7,6},{8,9},{9,8},{10,11... | collective-permute-start | bytes 221192 | tf_op jit(solution)/shard_map/ppermute | solution.py:378

commit v4 on v3

--- a/solution.py
+++ b/solution.py
@@ -12,7 +12,7 @@
 FREQ = 256
 EPS = 1e-06
 NEG = -1e30
-STAT_ROWS = 8
+STAT_ROWS = 16
 ALIGN = 16
 NEAR = 2
 F32 = jnp.float32
@@ -66,6 +66,13 @@
     if sources != 4:
         return rank * tok_dev, tok_dev, True
     return rank // 2 * 2 * tok_dev, 2 * tok_dev, (rank == 1) | (rank == 2)
+
+
+def origins(rank, sources):
+    if sources == 4:
+        return [rank, rank ^ 1, 3 - rank, (3 - rank) ^ 1]
+    ahead = reversed(range(sources))
+    return [partner(rank, k if sources & (sources - 1) == 0 else sources - k, sources) for k in ahead]
 
 
 def cut_kernel(sources, plan, *refs):
@@ -100,9 +107,7 @@
     for copy in copies[:4]:
         copy.wait()
     mods[...] = jnp.dot(act_ref[...], mod_buf[...], preferred_element_type=F32)
-    scales = 1.0 + mods[:, width:]
     weight = wt_buf[...].astype(F32)
-    slopes = nt_dot(weight, scales, EXACT)
     shifts = nt_dot(weight, mods[:, :width], EXACT)
     first, count, active = summed_here(rank, sources, tok_dev)
     tok_clip = clip_index(info_ref, clips, (clips, count), 1, first)
@@ -112,7 +117,11 @@
     for c in range(clips):
         sizes = jnp.where(slot == c, info_ref[c].astype(F32), sizes)
     share_ref[...] = jnp.where(active, picks / sizes, 0.0)
-    slope_ref[...] = jnp.dot(slopes, picks, precision=EXACT, preferred_element_type=F32)
+    for place, source in enumerate(origins(rank, sources)):
+        low = pl.multiple_of(source * local, HEAD_DIM)
+        scales = 1.0 + mods[:, pl.ds(pl.multiple_of(width + low, HEAD_DIM), local)]
+        slopes = nt_dot(wt_buf[:, pl.ds(low, local)].astype(F32), scales, EXACT)
+        slope_ref[place] = jnp.dot(slopes, picks, precision=EXACT, preferred_element_type=F32)
     shift_ref[...] = jnp.dot(shifts, picks, precision=EXACT, preferred_element_type=F32)
     target_ref[...] = noise_buf[...] - clean_buf[...]
     row_clip = clip_index(info_ref, clips, (group_rows, clips), 0, 0)
@@ -219,32 +228,42 @@
     ]
     attended = jnp.concatenate([(mixed[h] + base_ref[rows, head_cols(h)]).astype(BF16) for h in range(heads)], axis=1)
     attended_full = attended.astype(F32)
-    y_high, y_low = two_parts(attended_full * scale_ref[rows, :])
+    local_mean = jnp.sum(attended_full, axis=1, keepdims=True) * (1.0 / local)
+    y_high, y_low = two_parts((attended_full - local_mean) * scale_ref[rows, :])
     s_high, s_low = two_parts(attended_full * attended_full)
     weight = wt_ref[...]
     every = jnp.ones((STAT_ROWS, local), BF16)
-    out_ref[:channels, :] = nt_dot(weight, y_high) + nt_dot(weight, y_low)
-    is_sum = lax.broadcasted_iota(jnp.int32, (STAT_ROWS, count), 0) == 0
-    squares = nt_dot(every, s_high) + nt_dot(every, s_low)
-    out_ref[channels:, :] = jnp.where(is_sum, nt_dot(every, attended), squares)
+    out_ref[:channels, :] = (nt_dot(weight, y_high) + nt_dot(weight, y_low)).astype(BF16)
+    row = lax.broadcasted_iota(jnp.int32, (STAT_ROWS, count), 0)
+    rest = jnp.where(row < 3, nt_dot(every, attended), nt_dot(every, s_high) + nt_dot(every, s_low))
+    terms = jnp.zeros((STAT_ROWS, count), F32)
+    for place in range(3):
+        term = rest.astype(BF16).astype(F32)
+        terms = jnp.where((row == place) | (row == place + 3), term, terms)
+        rest = rest - term
+    out_ref[channels:, :] = terms.astype(BF16)
 
 
 def loss_kernel(count, width, *refs):
     part_refs = refs[:count]
     slope_ref, shift_ref, share_ref, *target_refs, out_ref = refs[count:]
-    channels = slope_ref.shape[0]
+    channels = slope_ref.shape[1]
     clips = share_ref.shape[0]
-    total = part_refs[0][...]
-    for part in part_refs[1:]:
-        total = total + part[...]
+    parts = [part[...].astype(F32) for part in part_refs]
+    stats = [part[channels:] for part in parts]
+    sums = [stat[0:1] + stat[1:2] + stat[2:3] for stat in stats]
+    squares = [stat[3:4] + stat[4:5] + stat[5:6] for stat in stats]
+    center = sum(sums[1:], sums[0]) * (1.0 / width)
+    spread = sum(squares[1:], squares[0]) * (1.0 / width) - center * center
+    total = jnp.zeros(slope_ref.shape[1:], F32)
+    for place, part in enumerate(parts):
+        total = total + part[:channels] + (sums[place] * (count / width) - center) * slope_ref[place]
     targets = [target[...] for target in target_refs]
     if len(targets) == 2:
         swap = lax.axis_index("seq") == 1
         targets = [jnp.where(swap, *targets[::-1]), jnp.where(swap, *targets)]
     offset = shift_ref[...] - jnp.concatenate(targets, axis=1)
-    center = total[channels : channels + 1, :] * (1.0 / width)
-    spread = total[channels + 1 : channels + 2, :] * (1.0 / width) - center * center
-    diff = (total[:channels, :] - center * slope_ref[...]) * lax.rsqrt(spread + EPS) + offset
+    diff = total * lax.rsqrt(spread + EPS) + offset
     error = jnp.sum(diff * diff, axis=0, keepdims=True) * (1.0 / channels)
     share = share_ref[...]
     sums = jnp.sum(jnp.where(share > 0.0, share * error, 0.0), axis=1, keepdims=True)
@@ -331,8 +350,8 @@
         functools.partial(prep_kernel, sources, clips), "prep",
         [activated, mod_weight, weight_t, noise.T, clean.T, text_kv],
         [
-            ((group_rows, local), F32), ((channels, summed), F32), ((channels, summed), F32), ((clips, summed), F32),
-            ((channels, tok_dev), F32),
+            ((group_rows, local), F32), ((sources, channels, summed), F32), ((channels, summed), F32),
+            ((clips, summed), F32), ((channels, tok_dev), F32),
             ((channels, local), BF16), ((clips, text_len, local), BF16), ((clips, text_len, local), BF16),
         ],
         [
@@ -369,7 +388,7 @@
         return call(
             functools.partial(mix_kernel, sources, reach, place), "mix",
             [*near_blocks, *v_blocks, weights, base, scale_tok, weight_local],
-            [((channels + STAT_ROWS, summed), F32)],
+            [((channels + STAT_ROWS, summed), BF16)],
             [pltpu.VMEM((group_rows, local), BF16)], flops=4 * summed * reach[1] * local, traffic=2**20,
         )[0]
 

time: 61.4 us -> 62.1 us (1.011)
    ppermute x1, starting transfers between devices: 1.96 us -> 2.86 us  [per_device(): parts = [here, lax.ppermute(here, 'seq', swap)]]
    ppermute x2, starting transfers between devices: 5.67 us -> 4.99 us  [per_device(): parts.append(lax.ppermute(there, 'seq', pairs))]
    pallas_call x8, Pallas kernels: 24.7 us -> 25.3 us  [call(): pl.pallas_call(kernel, in_specs=[smem()] * len(scalars) + [hbm() if i in...]
where the time goes in v4:
time: 62.1 us; the launch traced here: 61.9 us
  Pallas kernels  25.3 us (41%)
  starting transfers between devices  21 us (34%)
  blocking collectives  11.2 us (18%)
  waiting for transfers between devices  3.23 us (5%)
  other arithmetic  0.92 us (1%)
    pallas_call x8, Pallas kernels, call(): pl.pallas_call(kernel, in_specs=[smem()] * len(scalars) + [hbm() if i in...  25.3 us
    ppermute x7, starting transfers between devices, onward(): lax.ppermute(x, 'seq', [(i, partner(i, k, sources)) for i in range(source...  12.6 us
    all_to_all x1, blocking collectives, per_device(): lax.all_to_all(shares, ('dp', 'seq'), split_axis=0, concat_axis=0, tiled=...  11.2 us
    ppermute x2, starting transfers between devices, per_device(): parts.append(lax.ppermute(there, 'seq', pairs))  4.99 us
    ppermute x1, starting transfers between devices, per_device(): parts = [here, lax.ppermute(here, 'seq', swap)]  2.86 us
    ppermute x1, waiting for transfers between devices, per_device(): parts = [here, lax.ppermute(here, 'seq', swap)]  1.98 us
    ppermute x7, waiting for transfers between devices, onward(): lax.ppermute(x, 'seq', [(i, partner(i, k, sources)) for i in range(source...  1.25 us
  transfers between devices with their start and end apart: 11, of which 2 were waited for; matrix products, arithmetic and copies ran while one was open for 0% of the time, Pallas kernels for 37%

profile of v4, /device:TPU:0, one launch (start us, length us, event | category | flops | bytes accessed | tf_op | source)
XLA Modules:
  0.0 61.9 jit_solution(13495280273707315093)
XLA Ops:
  0.0 1.0 %cut_first.1 = (bf16[1,128,512]{2,1,0:T(8,128)(2,1)S(1)}, bf16[1,128,512]{2,1,0:T(8,128)(2,1)S(1)}) custom-call(bf16[128,2048]{1,0:T(8,128)(2,1)} %refs_0_.3), custom_call_target="tpu_custom_call" | custom-call | bytes 524288 | tf_op jit(solution)/shard_map/cut_first/pallas_call | solution.py:289
  1.0 4.1 %collective-permute-start.3 = (bf16[1,128,512]{2,1,0:T(8,128)(2,1)S(1)}, bf16[1,128,512]{2,1,0:T(8,128)(2,1)S(1)}, u32[]{:S(2)}, u32[]{:S(2)}) collective-permute-start(bf16[1,128,512]{2,1,0:T(8,128)(2,1)S(1)} %get-tuple-element.31), channel_id=1, source_target_pairs={{0,2},{1,3},{2,0},{3,1},{4,6},{5,7},{6,4},{7,5},{8,10},{9,11},{10,... | collective-permute-start | bytes 393224 | tf_op jit(solution)/shard_map/ppermute | solution.py:331
  5.1 1.5 %cut_rest.1 = (bf16[3,128,512]{2,1,0:T(8,128)(2,1)S(1)}, bf16[3,128,512]{2,1,0:T(8,128)(2,1)S(1)}, bf16[1,128,512]{2,1,0:T(8,128)(2,1)S(1)}, bf16[1,128,512]{2,1...) custom-call(bf16[128,2048]{1,0:T(8,128)(2,1)} %refs_0_.3, ...), custom_call_target="tpu_custom_call" | custom-call | bytes 2621440 | tf_op jit(solution)/shard_map/cut_rest/pallas_call | solution.py:289
  6.6 1.6 %collective-permute-start = (bf16[3,128,512]{2,1,0:T(8,128)(2,1)S(1)}, bf16[3,128,512]{2,1,0:T(8,128)(2,1)S(1)}, u32[]{:S(2)}, u32[]{:S(2)}) collective-permute-start(bf16[3,128,512]{2,1,0:T(8,128)(2,1)S(1)} %get-tuple-element.34), channel_id=1, source_target_pairs={{0,1},{1,0},{2,3},{3,2},{4,5},{5,4},{6,7},{7,6},{8,9},{9,8},{10,11... | collective-permute-start | bytes 1179656 | tf_op jit(solution)/shard_map/ppermute | solution.py:331
  8.2 1.9 %collective-permute-start.5 = (bf16[1,128,512]{2,1,0:T(8,128)(2,1)S(1)}, bf16[1,128,512]{2,1,0:T(8,128)(2,1)S(1)}, u32[]{:S(2)}, u32[]{:S(2)}) collective-permute-start(bf16[1,128,512]{2,1,0:T(8,128)(2,1)S(1)} %get-tuple-element.41), channel_id=1, source_target_pairs={{0,2},{1,3},{2,0},{3,1},{4,6},{5,7},{6,4},{7,5},{8,10},{9,11},{10,... | collective-permute-start | bytes 393224 | tf_op jit(solution)/shard_map/ppermute | solution.py:331
  10.2 1.9 %collective-permute-start.6 = (bf16[1,128,512]{2,1,0:T(8,128)(2,1)S(1)}, bf16[1,128,512]{2,1,0:T(8,128)(2,1)S(1)}, u32[]{:S(2)}, u32[]{:S(2)}) collective-permute-start(bf16[1,128,512]{2,1,0:T(8,128)(2,1)S(1)} %get-tuple-element.42), channel_id=1, source_target_pairs={{0,3},{1,2},{2,1},{3,0},{4,7},{5,6},{6,5},{7,4},{8,11},{9,10},{10,... | collective-permute-start | bytes 393224 | tf_op jit(solution)/shard_map/ppermute | solution.py:331
  12.1 0.1 multiply_cosine_fusion
  12.2 0.1 pad_add_fusion.info_ref
  12.3 14.0 %prep.1 = (f32[512,512]{1,0:T(8,128)S(1)}, f32[4,64,256]{2,1,0:T(8,128)S(1)}, f32[64,256]{1,0:T(8,128)S(1)}, f32[8,256]{1,0:T(8,128)S(1)}, f32[64,128]{1,0:T(8,1...) custom-call(s32[16]{0:T(128)S(1)} %pad_add_fusion.info_ref, ...), custom_call_target="tpu_custom_call" | custom-call | tf_op jit(solution)/shard_map/prep/pallas_call | solution.py:289
  26.4 0.0 collective-permute-done.3.refs_2_
  26.4 2.1 %collective-permute-start.1 = (bf16[1,128,512]{2,1,0:T(8,128)(2,1)S(1)}, bf16[1,128,512]{2,1,0:T(8,128)(2,1)S(1)}, u32[]{:S(2)}, u32[]{:S(2)}) collective-permute-start(bf16[1,128,512]{2,1,0:T(8,128)(2,1)S(1)} %get-tuple-element.38), channel_id=1, source_target_pairs={{0,2},{1,3},{2,0},{3,1},{4,6},{5,7},{6,4},{7,5},{8,10},{9,11},{10,... | collective-permute-start | bytes 393224 | tf_op jit(solution)/shard_map/ppermute | solution.py:331
  28.5 0.0 collective-permute-done.4.refs_3_
  28.5 0.9 %collective-permute-start.2 = (bf16[1,128,512]{2,1,0:T(8,128)(2,1)S(1)}, bf16[1,128,512]{2,1,0:T(8,128)(2,1)S(1)}, u32[]{:S(2)}, u32[]{:S(2)}) collective-permute-start(bf16[1,128,512]{2,1,0:T(8,128)(2,1)S(1)} %get-tuple-element.39), channel_id=1, source_target_pairs={{0,3},{1,2},{2,1},{3,0},{4,7},{5,6},{6,5},{7,4},{8,11},{9,10},{10,... | collective-permute-start | bytes 393224 | tf_op jit(solution)/shard_map/ppermute | solution.py:331
  29.4 0.0 collective-permute-done.refs_1_
  29.4 0.6 collective-permute-start.7
  29.9 4.5 %text.1 = (f32[656,512]{1,0:T(8,128)S(1)}, f32[4,656,128]{2,1,0:T(8,128)S(1)}) custom-call(s32[16]{0:T(128)S(1)} %pad_add_fusion.info_ref, bf16[3,128,512]{2,1,0:T(8,128)(2,1)S(1)} %get-tuple-element.33.refs_0_, bf16[3,128,512]{2,1,0:T(8,128)(2,1)S(1)} %collective-permute-done.refs_1_, bf16[1,128,512]{2,1,0:T(8,128)(2,1)S(1)} %collective-permute-done.3.refs_2_, ...), custom_call_target="tpu_custom_call" | custom-call | tf_op jit(solution)/shard_map/text/pallas_call | solution.py:289
  34.4 0.0 collective-permute-done.7.refs_8_
  34.4 0.0 collective-permute-done.5.refs_4_
  34.5 2.3 %weigh.1 = (bf16[4,512,384]{2,1,0:T(8,128)(2,1)S(1)}, f32[512,512]{1,0:T(8,128)S(1)}) custom-call(s32[16]{0:T(128)S(1)} %pad_add_fusion.info_ref, bf16[3,128,512]{2,1,0:T(8,128)(2,1)S(1)} %get-tuple-element.33.refs_0_, bf16[3,128,512]{2,1,0:T(8,128)(2,1)S(1)} %collective-permute-done.refs_1_, bf16[1,128,512]{2,1,0:T(8,128)(2,1)S(1)} %collective-permute-done.3.refs_2_, ...), custom_call_target="tpu_custom_call" | custom-call | tf_op jit(solution)/shard_map/weigh/pallas_call | solution.py:289
  36.7 1.2 %collective-permute-done.1.refs_2_ = bf16[1,128,512]{2,1,0:T(8,128)(2,1)S(1)} collective-permute-done((bf16[1,128,512]{2,1,0:T(8,128)(2,1)S(1)}, bf16[1,128,512]{2,1,0:T(8,128)(2,1)S(1)}, u32[]{:S(2)}, u32[]{:S(2)}) %collective-permute-start.1) | collective-permute-done | bytes 131104 | tf_op jit(solution)/shard_map/ppermute | solution.py:331
  38.0 0.9 %mix.3 = bf16[80,256]{1,0:T(8,128)(2,1)S(1)} custom-call(bf16[3,128,512]{2,1,0:T(8,128)(2,1)S(1)} %get-tuple-element.33.refs_0_, bf16[3,128,512]{2,1,0:T(8,128)(2,1)S(1)} %collective-permute-done.refs_1_, bf16[1,128,512]{2,1,0:T(8,128)(2,1)S(1)} %collective-permute-done.1.refs_2_, bf16[1,128,512]{2,1,0:T(8,128)(2,1)S(1)} %collective-permute-done.2.refs_3_, ...), custom_call_target="tpu_custom_call" | custom-call | flops 201326592 | bytes 1048576 | tf_op jit(solution)/shard_map/mix/pallas_call | solution.py:289
  38.9 0.0 copy-start.3
  38.9 4.3 %collective-permute-start.10 = (bf16[80,256]{1,0:T(8,128)(2,1)S(1)}, bf16[80,256]{1,0:T(8,128)(2,1)S(1)}, u32[]{:S(2)}, u32[]{:S(2)}) collective-permute-start(bf16[80,256]{1,0:T(8,128)(2,1)S(1)} %mix.3), channel_id=1, source_target_pairs={{0,2},{2,3},{3,1},{1,0},{4,6},{6,7},{7,5},{5,4},{8,10},{10,11},{11... | collective-permute-start | bytes 122888 | tf_op jit(solution)/shard_map/ppermute | solution.py:400
  43.3 0.7 %collective-permute-start.9 = (bf16[80,256]{1,0:T(8,128)(2,1)S(1)}, bf16[80,256]{1,0:T(8,128)(2,1)S(1)}, u32[]{:S(2)}, u32[]{:S(2)}) collective-permute-start(bf16[80,256]{1,0:T(8,128)(2,1)S(1)} %mix.3), channel_id=1, source_target_pairs={{1,2},{2,1},{0,0},{3,3},{5,6},{6,5},{4,4},{7,7},{9,10},{10,9},{8,8... | collective-permute-start | bytes 122888 | tf_op jit(solution)/shard_map/ppermute | solution.py:400
  43.9 0.9 %mix.2.refs_0_ = bf16[80,256]{1,0:T(8,128)(2,1)S(1)} custom-call(bf16[3,128,512]{2,1,0:T(8,128)(2,1)S(1)} %get-tuple-element.33.refs_0_, bf16[3,128,512]{2,1,0:T(8,128)(2,1)S(1)} %collective-permute-done.refs_1_, bf16[1,128,512]{2,1,0:T(8,128)(2,1)S(1)} %collective-permute-done.1.refs_2_, bf16[1,128,512]{2,1,0:T(8,128)(2,1)S(1)} %collective-permute-done.2.refs_3_, ...), custom_call_target="tpu_custom_call" | custom-call | flops 201326592 | bytes 1048576 | tf_op jit(solution)/shard_map/mix/pallas_call | solution.py:289
  44.9 2.9 %collective-permute-start.8 = (bf16[80,256]{1,0:T(8,128)(2,1)S(1)}, bf16[80,256]{1,0:T(8,128)(2,1)S(1)}, u32[]{:S(2)}, u32[]{:S(2)}) collective-permute-start(bf16[80,256]{1,0:T(8,128)(2,1)S(1)} %mix.2.refs_0_), channel_id=1, source_target_pairs={{0,1},{1,0},{2,3},{3,2},{4,5},{5,4},{6,7},{7,6},{8,9},{9,8},{10,11... | collective-permute-start | bytes 122888 | tf_op jit(solution)/shard_map/ppermute | solution.py:397
  47.7 0.0 collective-permute-done.9.refs_2_
  47.7 2.0 %collective-permute-done.8.refs_1_ = bf16[80,256]{1,0:T(8,128)(2,1)S(1)} collective-permute-done((bf16[80,256]{1,0:T(8,128)(2,1)S(1)}, bf16[80,256]{1,0:T(8,128)(2,1)S(1)}, u32[]{:S(2)}, u32[]{:S(2)}) %collective-permute-start.8) | collective-permute-done | bytes 40992 | tf_op jit(solution)/shard_map/ppermute | solution.py:397
  49.7 0.2 loss.1
  49.9 11.2 %all_to_all.5 = f32[32,1,128]{2,1,0:T(1,128)S(1)} all-to-all(f32[32,1,128]{2,1,0:T(1,128)S(1)} %loss.1), channel_id=1, replica_groups=mesh['dp'=8,'seq'=4] {'dp','seq'}, dimensions={0} | all-to-all | bytes 32768 | tf_op jit(solution)/shard_map/all_to_all | solution.py:408
  61.1 0.1 broadcast_in_dim.18
  61.2 0.7 %select_reduce_fusion = f32[8]{0:T(128)} fusion(f32[64]{0:T(128)S(1)} %broadcast_in_dim.18, s32[8]{0:T(128)S(1)} %copy-done.3), kind=kLoop, calls=%fused_computation.4 | loop fusion | flops 1528 | bytes 320 | tf_op jit(solution)/shard_map/reduce_sum | solution.py:411
  (15 shorter events, 0.1 us)
Async XLA Ops:
  0.0 12.1 %copy-start = (s32[8]{0:T(128)S(1)}, s32[8]{0:T(128)}, u32[]{:S(2)}) copy-start(s32[8]{0:T(128)} %param.18) | copy-start | bytes 100
  0.0 12.2 %copy-start.2 = (s32[1,8]{1,0:T(1,128)S(1)}, s32[1,8]{1,0:T(1,128)}, u32[]{:S(2)}) copy-start(s32[1,8]{1,0:T(1,128)} %param.17) | copy-start | bytes 100
  0.0 12.2 %copy-start.1 = (s32[8]{0:T(128)S(1)}, s32[8]{0:T(128)}, u32[]{:S(2)}) copy-start(s32[8]{0:T(128)} %param.16) | copy-start | bytes 100
  1.0 25.3 %collective-permute-start.3 = (bf16[1,128,512]{2,1,0:T(8,128)(2,1)S(1)}, bf16[1,128,512]{2,1,0:T(8,128)(2,1)S(1)}, u32[]{:S(2)}, u32[]{:S(2)}) collective-permute-start(bf16[1,128,512]{2,1,0:T(8,128)(2,1)S(1)} %get-tuple-element.31), channel_id=1, source_target_pairs={{0,2},{1,3},{2,0},{3,1},{4,6},{5,7},{6,4},{7,5},{8,10},{9,11},{10,... | collective-permute-start | bytes 393224 | tf_op jit(solution)/shard_map/ppermute | solution.py:331
  6.6 22.8 %collective-permute-start = (bf16[3,128,512]{2,1,0:T(8,128)(2,1)S(1)}, bf16[3,128,512]{2,1,0:T(8,128)(2,1)S(1)}, u32[]{:S(2)}, u32[]{:S(2)}) collective-permute-start(bf16[3,128,512]{2,1,0:T(8,128)(2,1)S(1)} %get-tuple-element.34), channel_id=1, source_target_pairs={{0,1},{1,0},{2,3},{3,2},{4,5},{5,4},{6,7},{7,6},{8,9},{9,8},{10,11... | collective-permute-start | bytes 1179656 | tf_op jit(solution)/shard_map/ppermute | solution.py:331
  8.2 20.2 %collective-permute-start.4 = (bf16[1,128,512]{2,1,0:T(8,128)(2,1)S(1)}, bf16[1,128,512]{2,1,0:T(8,128)(2,1)S(1)}, u32[]{:S(2)}, u32[]{:S(2)}) collective-permute-start(bf16[1,128,512]{2,1,0:T(8,128)(2,1)S(1)} %get-tuple-element.40), channel_id=1, source_target_pairs={{0,3},{1,2},{2,1},{3,0},{4,7},{5,6},{6,5},{7,4},{8,11},{9,10},{10,... | collective-permute-start | bytes 393224 | tf_op jit(solution)/shard_map/ppermute | solution.py:331
  8.2 26.2 %collective-permute-start.5 = (bf16[1,128,512]{2,1,0:T(8,128)(2,1)S(1)}, bf16[1,128,512]{2,1,0:T(8,128)(2,1)S(1)}, u32[]{:S(2)}, u32[]{:S(2)}) collective-permute-start(bf16[1,128,512]{2,1,0:T(8,128)(2,1)S(1)} %get-tuple-element.41), channel_id=1, source_target_pairs={{0,2},{1,3},{2,0},{3,1},{4,6},{5,7},{6,4},{7,5},{8,10},{9,11},{10,... | collective-permute-start | bytes 393224 | tf_op jit(solution)/shard_map/ppermute | solution.py:331
  10.2 24.3 %collective-permute-start.6 = (bf16[1,128,512]{2,1,0:T(8,128)(2,1)S(1)}, bf16[1,128,512]{2,1,0:T(8,128)(2,1)S(1)}, u32[]{:S(2)}, u32[]{:S(2)}) collective-permute-start(bf16[1,128,512]{2,1,0:T(8,128)(2,1)S(1)} %get-tuple-element.42), channel_id=1, source_target_pairs={{0,3},{1,2},{2,1},{3,0},{4,7},{5,6},{6,5},{7,4},{8,11},{9,10},{10,... | collective-permute-start | bytes 393224 | tf_op jit(solution)/shard_map/ppermute | solution.py:331
  26.4 11.6 %collective-permute-start.1 = (bf16[1,128,512]{2,1,0:T(8,128)(2,1)S(1)}, bf16[1,128,512]{2,1,0:T(8,128)(2,1)S(1)}, u32[]{:S(2)}, u32[]{:S(2)}) collective-permute-start(bf16[1,128,512]{2,1,0:T(8,128)(2,1)S(1)} %get-tuple-element.38), channel_id=1, source_target_pairs={{0,2},{1,3},{2,0},{3,1},{4,6},{5,7},{6,4},{7,5},{8,10},{9,11},{10,... | collective-permute-start | bytes 393224 | tf_op jit(solution)/shard_map/ppermute | solution.py:331
  28.5 9.5 %collective-permute-start.2 = (bf16[1,128,512]{2,1,0:T(8,128)(2,1)S(1)}, bf16[1,128,512]{2,1,0:T(8,128)(2,1)S(1)}, u32[]{:S(2)}, u32[]{:S(2)}) collective-permute-start(bf16[1,128,512]{2,1,0:T(8,128)(2,1)S(1)} %get-tuple-element.39), channel_id=1, source_target_pairs={{0,3},{1,2},{2,1},{3,0},{4,7},{5,6},{6,5},{7,4},{8,11},{9,10},{10,... | collective-permute-start | bytes 393224 | tf_op jit(solution)/shard_map/ppermute | solution.py:331
  29.4 5.1 %collective-permute-start.7 = (f32[64,128]{1,0:T(8,128)S(1)}, f32[64,128]{1,0:T(8,128)S(1)}, u32[]{:S(2)}, u32[]{:S(2)}) collective-permute-start(f32[64,128]{1,0:T(8,128)S(1)} %get-tuple-element.46.refs_7_), channel_id=1, source_target_pairs={{0,1},{1,0},{2,3},{3,2},{4,5},{5,4},{6,7},{7,6},{8,9},{9,8},{10,11... | collective-permute-start | bytes 98312 | tf_op jit(solution)/shard_map/ppermute | solution.py:378
  38.9 22.3 %copy-start.3 = (s32[8]{0:T(128)S(1)}, s32[8]{0:T(128)}, u32[]{:S(2)}) copy-start(s32[8]{0:T(128)} %param.23) | copy-start | bytes 100
  38.9 8.8 %collective-permute-start.10 = (bf16[80,256]{1,0:T(8,128)(2,1)S(1)}, bf16[80,256]{1,0:T(8,128)(2,1)S(1)}, u32[]{:S(2)}, u32[]{:S(2)}) collective-permute-start(bf16[80,256]{1,0:T(8,128)(2,1)S(1)} %mix.3), channel_id=1, source_target_pairs={{0,2},{2,3},{3,1},{1,0},{4,6},{6,7},{7,5},{5,4},{8,10},{10,11},{11... | collective-permute-start | bytes 122888 | tf_op jit(solution)/shard_map/ppermute | solution.py:400
  43.3 4.5 %collective-permute-start.9 = (bf16[80,256]{1,0:T(8,128)(2,1)S(1)}, bf16[80,256]{1,0:T(8,128)(2,1)S(1)}, u32[]{:S(2)}, u32[]{:S(2)}) collective-permute-start(bf16[80,256]{1,0:T(8,128)(2,1)S(1)} %mix.3), channel_id=1, source_target_pairs={{1,2},{2,1},{0,0},{3,3},{5,6},{6,5},{4,4},{7,7},{9,10},{10,9},{8,8... | collective-permute-start | bytes 122888 | tf_op jit(solution)/shard_map/ppermute | solution.py:400
  44.9 4.8 %collective-permute-start.8 = (bf16[80,256]{1,0:T(8,128)(2,1)S(1)}, bf16[80,256]{1,0:T(8,128)(2,1)S(1)}, u32[]{:S(2)}, u32[]{:S(2)}) collective-permute-start(bf16[80,256]{1,0:T(8,128)(2,1)S(1)} %mix.2.refs_0_), channel_id=1, source_target_pairs={{0,1},{1,0},{2,3},{3,2},{4,5},{5,4},{6,7},{7,6},{8,9},{9,8},{10,11... | collective-permute-start | bytes 122888 | tf_op jit(solution)/shard_map/ppermute | solution.py:397

commit v5 on v4

--- a/solution.py
+++ b/solution.py
@@ -372,17 +372,17 @@
         [pltpu.VMEM((padded, local), BF16)], scalars=[info],
     )
 
-    swap = [(0, 1), (1, 0), (2, 3), (3, 2)]
-    targets = [target]
-    if sources == 4:
-        text_out, moved = lax.optimization_barrier((text_out, lax.ppermute(target, "seq", swap)))
-        targets.append(moved)
-
     weights, base = call(
         functools.partial(weigh_kernel, sources, clips, reach), "weigh", [*q_blocks, *k_blocks, text_out, level],
         [((heads, group_rows, reach[1]), BF16), ((group_rows, local), F32)],
         [pltpu.VMEM((group_rows, local), BF16)] * 2, scalars=[info],
     )
+
+    swap = [(0, 1), (1, 0), (2, 3), (3, 2)]
+    targets = [target]
+    if sources == 4:
+        weights, moved = lax.optimization_barrier((weights, lax.ppermute(target, "seq", swap)))
+        targets.append(moved)
 
     def mix(place):
         return call(
@@ -396,7 +396,7 @@
         here = mix(lambda rank: rank // 2 * 2)
         parts = [here, lax.ppermute(here, "seq", swap)]
         there = mix(lambda rank: 2 - rank // 2 * 2)
-        for pairs in ([(1, 2), (2, 1), (0, 0), (3, 3)], [(0, 2), (2, 3), (3, 1), (1, 0)]):
+        for pairs in ([(1, 2), (2, 1), (0, 3), (3, 0)], [(0, 2), (2, 3), (3, 1), (1, 0)]):
             parts.append(lax.ppermute(there, "seq", pairs))
     else:
         parts = [onward(mix(lambda rank, k=k: partner(rank, k, sources)), k) for k in reversed(range(sources))]

time: 62.1 us -> 62.5 us (level)
  starting transfers between devices: 21 us -> 18.2 us
  waiting for transfers between devices: 3.23 us -> 5.62 us
  blocking collectives: 11.2 us -> 12 us
    ppermute x2, waiting for transfers between devices: 0.01 us -> 4.37 us  [per_device(): parts.append(lax.ppermute(there, 'seq', pairs))]
    ppermute x1, starting transfers between devices: 2.86 us -> 0.17 us  [per_device(): parts = [here, lax.ppermute(here, 'seq', swap)]]
    ppermute x1, waiting for transfers between devices: 1.98 us -> 0.01 us  [per_device(): parts = [here, lax.ppermute(here, 'seq', swap)]]
    all_to_all x1, blocking collectives: 11.2 us -> 12 us  [per_device(): lax.all_to_all(shares, ('dp', 'seq'), split_axis=0, concat_axis=0, tiled=...]
where the time goes in v5:
time: 62.5 us; the launch traced here: 62.3 us
  Pallas kernels  25.3 us (40%)
  starting transfers between devices  18.2 us (29%)
  blocking collectives  12 us (19%)
  waiting for transfers between devices  5.62 us (9%)
  other arithmetic  0.92 us (1%)
    pallas_call x8, Pallas kernels, call(): pl.pallas_call(kernel, in_specs=[smem()] * len(scalars) + [hbm() if i in...  25.3 us
    ppermute x7, starting transfers between devices, onward(): lax.ppermute(x, 'seq', [(i, partner(i, k, sources)) for i in range(source...  12.6 us
    all_to_all x1, blocking collectives, per_device(): lax.all_to_all(shares, ('dp', 'seq'), split_axis=0, concat_axis=0, tiled=...  12 us
    ppermute x2, starting transfers between devices, per_device(): parts.append(lax.ppermute(there, 'seq', pairs))  4.87 us
    ppermute x2, waiting for transfers between devices, per_device(): parts.append(lax.ppermute(there, 'seq', pairs))  4.37 us
  transfers between devices with their start and end apart: 11, of which 2 were waited for; matrix products, arithmetic and copies ran while one was open for 0% of the time, Pallas kernels for 37%

profile of v5, /device:TPU:0, one launch (start us, length us, event | category | flops | bytes accessed | tf_op | source)
XLA Modules:
  0.0 62.3 jit_solution(18426613013504554738)
XLA Ops:
  0.0 1.0 %cut_first.1 = (bf16[1,128,512]{2,1,0:T(8,128)(2,1)S(1)}, bf16[1,128,512]{2,1,0:T(8,128)(2,1)S(1)}) custom-call(bf16[128,2048]{1,0:T(8,128)(2,1)} %refs_0_.3), custom_call_target="tpu_custom_call" | custom-call | bytes 524288 | tf_op jit(solution)/shard_map/cut_first/pallas_call | solution.py:289
  1.0 4.1 %collective-permute-start.3 = (bf16[1,128,512]{2,1,0:T(8,128)(2,1)S(1)}, bf16[1,128,512]{2,1,0:T(8,128)(2,1)S(1)}, u32[]{:S(2)}, u32[]{:S(2)}) collective-permute-start(bf16[1,128,512]{2,1,0:T(8,128)(2,1)S(1)} %get-tuple-element.31), channel_id=1, source_target_pairs={{0,2},{1,3},{2,0},{3,1},{4,6},{5,7},{6,4},{7,5},{8,10},{9,11},{10,... | collective-permute-start | bytes 393224 | tf_op jit(solution)/shard_map/ppermute | solution.py:331
  5.1 1.5 %cut_rest.1 = (bf16[3,128,512]{2,1,0:T(8,128)(2,1)S(1)}, bf16[3,128,512]{2,1,0:T(8,128)(2,1)S(1)}, bf16[1,128,512]{2,1,0:T(8,128)(2,1)S(1)}, bf16[1,128,512]{2,1...) custom-call(bf16[128,2048]{1,0:T(8,128)(2,1)} %refs_0_.3, ...), custom_call_target="tpu_custom_call" | custom-call | bytes 2621440 | tf_op jit(solution)/shard_map/cut_rest/pallas_call | solution.py:289
  6.6 1.6 %collective-permute-start = (bf16[3,128,512]{2,1,0:T(8,128)(2,1)S(1)}, bf16[3,128,512]{2,1,0:T(8,128)(2,1)S(1)}, u32[]{:S(2)}, u32[]{:S(2)}) collective-permute-start(bf16[3,128,512]{2,1,0:T(8,128)(2,1)S(1)} %get-tuple-element.34), channel_id=1, source_target_pairs={{0,1},{1,0},{2,3},{3,2},{4,5},{5,4},{6,7},{7,6},{8,9},{9,8},{10,11... | collective-permute-start | bytes 1179656 | tf_op jit(solution)/shard_map/ppermute | solution.py:331
  8.2 1.9 %collective-permute-start.5 = (bf16[1,128,512]{2,1,0:T(8,128)(2,1)S(1)}, bf16[1,128,512]{2,1,0:T(8,128)(2,1)S(1)}, u32[]{:S(2)}, u32[]{:S(2)}) collective-permute-start(bf16[1,128,512]{2,1,0:T(8,128)(2,1)S(1)} %get-tuple-element.41), channel_id=1, source_target_pairs={{0,2},{1,3},{2,0},{3,1},{4,6},{5,7},{6,4},{7,5},{8,10},{9,11},{10,... | collective-permute-start | bytes 393224 | tf_op jit(solution)/shard_map/ppermute | solution.py:331
  10.2 1.9 %collective-permute-start.6 = (bf16[1,128,512]{2,1,0:T(8,128)(2,1)S(1)}, bf16[1,128,512]{2,1,0:T(8,128)(2,1)S(1)}, u32[]{:S(2)}, u32[]{:S(2)}) collective-permute-start(bf16[1,128,512]{2,1,0:T(8,128)(2,1)S(1)} %get-tuple-element.42), channel_id=1, source_target_pairs={{0,3},{1,2},{2,1},{3,0},{4,7},{5,6},{6,5},{7,4},{8,11},{9,10},{10,... | collective-permute-start | bytes 393224 | tf_op jit(solution)/shard_map/ppermute | solution.py:331
  12.1 0.1 multiply_cosine_fusion
  12.2 0.1 pad_add_fusion.info_ref
  12.3 14.0 %prep.1 = (f32[512,512]{1,0:T(8,128)S(1)}, f32[4,64,256]{2,1,0:T(8,128)S(1)}, f32[64,256]{1,0:T(8,128)S(1)}, f32[8,256]{1,0:T(8,128)S(1)}, f32[64,128]{1,0:T(8,1...) custom-call(s32[16]{0:T(128)S(1)} %pad_add_fusion.info_ref, ...), custom_call_target="tpu_custom_call" | custom-call | tf_op jit(solution)/shard_map/prep/pallas_call | solution.py:289
  26.4 0.0 collective-permute-done.3.refs_2_
  26.4 2.1 %collective-permute-start.1 = (bf16[1,128,512]{2,1,0:T(8,128)(2,1)S(1)}, bf16[1,128,512]{2,1,0:T(8,128)(2,1)S(1)}, u32[]{:S(2)}, u32[]{:S(2)}) collective-permute-start(bf16[1,128,512]{2,1,0:T(8,128)(2,1)S(1)} %get-tuple-element.38), channel_id=1, source_target_pairs={{0,2},{1,3},{2,0},{3,1},{4,6},{5,7},{6,4},{7,5},{8,10},{9,11},{10,... | collective-permute-start | bytes 393224 | tf_op jit(solution)/shard_map/ppermute | solution.py:331
  28.5 0.0 collective-permute-done.4.refs_3_
  28.5 0.9 %collective-permute-start.2 = (bf16[1,128,512]{2,1,0:T(8,128)(2,1)S(1)}, bf16[1,128,512]{2,1,0:T(8,128)(2,1)S(1)}, u32[]{:S(2)}, u32[]{:S(2)}) collective-permute-start(bf16[1,128,512]{2,1,0:T(8,128)(2,1)S(1)} %get-tuple-element.39), channel_id=1, source_target_pairs={{0,3},{1,2},{2,1},{3,0},{4,7},{5,6},{6,5},{7,4},{8,11},{9,10},{10,... | collective-permute-start | bytes 393224 | tf_op jit(solution)/shard_map/ppermute | solution.py:331
  29.4 0.0 collective-permute-done.refs_1_
  29.4 0.6 collective-permute-start.7
  29.9 4.5 %text.1 = (f32[656,512]{1,0:T(8,128)S(1)}, f32[4,656,128]{2,1,0:T(8,128)S(1)}) custom-call(s32[16]{0:T(128)S(1)} %pad_add_fusion.info_ref, bf16[3,128,512]{2,1,0:T(8,128)(2,1)S(1)} %get-tuple-element.33.refs_0_, bf16[3,128,512]{2,1,0:T(8,128)(2,1)S(1)} %collective-permute-done.refs_1_, bf16[1,128,512]{2,1,0:T(8,128)(2,1)S(1)} %collective-permute-done.3.refs_2_, ...), custom_call_target="tpu_custom_call" | custom-call | tf_op jit(solution)/shard_map/text/pallas_call | solution.py:289
  34.4 0.0 collective-permute-done.5.refs_4_
  34.4 0.0 collective-permute-done.6.refs_5_
  34.4 2.3 %weigh.1 = (bf16[4,512,384]{2,1,0:T(8,128)(2,1)S(1)}, f32[512,512]{1,0:T(8,128)S(1)}) custom-call(s32[16]{0:T(128)S(1)} %pad_add_fusion.info_ref, bf16[3,128,512]{2,1,0:T(8,128)(2,1)S(1)} %get-tuple-element.33.refs_0_, bf16[3,128,512]{2,1,0:T(8,128)(2,1)S(1)} %collective-permute-done.refs_1_, bf16[1,128,512]{2,1,0:T(8,128)(2,1)S(1)} %collective-permute-done.3.refs_2_, ...), custom_call_target="tpu_custom_call" | custom-call | tf_op jit(solution)/shard_map/weigh/pallas_call | solution.py:289
  36.7 1.2 %collective-permute-done.1.refs_2_ = bf16[1,128,512]{2,1,0:T(8,128)(2,1)S(1)} collective-permute-done((bf16[1,128,512]{2,1,0:T(8,128)(2,1)S(1)}, bf16[1,128,512]{2,1,0:T(8,128)(2,1)S(1)}, u32[]{:S(2)}, u32[]{:S(2)}) %collective-permute-start.1) | collective-permute-done | bytes 131104 | tf_op jit(solution)/shard_map/ppermute | solution.py:331
  38.0 0.9 %mix.3 = bf16[80,256]{1,0:T(8,128)(2,1)S(1)} custom-call(bf16[3,128,512]{2,1,0:T(8,128)(2,1)S(1)} %get-tuple-element.33.refs_0_, bf16[3,128,512]{2,1,0:T(8,128)(2,1)S(1)} %collective-permute-done.refs_1_, bf16[1,128,512]{2,1,0:T(8,128)(2,1)S(1)} %collective-permute-done.1.refs_2_, bf16[1,128,512]{2,1,0:T(8,128)(2,1)S(1)} %collective-permute-done.2.refs_3_, ...), custom_call_target="tpu_custom_call" | custom-call | flops 201326592 | bytes 1048576 | tf_op jit(solution)/shard_map/mix/pallas_call | solution.py:289
  38.9 0.0 copy-start.3
  38.9 4.3 %collective-permute-start.10 = (bf16[80,256]{1,0:T(8,128)(2,1)S(1)}, bf16[80,256]{1,0:T(8,128)(2,1)S(1)}, u32[]{:S(2)}, u32[]{:S(2)}) collective-permute-start(bf16[80,256]{1,0:T(8,128)(2,1)S(1)} %mix.3), channel_id=1, source_target_pairs={{0,2},{2,3},{3,1},{1,0},{4,6},{6,7},{7,5},{5,4},{8,10},{10,11},{11... | collective-permute-start | bytes 122888 | tf_op jit(solution)/shard_map/ppermute | solution.py:400
  43.3 0.5 collective-permute-start.9
  43.8 0.9 %mix.2.refs_0_ = bf16[80,256]{1,0:T(8,128)(2,1)S(1)} custom-call(bf16[3,128,512]{2,1,0:T(8,128)(2,1)S(1)} %get-tuple-element.33.refs_0_, bf16[3,128,512]{2,1,0:T(8,128)(2,1)S(1)} %collective-permute-done.refs_1_, bf16[1,128,512]{2,1,0:T(8,128)(2,1)S(1)} %collective-permute-done.1.refs_2_, bf16[1,128,512]{2,1,0:T(8,128)(2,1)S(1)} %collective-permute-done.2.refs_3_, ...), custom_call_target="tpu_custom_call" | custom-call | flops 201326592 | bytes 1048576 | tf_op jit(solution)/shard_map/mix/pallas_call | solution.py:289
  44.7 0.2 collective-permute-start.8
  44.9 0.0 collective-permute-done.10.refs_3_
  44.9 4.3 %collective-permute-done.9.refs_2_ = bf16[80,256]{1,0:T(8,128)(2,1)S(1)} collective-permute-done((bf16[80,256]{1,0:T(8,128)(2,1)S(1)}, bf16[80,256]{1,0:T(8,128)(2,1)S(1)}, u32[]{:S(2)}, u32[]{:S(2)}) %collective-permute-start.9) | collective-permute-done | bytes 40992 | tf_op jit(solution)/shard_map/ppermute | solution.py:400
  49.3 0.2 loss.1
  49.5 12.0 %all_to_all.5 = f32[32,1,128]{2,1,0:T(1,128)S(1)} all-to-all(f32[32,1,128]{2,1,0:T(1,128)S(1)} %loss.1), channel_id=1, replica_groups=mesh['dp'=8,'seq'=4] {'dp','seq'}, dimensions={0} | all-to-all | bytes 32768 | tf_op jit(solution)/shard_map/all_to_all | solution.py:408
  61.5 0.1 broadcast_in_dim.18
  61.6 0.7 %select_reduce_fusion = f32[8]{0:T(128)} fusion(f32[64]{0:T(128)S(1)} %broadcast_in_dim.18, s32[8]{0:T(128)S(1)} %copy-done.3), kind=kLoop, calls=%fused_computation.4 | loop fusion | flops 1528 | bytes 320 | tf_op jit(solution)/shard_map/reduce_sum | solution.py:411
  (15 shorter events, 0.1 us)
Async XLA Ops:
  0.0 12.1 %copy-start = (s32[8]{0:T(128)S(1)}, s32[8]{0:T(128)}, u32[]{:S(2)}) copy-start(s32[8]{0:T(128)} %param.18) | copy-start | bytes 100
  0.0 12.2 %copy-start.2 = (s32[1,8]{1,0:T(1,128)S(1)}, s32[1,8]{1,0:T(1,128)}, u32[]{:S(2)}) copy-start(s32[1,8]{1,0:T(1,128)} %param.17) | copy-start | bytes 100
  0.0 12.2 %copy-start.1 = (s32[8]{0:T(128)S(1)}, s32[8]{0:T(128)}, u32[]{:S(2)}) copy-start(s32[8]{0:T(128)} %param.16) | copy-start | bytes 100
  1.0 25.3 %collective-permute-start.3 = (bf16[1,128,512]{2,1,0:T(8,128)(2,1)S(1)}, bf16[1,128,512]{2,1,0:T(8,128)(2,1)S(1)}, u32[]{:S(2)}, u32[]{:S(2)}) collective-permute-start(bf16[1,128,512]{2,1,0:T(8,128)(2,1)S(1)} %get-tuple-element.31), channel_id=1, source_target_pairs={{0,2},{1,3},{2,0},{3,1},{4,6},{5,7},{6,4},{7,5},{8,10},{9,11},{10,... | collective-permute-start | bytes 393224 | tf_op jit(solution)/shard_map/ppermute | solution.py:331
  6.6 22.8 %collective-permute-start = (bf16[3,128,512]{2,1,0:T(8,128)(2,1)S(1)}, bf16[3,128,512]{2,1,0:T(8,128)(2,1)S(1)}, u32[]{:S(2)}, u32[]{:S(2)}) collective-permute-start(bf16[3,128,512]{2,1,0:T(8,128)(2,1)S(1)} %get-tuple-element.34), channel_id=1, source_target_pairs={{0,1},{1,0},{2,3},{3,2},{4,5},{5,4},{6,7},{7,6},{8,9},{9,8},{10,11... | collective-permute-start | bytes 1179656 | tf_op jit(solution)/shard_map/ppermute | solution.py:331
  8.2 20.2 %collective-permute-start.4 = (bf16[1,128,512]{2,1,0:T(8,128)(2,1)S(1)}, bf16[1,128,512]{2,1,0:T(8,128)(2,1)S(1)}, u32[]{:S(2)}, u32[]{:S(2)}) collective-permute-start(bf16[1,128,512]{2,1,0:T(8,128)(2,1)S(1)} %get-tuple-element.40), channel_id=1, source_target_pairs={{0,3},{1,2},{2,1},{3,0},{4,7},{5,6},{6,5},{7,4},{8,11},{9,10},{10,... | collective-permute-start | bytes 393224 | tf_op jit(solution)/shard_map/ppermute | solution.py:331
  8.2 26.2 %collective-permute-start.5 = (bf16[1,128,512]{2,1,0:T(8,128)(2,1)S(1)}, bf16[1,128,512]{2,1,0:T(8,128)(2,1)S(1)}, u32[]{:S(2)}, u32[]{:S(2)}) collective-permute-start(bf16[1,128,512]{2,1,0:T(8,128)(2,1)S(1)} %get-tuple-element.41), channel_id=1, source_target_pairs={{0,2},{1,3},{2,0},{3,1},{4,6},{5,7},{6,4},{7,5},{8,10},{9,11},{10,... | collective-permute-start | bytes 393224 | tf_op jit(solution)/shard_map/ppermute | solution.py:331
  10.2 24.3 %collective-permute-start.6 = (bf16[1,128,512]{2,1,0:T(8,128)(2,1)S(1)}, bf16[1,128,512]{2,1,0:T(8,128)(2,1)S(1)}, u32[]{:S(2)}, u32[]{:S(2)}) collective-permute-start(bf16[1,128,512]{2,1,0:T(8,128)(2,1)S(1)} %get-tuple-element.42), channel_id=1, source_target_pairs={{0,3},{1,2},{2,1},{3,0},{4,7},{5,6},{6,5},{7,4},{8,11},{9,10},{10,... | collective-permute-start | bytes 393224 | tf_op jit(solution)/shard_map/ppermute | solution.py:331
  26.4 11.6 %collective-permute-start.1 = (bf16[1,128,512]{2,1,0:T(8,128)(2,1)S(1)}, bf16[1,128,512]{2,1,0:T(8,128)(2,1)S(1)}, u32[]{:S(2)}, u32[]{:S(2)}) collective-permute-start(bf16[1,128,512]{2,1,0:T(8,128)(2,1)S(1)} %get-tuple-element.38), channel_id=1, source_target_pairs={{0,2},{1,3},{2,0},{3,1},{4,6},{5,7},{6,4},{7,5},{8,10},{9,11},{10,... | collective-permute-start | bytes 393224 | tf_op jit(solution)/shard_map/ppermute | solution.py:331
  28.5 9.5 %collective-permute-start.2 = (bf16[1,128,512]{2,1,0:T(8,128)(2,1)S(1)}, bf16[1,128,512]{2,1,0:T(8,128)(2,1)S(1)}, u32[]{:S(2)}, u32[]{:S(2)}) collective-permute-start(bf16[1,128,512]{2,1,0:T(8,128)(2,1)S(1)} %get-tuple-element.39), channel_id=1, source_target_pairs={{0,3},{1,2},{2,1},{3,0},{4,7},{5,6},{6,5},{7,4},{8,11},{9,10},{10,... | collective-permute-start | bytes 393224 | tf_op jit(solution)/shard_map/ppermute | solution.py:331
  29.4 7.4 %collective-permute-start.7 = (f32[64,128]{1,0:T(8,128)S(1)}, f32[64,128]{1,0:T(8,128)S(1)}, u32[]{:S(2)}, u32[]{:S(2)}) collective-permute-start(f32[64,128]{1,0:T(8,128)S(1)} %get-tuple-element.48.refs_7_), channel_id=1, source_target_pairs={{0,1},{1,0},{2,3},{3,2},{4,5},{5,4},{6,7},{7,6},{8,9},{9,8},{10,11... | collective-permute-start | bytes 98312 | tf_op jit(solution)/shard_map/ppermute | solution.py:384
  38.9 22.7 %copy-start.3 = (s32[8]{0:T(128)S(1)}, s32[8]{0:T(128)}, u32[]{:S(2)}) copy-start(s32[8]{0:T(128)} %param.23) | copy-start | bytes 100
  38.9 6.0 %collective-permute-start.10 = (bf16[80,256]{1,0:T(8,128)(2,1)S(1)}, bf16[80,256]{1,0:T(8,128)(2,1)S(1)}, u32[]{:S(2)}, u32[]{:S(2)}) collective-permute-start(bf16[80,256]{1,0:T(8,128)(2,1)S(1)} %mix.3), channel_id=1, source_target_pairs={{0,2},{2,3},{3,1},{1,0},{4,6},{6,7},{7,5},{5,4},{8,10},{10,11},{11... | collective-permute-start | bytes 122888 | tf_op jit(solution)/shard_map/ppermute | solution.py:400
  43.3 6.0 %collective-permute-start.9 = (bf16[80,256]{1,0:T(8,128)(2,1)S(1)}, bf16[80,256]{1,0:T(8,128)(2,1)S(1)}, u32[]{:S(2)}, u32[]{:S(2)}) collective-permute-start(bf16[80,256]{1,0:T(8,128)(2,1)S(1)} %mix.3), channel_id=1, source_target_pairs={{1,2},{2,1},{0,3},{3,0},{5,6},{6,5},{4,7},{7,4},{9,10},{10,9},{8,1... | collective-permute-start | bytes 122888 | tf_op jit(solution)/shard_map/ppermute | solution.py:400
  44.7 4.5 %collective-permute-start.8 = (bf16[80,256]{1,0:T(8,128)(2,1)S(1)}, bf16[80,256]{1,0:T(8,128)(2,1)S(1)}, u32[]{:S(2)}, u32[]{:S(2)}) collective-permute-start(bf16[80,256]{1,0:T(8,128)(2,1)S(1)} %mix.2.refs_0_), channel_id=1, source_target_pairs={{0,1},{1,0},{2,3},{3,2},{4,5},{5,4},{6,7},{7,6},{8,9},{9,8},{10,11... | collective-permute-start | bytes 122888 | tf_op jit(solution)/shard_map/ppermute | solution.py:397

commit v6 on v5

--- a/solution.py
+++ b/solution.py
@@ -13,6 +13,7 @@
 EPS = 1e-06
 NEG = -1e30
 STAT_ROWS = 16
+MERGED_ROWS = 8
 ALIGN = 16
 NEAR = 2
 F32 = jnp.float32
@@ -62,15 +63,9 @@
     return pl.ds(pl.multiple_of(source * tok_dev, tok_dev), tok_dev)
 
 
-def summed_here(rank, sources, tok_dev):
-    if sources != 4:
-        return rank * tok_dev, tok_dev, True
-    return rank // 2 * 2 * tok_dev, 2 * tok_dev, (rank == 1) | (rank == 2)
-
-
 def origins(rank, sources):
     if sources == 4:
-        return [rank, rank ^ 1, 3 - rank, (3 - rank) ^ 1]
+        return [rank, rank ^ 2, rank ^ 1, rank ^ 3]
     ahead = reversed(range(sources))
     return [partner(rank, k if sources & (sources - 1) == 0 else sources - k, sources) for k in ahead]
 
@@ -92,7 +87,7 @@
 
 def prep_kernel(
     sources, clips, info_ref, act_ref, mod_hbm, wt_hbm, noise_hbm, clean_hbm, kv_hbm,
-    scale_ref, slope_ref, shift_ref, share_ref, target_ref, weight_ref, keys_ref, values_ref,
+    scale_ref, slope_ref, offset_ref, share_ref, weight_ref, keys_ref, values_ref,
     mods, mod_buf, wt_buf, noise_buf, clean_buf, kv_buf, sems,
 ):
     width = wt_buf.shape[1]
@@ -109,21 +104,21 @@
     mods[...] = jnp.dot(act_ref[...], mod_buf[...], preferred_element_type=F32)
     weight = wt_buf[...].astype(F32)
     shifts = nt_dot(weight, mods[:, :width], EXACT)
-    first, count, active = summed_here(rank, sources, tok_dev)
-    tok_clip = clip_index(info_ref, clips, (clips, count), 1, first)
-    picks = (tok_clip == lax.broadcasted_iota(jnp.int32, (clips, count), 0)).astype(F32)
+    tok_clip = clip_index(info_ref, clips, (clips, tok_dev), 1, rank * tok_dev)
+    picks = (tok_clip == lax.broadcasted_iota(jnp.int32, (clips, tok_dev), 0)).astype(F32)
     slot = lax.broadcasted_iota(jnp.int32, (clips, 1), 0)
     sizes = jnp.zeros((clips, 1), F32)
     for c in range(clips):
         sizes = jnp.where(slot == c, info_ref[c].astype(F32), sizes)
-    share_ref[...] = jnp.where(active, picks / sizes, 0.0)
+    share_ref[...] = picks / sizes
     for place, source in enumerate(origins(rank, sources)):
         low = pl.multiple_of(source * local, HEAD_DIM)
         scales = 1.0 + mods[:, pl.ds(pl.multiple_of(width + low, HEAD_DIM), local)]
         slopes = nt_dot(wt_buf[:, pl.ds(low, local)].astype(F32), scales, EXACT)
         slope_ref[place] = jnp.dot(slopes, picks, precision=EXACT, preferred_element_type=F32)
-    shift_ref[...] = jnp.dot(shifts, picks, precision=EXACT, preferred_element_type=F32)
-    target_ref[...] = noise_buf[...] - clean_buf[...]
+    offset_ref[...] = jnp.dot(shifts, picks, precision=EXACT, preferred_element_type=F32) - (
+        noise_buf[...] - clean_buf[...]
+    )
     row_clip = clip_index(info_ref, clips, (group_rows, clips), 0, 0)
     row_picks = (row_clip == lax.broadcasted_iota(jnp.int32, (group_rows, clips), 1)).astype(F32)
     mine = 1.0 + mods[:, pl.ds(pl.multiple_of(width + rank * local, HEAD_DIM), local)]
@@ -233,40 +228,59 @@
     s_high, s_low = two_parts(attended_full * attended_full)
     weight = wt_ref[...]
     every = jnp.ones((STAT_ROWS, local), BF16)
-    out_ref[:channels, :] = (nt_dot(weight, y_high) + nt_dot(weight, y_low)).astype(BF16)
+    out_ref[:channels, :] = (nt_dot(weight, y_high) + nt_dot(weight, y_low)).astype(out_ref.dtype)
     row = lax.broadcasted_iota(jnp.int32, (STAT_ROWS, count), 0)
     rest = jnp.where(row < 3, nt_dot(every, attended), nt_dot(every, s_high) + nt_dot(every, s_low))
     terms = jnp.zeros((STAT_ROWS, count), F32)
     for place in range(3):
-        term = rest.astype(BF16).astype(F32)
+        term = rest.astype(out_ref.dtype).astype(F32)
         terms = jnp.where((row == place) | (row == place + 3), term, terms)
         rest = rest - term
-    out_ref[channels:, :] = terms.astype(BF16)
-
-
-def loss_kernel(count, width, *refs):
+    out_ref[channels:, :] = terms.astype(out_ref.dtype)
+
+
+def read_part(part, channels):
+    stat = part[channels:]
+    return part[:channels], stat[0:1] + stat[1:2] + stat[2:3], stat[3:4] + stat[4:5] + stat[5:6]
+
+
+def merge_kernel(near_ref, far_ref, keep_ref, send_ref):
+    tok_dev = keep_ref.shape[1]
+    channels = near_ref.shape[0] - STAT_ROWS
+    mine = lax.axis_index("seq") & 1
+    for ref, half in ((send_ref, 1 - mine), (keep_ref, mine)):
+        cols = pl.ds(pl.multiple_of(half * tok_dev, HEAD_DIM), tok_dev)
+        near, near_sum, near_square = read_part(near_ref[:, cols], channels)
+        far, far_sum, far_square = read_part(far_ref[:, cols].astype(F32), channels)
+        ref[:channels, :] = near + far
+        row = lax.broadcasted_iota(jnp.int32, (MERGED_ROWS, tok_dev), 0)
+        stats = jnp.where(row == 0, near_sum, jnp.where(row == 1, far_sum, near_square + far_square))
+        ref[channels:, :] = stats
+
+
+def loss_kernel(count, merged, width, *refs):
     part_refs = refs[:count]
-    slope_ref, shift_ref, share_ref, *target_refs, out_ref = refs[count:]
-    channels = slope_ref.shape[1]
+    slope_ref, offset_ref, share_ref, out_ref = refs[count:]
+    sources, channels = slope_ref.shape[:2]
     clips = share_ref.shape[0]
-    parts = [part[...].astype(F32) for part in part_refs]
-    stats = [part[channels:] for part in parts]
-    sums = [stat[0:1] + stat[1:2] + stat[2:3] for stat in stats]
-    squares = [stat[3:4] + stat[4:5] + stat[5:6] for stat in stats]
+    projected, sums, squares = [], [], []
+    for ref in part_refs:
+        part = ref[...].astype(F32)
+        if merged:
+            projected.append(part[:channels])
+            sums += [part[channels : channels + 1], part[channels + 1 : channels + 2]]
+            squares.append(part[channels + 2 : channels + 3])
+        else:
+            for place, value in zip((projected, sums, squares), read_part(part, channels)):
+                place.append(value)
     center = sum(sums[1:], sums[0]) * (1.0 / width)
     spread = sum(squares[1:], squares[0]) * (1.0 / width) - center * center
-    total = jnp.zeros(slope_ref.shape[1:], F32)
-    for place, part in enumerate(parts):
-        total = total + part[:channels] + (sums[place] * (count / width) - center) * slope_ref[place]
-    targets = [target[...] for target in target_refs]
-    if len(targets) == 2:
-        swap = lax.axis_index("seq") == 1
-        targets = [jnp.where(swap, *targets[::-1]), jnp.where(swap, *targets)]
-    offset = shift_ref[...] - jnp.concatenate(targets, axis=1)
-    diff = total * lax.rsqrt(spread + EPS) + offset
+    total = sum(projected[1:], projected[0])
+    for place in range(sources):
+        total = total + (sums[place] * (sources / width) - center) * slope_ref[place]
+    diff = total * lax.rsqrt(spread + EPS) + offset_ref[...]
     error = jnp.sum(diff * diff, axis=0, keepdims=True) * (1.0 / channels)
-    share = share_ref[...]
-    sums = jnp.sum(jnp.where(share > 0.0, share * error, 0.0), axis=1, keepdims=True)
+    sums = jnp.sum(share_ref[...] * error, axis=1, keepdims=True)
     lanes = lax.broadcasted_iota(jnp.int32, (clips, out_ref.shape[2]), 1)
     mine = lanes == lax.broadcasted_iota(jnp.int32, lanes.shape, 0)
     row = jnp.sum(jnp.where(mine, sums, 0.0), axis=0, keepdims=True)
@@ -345,13 +359,12 @@
 
     weight_t = final_weight.T
     activated = jax.nn.silu(step_embedding(timesteps)).astype(BF16)
-    _, summed, _ = summed_here(0, sources, tok_dev)
-    scale_tok, slope, shift, share, target, weight_local, text_keys, text_values = call(
+    scale_tok, slope, offset, share, weight_local, text_keys, text_values = call(
         functools.partial(prep_kernel, sources, clips), "prep",
         [activated, mod_weight, weight_t, noise.T, clean.T, text_kv],
         [
-            ((group_rows, local), F32), ((sources, channels, summed), F32), ((channels, summed), F32),
-            ((clips, summed), F32), ((channels, tok_dev), F32),
+            ((group_rows, local), F32), ((sources, channels, tok_dev), F32), ((channels, tok_dev), F32),
+            ((clips, tok_dev), F32),
             ((channels, local), BF16), ((clips, text_len, local), BF16), ((clips, text_len, local), BF16),
         ],
         [
@@ -378,31 +391,26 @@
         [pltpu.VMEM((group_rows, local), BF16)] * 2, scalars=[info],
     )
 
-    swap = [(0, 1), (1, 0), (2, 3), (3, 2)]
-    targets = [target]
-    if sources == 4:
-        weights, moved = lax.optimization_barrier((weights, lax.ppermute(target, "seq", swap)))
-        targets.append(moved)
-
-    def mix(place):
+    def mix(place, tiles=1, dtype=BF16):
         return call(
             functools.partial(mix_kernel, sources, reach, place), "mix",
             [*near_blocks, *v_blocks, weights, base, scale_tok, weight_local],
-            [((channels + STAT_ROWS, summed), BF16)],
-            [pltpu.VMEM((group_rows, local), BF16)], flops=4 * summed * reach[1] * local, traffic=2**20,
+            [((channels + STAT_ROWS, tiles * tok_dev), dtype)],
+            [pltpu.VMEM((group_rows, local), BF16)], flops=4 * tok_dev * reach[1] * local, traffic=2**20,
         )[0]
 
     if sources == 4:
-        here = mix(lambda rank: rank // 2 * 2)
-        parts = [here, lax.ppermute(here, "seq", swap)]
-        there = mix(lambda rank: 2 - rank // 2 * 2)
-        for pairs in ([(1, 2), (2, 1), (0, 3), (3, 0)], [(0, 2), (2, 3), (3, 1), (1, 0)]):
-            parts.append(lax.ppermute(there, "seq", pairs))
+        arrived = onward(mix(lambda rank: (rank ^ 2) // 2 * 2, 2), 2)
+        keep, send = call(
+            merge_kernel, "merge", [mix(lambda rank: rank // 2 * 2, 2, F32), arrived],
+            [((channels + MERGED_ROWS, tok_dev), F32)] * 2,
+        )
+        parts = [keep, onward(send, 1)]
     else:
         parts = [onward(mix(lambda rank, k=k: partner(rank, k, sources)), k) for k in reversed(range(sources))]
 
     (shares,) = call(
-        functools.partial(loss_kernel, len(parts), width), "loss", [*parts, slope, shift, share, *targets],
+        functools.partial(loss_kernel, len(parts), sources == 4, width), "loss", [*parts, slope, offset, share],
         [((groups * sources, 1, HEAD_DIM), F32)],
     )
     everyone = lax.all_to_all(shares, ("dp", "seq"), split_axis=0, concat_axis=0, tiled=True)

time: 62.5 us -> 61.7 us (0.987)
  waiting for transfers between devices: 5.62 us -> 4.9 us
    ppermute x4 -> x0, starting transfers between devices: 5.6 us -> none  [the longest x2 4.87 us: per_device(): parts.append(lax.ppermute(there, 'seq', pairs))]
    ppermute x7 -> x9, starting transfers between devices: 12.6 us -> 18.1 us  [onward(): lax.ppermute(x, 'seq', [(i, partner(i, k, sources)) for i in range(source...]
    ppermute x4 -> x0, waiting for transfers between devices: 4.37 us -> none  [the longest x2 4.37 us: per_device(): parts.append(lax.ppermute(there, 'seq', pairs))]
    ppermute x7 -> x9, waiting for transfers between devices: 1.25 us -> 4.9 us  [onward(): lax.ppermute(x, 'seq', [(i, partner(i, k, sources)) for i in range(source...]
    pallas_call x8 -> x9, Pallas kernels: 25.3 us -> 25.4 us  [call(): pl.pallas_call(kernel, in_specs=[smem()] * len(scalars) + [hbm() if i in...]
  transfers between devices with their start and end apart: 11 -> 9, of which waited for: 2 -> 3; matrix products, arithmetic and copies ran while one was open for 0% -> 0% of each run, Pallas kernels for 37% -> 38%
where the time goes in v6:
time: 61.7 us; the launch traced here: 61.6 us
  Pallas kernels  25.4 us (41%)
  starting transfers between devices  18.1 us (29%)
  blocking collectives  12.1 us (20%)
  waiting for transfers between devices  4.9 us (8%)
  other arithmetic  0.92 us (1%)
    pallas_call x9, Pallas kernels, call(): pl.pallas_call(kernel, in_specs=[smem()] * len(scalars) + [hbm() if i in...  25.4 us
    ppermute x9, starting transfers between devices, onward(): lax.ppermute(x, 'seq', [(i, partner(i, k, sources)) for i in range(source...  18.1 us
    all_to_all x1, blocking collectives, per_device(): lax.all_to_all(shares, ('dp', 'seq'), split_axis=0, concat_axis=0, tiled=...  12.1 us
    ppermute x9, waiting for transfers between devices, onward(): lax.ppermute(x, 'seq', [(i, partner(i, k, sources)) for i in range(source...  4.9 us
  transfers between devices with their start and end apart: 9, of which 3 were waited for; matrix products, arithmetic and copies ran while one was open for 0% of the time, Pallas kernels for 38%

profile of v6, /device:TPU:0, one launch (start us, length us, event | category | flops | bytes accessed | tf_op | source)
XLA Modules:
  0.0 61.6 jit_solution(5860071346872108951)
XLA Ops:
  0.0 1.0 %cut_first.1 = (bf16[1,128,512]{2,1,0:T(8,128)(2,1)S(1)}, bf16[1,128,512]{2,1,0:T(8,128)(2,1)S(1)}) custom-call(bf16[128,2048]{1,0:T(8,128)(2,1)} %refs_0_.3), custom_call_target="tpu_custom_call" | custom-call | bytes 524288 | tf_op jit(solution)/shard_map/cut_first/pallas_call | solution.py:303
  1.0 5.1 %collective-permute-start.4 = (bf16[1,128,512]{2,1,0:T(8,128)(2,1)S(1)}, bf16[1,128,512]{2,1,0:T(8,128)(2,1)S(1)}, u32[]{:S(2)}, u32[]{:S(2)}) collective-permute-start(bf16[1,128,512]{2,1,0:T(8,128)(2,1)S(1)} %get-tuple-element.39), channel_id=1, source_target_pairs={{0,3},{1,2},{2,1},{3,0},{4,7},{5,6},{6,5},{7,4},{8,11},{9,10},{10,... | collective-permute-start | bytes 393224 | tf_op jit(solution)/shard_map/ppermute | solution.py:345
  6.2 0.0 collective-permute-start.3
  6.2 1.5 %cut_rest.1 = (bf16[3,128,512]{2,1,0:T(8,128)(2,1)S(1)}, bf16[3,128,512]{2,1,0:T(8,128)(2,1)S(1)}, bf16[1,128,512]{2,1,0:T(8,128)(2,1)S(1)}, bf16[1,128,512]{2,1...) custom-call(bf16[128,2048]{1,0:T(8,128)(2,1)} %refs_0_.3, ...), custom_call_target="tpu_custom_call" | custom-call | bytes 2621440 | tf_op jit(solution)/shard_map/cut_rest/pallas_call | solution.py:303
  7.6 3.0 %collective-permute-start.5 = (bf16[1,128,512]{2,1,0:T(8,128)(2,1)S(1)}, bf16[1,128,512]{2,1,0:T(8,128)(2,1)S(1)}, u32[]{:S(2)}, u32[]{:S(2)}) collective-permute-start(bf16[1,128,512]{2,1,0:T(8,128)(2,1)S(1)} %get-tuple-element.40), channel_id=1, source_target_pairs={{0,2},{1,3},{2,0},{3,1},{4,6},{5,7},{6,4},{7,5},{8,10},{9,11},{10,... | collective-permute-start | bytes 393224 | tf_op jit(solution)/shard_map/ppermute | solution.py:345
  10.6 0.1 collective-permute-start.6
  10.7 0.6 collective-permute-start
  11.3 0.1 multiply_cosine_fusion
  11.4 0.1 pad_add_fusion.info_ref
  11.5 14.1 %prep.1 = (f32[512,512]{1,0:T(8,128)S(1)}, f32[4,64,128]{2,1,0:T(8,128)S(1)}, f32[64,128]{1,0:T(8,128)S(1)}, f32[8,128]{1,0:T(8,128)S(1)}, bf16[64,512]{1,0:T(8,...) custom-call(s32[16]{0:T(128)S(1)} %pad_add_fusion.info_ref, ...), custom_call_target="tpu_custom_call" | custom-call | tf_op jit(solution)/shard_map/prep/pallas_call | solution.py:303
  25.6 0.0 collective-permute-done.4.refs_3_
  25.6 3.8 %collective-permute-start.1 = (bf16[1,128,512]{2,1,0:T(8,128)(2,1)S(1)}, bf16[1,128,512]{2,1,0:T(8,128)(2,1)S(1)}, u32[]{:S(2)}, u32[]{:S(2)}) collective-permute-start(bf16[1,128,512]{2,1,0:T(8,128)(2,1)S(1)} %get-tuple-element.37), channel_id=1, source_target_pairs={{0,2},{1,3},{2,0},{3,1},{4,6},{5,7},{6,4},{7,5},{8,10},{9,11},{10,... | collective-permute-start | bytes 393224 | tf_op jit(solution)/shard_map/ppermute | solution.py:345
  29.4 0.0 collective-permute-done.3.refs_2_
  29.4 0.1 collective-permute-start.2
  29.5 0.0 collective-permute-done.refs_1_
  29.5 4.5 %text.1 = (f32[656,512]{1,0:T(8,128)S(1)}, f32[4,656,128]{2,1,0:T(8,128)S(1)}) custom-call(s32[16]{0:T(128)S(1)} %pad_add_fusion.info_ref, bf16[3,128,512]{2,1,0:T(8,128)(2,1)S(1)} %get-tuple-element.32.refs_0_, bf16[3,128,512]{2,1,0:T(8,128)(2,1)S(1)} %collective-permute-done.refs_1_, bf16[1,128,512]{2,1,0:T(8,128)(2,1)S(1)} %collective-permute-done.3.refs_2_, ...), custom_call_target="tpu_custom_call" | custom-call | tf_op jit(solution)/shard_map/text/pallas_call | solution.py:303
  34.0 0.0 collective-permute-done.5.refs_4_
  34.0 0.0 collective-permute-done.6.refs_5_
  34.0 2.3 %weigh.1 = (bf16[4,512,384]{2,1,0:T(8,128)(2,1)S(1)}, f32[512,512]{1,0:T(8,128)S(1)}) custom-call(s32[16]{0:T(128)S(1)} %pad_add_fusion.info_ref, bf16[3,128,512]{2,1,0:T(8,128)(2,1)S(1)} %get-tuple-element.32.refs_0_, bf16[3,128,512]{2,1,0:T(8,128)(2,1)S(1)} %collective-permute-done.refs_1_, bf16[1,128,512]{2,1,0:T(8,128)(2,1)S(1)} %collective-permute-done.3.refs_2_, ...), custom_call_target="tpu_custom_call" | custom-call | tf_op jit(solution)/shard_map/weigh/pallas_call | solution.py:303
  36.3 1.7 %collective-permute-done.1.refs_2_ = bf16[1,128,512]{2,1,0:T(8,128)(2,1)S(1)} collective-permute-done((bf16[1,128,512]{2,1,0:T(8,128)(2,1)S(1)}, bf16[1,128,512]{2,1,0:T(8,128)(2,1)S(1)}, u32[]{:S(2)}, u32[]{:S(2)}) %collective-permute-start.1) | collective-permute-done | bytes 131104 | tf_op jit(solution)/shard_map/ppermute | solution.py:345
  38.0 0.0 collective-permute-done.2.refs_3_
  38.0 0.9 %mix.3 = bf16[80,256]{1,0:T(8,128)(2,1)S(1)} custom-call(bf16[3,128,512]{2,1,0:T(8,128)(2,1)S(1)} %get-tuple-element.32.refs_0_, bf16[3,128,512]{2,1,0:T(8,128)(2,1)S(1)} %collective-permute-done.refs_1_, bf16[1,128,512]{2,1,0:T(8,128)(2,1)S(1)} %collective-permute-done.1.refs_2_, bf16[1,128,512]{2,1,0:T(8,128)(2,1)S(1)} %collective-permute-done.2.refs_3_, ...), custom_call_target="tpu_custom_call" | custom-call | flops 100663296 | bytes 1048576 | tf_op jit(solution)/shard_map/mix/pallas_call | solution.py:303
  39.0 0.0 copy-start.3
  39.0 3.5 %collective-permute-start.7 = (bf16[80,256]{1,0:T(8,128)(2,1)S(1)}, bf16[80,256]{1,0:T(8,128)(2,1)S(1)}, u32[]{:S(2)}, u32[]{:S(2)}) collective-permute-start(bf16[80,256]{1,0:T(8,128)(2,1)S(1)} %mix.3), channel_id=1, source_target_pairs={{0,2},{1,3},{2,0},{3,1},{4,6},{5,7},{6,4},{7,5},{8,10},{9,11},{10,... | collective-permute-start | bytes 122888 | tf_op jit(solution)/shard_map/ppermute | solution.py:345
  42.5 0.9 %mix.2.near_ref = f32[80,256]{1,0:T(8,128)S(1)} custom-call(bf16[3,128,512]{2,1,0:T(8,128)(2,1)S(1)} %get-tuple-element.32.refs_0_, bf16[3,128,512]{2,1,0:T(8,128)(2,1)S(1)} %collective-permute-done.refs_1_, bf16[1,128,512]{2,1,0:T(8,128)(2,1)S(1)} %collective-permute-done.1.refs_2_, bf16[1,128,512]{2,1,0:T(8,128)(2,1)S(1)} %collective-permute-done.2.refs_3_, ...), custom_call_target="tpu_custom_call" | custom-call | flops 100663296 | bytes 1048576 | tf_op jit(solution)/shard_map/mix/pallas_call | solution.py:303
  43.4 1.1 %collective-permute-done.7.far_ref = bf16[80,256]{1,0:T(8,128)(2,1)S(1)} collective-permute-done((bf16[80,256]{1,0:T(8,128)(2,1)S(1)}, bf16[80,256]{1,0:T(8,128)(2,1)S(1)}, u32[]{:S(2)}, u32[]{:S(2)}) %collective-permute-start.7) | collective-permute-done | bytes 40992 | tf_op jit(solution)/shard_map/ppermute | solution.py:345
  44.5 2.0 %collective-permute-start.8 = (f32[72,128]{1,0:T(8,128)S(1)}, f32[72,128]{1,0:T(8,128)S(1)}, u32[]{:S(2)}, u32[]{:S(2)}) collective-permute-start(f32[72,128]{1,0:T(8,128)S(1)} %get-tuple-element.51), channel_id=1, source_target_pairs={{0,1},{1,0},{2,3},{3,2},{4,5},{5,4},{6,7},{7,6},{8,9},{9,8},{10,11... | collective-permute-start | bytes 110600 | tf_op jit(solution)/shard_map/ppermute | solution.py:345
  46.5 2.1 %collective-permute-done.8.refs_1_ = f32[72,128]{1,0:T(8,128)S(1)} collective-permute-done((f32[72,128]{1,0:T(8,128)S(1)}, f32[72,128]{1,0:T(8,128)S(1)}, u32[]{:S(2)}, u32[]{:S(2)}) %collective-permute-start.8) | collective-permute-done | bytes 36896 | tf_op jit(solution)/shard_map/ppermute | solution.py:345
  48.5 0.1 loss.1
  48.7 12.1 %all_to_all.5 = f32[32,1,128]{2,1,0:T(1,128)S(1)} all-to-all(f32[32,1,128]{2,1,0:T(1,128)S(1)} %loss.1), channel_id=1, replica_groups=mesh['dp'=8,'seq'=4] {'dp','seq'}, dimensions={0} | all-to-all | bytes 32768 | tf_op jit(solution)/shard_map/all_to_all | solution.py:416
  60.8 0.1 broadcast_in_dim.18
  60.9 0.7 %select_reduce_fusion = f32[8]{0:T(128)} fusion(f32[64]{0:T(128)S(1)} %broadcast_in_dim.18, s32[8]{0:T(128)S(1)} %copy-done.3), kind=kLoop, calls=%fused_computation.4 | loop fusion | flops 1528 | bytes 320 | tf_op jit(solution)/shard_map/reduce_sum | solution.py:419
  (12 shorter events, 0.1 us)
Async XLA Ops:
  0.0 11.3 %copy-start = (s32[8]{0:T(128)S(1)}, s32[8]{0:T(128)}, u32[]{:S(2)}) copy-start(s32[8]{0:T(128)} %param.18) | copy-start | bytes 100
  0.0 11.4 %copy-start.2 = (s32[1,8]{1,0:T(1,128)S(1)}, s32[1,8]{1,0:T(1,128)}, u32[]{:S(2)}) copy-start(s32[1,8]{1,0:T(1,128)} %param.17) | copy-start | bytes 100
  0.0 11.4 %copy-start.1 = (s32[8]{0:T(128)S(1)}, s32[8]{0:T(128)}, u32[]{:S(2)}) copy-start(s32[8]{0:T(128)} %param.16) | copy-start | bytes 100
  1.0 24.5 %collective-permute-start.4 = (bf16[1,128,512]{2,1,0:T(8,128)(2,1)S(1)}, bf16[1,128,512]{2,1,0:T(8,128)(2,1)S(1)}, u32[]{:S(2)}, u32[]{:S(2)}) collective-permute-start(bf16[1,128,512]{2,1,0:T(8,128)(2,1)S(1)} %get-tuple-element.39), channel_id=1, source_target_pairs={{0,3},{1,2},{2,1},{3,0},{4,7},{5,6},{6,5},{7,4},{8,11},{9,10},{10,... | collective-permute-start | bytes 393224 | tf_op jit(solution)/shard_map/ppermute | solution.py:345
  6.2 23.2 %collective-permute-start.3 = (bf16[1,128,512]{2,1,0:T(8,128)(2,1)S(1)}, bf16[1,128,512]{2,1,0:T(8,128)(2,1)S(1)}, u32[]{:S(2)}, u32[]{:S(2)}) collective-permute-start(bf16[1,128,512]{2,1,0:T(8,128)(2,1)S(1)} %get-tuple-element.30), channel_id=1, source_target_pairs={{0,2},{1,3},{2,0},{3,1},{4,6},{5,7},{6,4},{7,5},{8,10},{9,11},{10,... | collective-permute-start | bytes 393224 | tf_op jit(solution)/shard_map/ppermute | solution.py:345
  7.6 26.4 %collective-permute-start.5 = (bf16[1,128,512]{2,1,0:T(8,128)(2,1)S(1)}, bf16[1,128,512]{2,1,0:T(8,128)(2,1)S(1)}, u32[]{:S(2)}, u32[]{:S(2)}) collective-permute-start(bf16[1,128,512]{2,1,0:T(8,128)(2,1)S(1)} %get-tuple-element.40), channel_id=1, source_target_pairs={{0,2},{1,3},{2,0},{3,1},{4,6},{5,7},{6,4},{7,5},{8,10},{9,11},{10,... | collective-permute-start | bytes 393224 | tf_op jit(solution)/shard_map/ppermute | solution.py:345
  10.6 23.4 %collective-permute-start.6 = (bf16[1,128,512]{2,1,0:T(8,128)(2,1)S(1)}, bf16[1,128,512]{2,1,0:T(8,128)(2,1)S(1)}, u32[]{:S(2)}, u32[]{:S(2)}) collective-permute-start(bf16[1,128,512]{2,1,0:T(8,128)(2,1)S(1)} %get-tuple-element.41), channel_id=1, source_target_pairs={{0,3},{1,2},{2,1},{3,0},{4,7},{5,6},{6,5},{7,4},{8,11},{9,10},{10,... | collective-permute-start | bytes 393224 | tf_op jit(solution)/shard_map/ppermute | solution.py:345
  10.7 18.8 %collective-permute-start = (bf16[3,128,512]{2,1,0:T(8,128)(2,1)S(1)}, bf16[3,128,512]{2,1,0:T(8,128)(2,1)S(1)}, u32[]{:S(2)}, u32[]{:S(2)}) collective-permute-start(bf16[3,128,512]{2,1,0:T(8,128)(2,1)S(1)} %get-tuple-element.33), channel_id=1, source_target_pairs={{0,1},{1,0},{2,3},{3,2},{4,5},{5,4},{6,7},{7,6},{8,9},{9,8},{10,11... | collective-permute-start | bytes 1179656 | tf_op jit(solution)/shard_map/ppermute | solution.py:345
  25.6 12.4 %collective-permute-start.1 = (bf16[1,128,512]{2,1,0:T(8,128)(2,1)S(1)}, bf16[1,128,512]{2,1,0:T(8,128)(2,1)S(1)}, u32[]{:S(2)}, u32[]{:S(2)}) collective-permute-start(bf16[1,128,512]{2,1,0:T(8,128)(2,1)S(1)} %get-tuple-element.37), channel_id=1, source_target_pairs={{0,2},{1,3},{2,0},{3,1},{4,6},{5,7},{6,4},{7,5},{8,10},{9,11},{10,... | collective-permute-start | bytes 393224 | tf_op jit(solution)/shard_map/ppermute | solution.py:345
  29.4 8.6 %collective-permute-start.2 = (bf16[1,128,512]{2,1,0:T(8,128)(2,1)S(1)}, bf16[1,128,512]{2,1,0:T(8,128)(2,1)S(1)}, u32[]{:S(2)}, u32[]{:S(2)}) collective-permute-start(bf16[1,128,512]{2,1,0:T(8,128)(2,1)S(1)} %get-tuple-element.38), channel_id=1, source_target_pairs={{0,3},{1,2},{2,1},{3,0},{4,7},{5,6},{6,5},{7,4},{8,11},{9,10},{10,... | collective-permute-start | bytes 393224 | tf_op jit(solution)/shard_map/ppermute | solution.py:345
  39.0 21.9 %copy-start.3 = (s32[8]{0:T(128)S(1)}, s32[8]{0:T(128)}, u32[]{:S(2)}) copy-start(s32[8]{0:T(128)} %param.23) | copy-start | bytes 100
  39.0 5.5 %collective-permute-start.7 = (bf16[80,256]{1,0:T(8,128)(2,1)S(1)}, bf16[80,256]{1,0:T(8,128)(2,1)S(1)}, u32[]{:S(2)}, u32[]{:S(2)}) collective-permute-start(bf16[80,256]{1,0:T(8,128)(2,1)S(1)} %mix.3), channel_id=1, source_target_pairs={{0,2},{1,3},{2,0},{3,1},{4,6},{5,7},{6,4},{7,5},{8,10},{9,11},{10,... | collective-permute-start | bytes 122888 | tf_op jit(solution)/shard_map/ppermute | solution.py:345
  44.5 4.0 %collective-permute-start.8 = (f32[72,128]{1,0:T(8,128)S(1)}, f32[72,128]{1,0:T(8,128)S(1)}, u32[]{:S(2)}, u32[]{:S(2)}) collective-permute-start(f32[72,128]{1,0:T(8,128)S(1)} %get-tuple-element.51), channel_id=1, source_target_pairs={{0,1},{1,0},{2,3},{3,2},{4,5},{5,4},{6,7},{7,6},{8,9},{9,8},{10,11... | collective-permute-start | bytes 110600 | tf_op jit(solution)/shard_map/ppermute | solution.py:345

commit v7 on v6

--- a/solution.py
+++ b/solution.py
@@ -13,7 +13,6 @@
 EPS = 1e-06
 NEG = -1e30
 STAT_ROWS = 16
-MERGED_ROWS = 8
 ALIGN = 16
 NEAR = 2
 F32 = jnp.float32
@@ -64,8 +63,6 @@
 
 
 def origins(rank, sources):
-    if sources == 4:
-        return [rank, rank ^ 2, rank ^ 1, rank ^ 3]
     ahead = reversed(range(sources))
     return [partner(rank, k if sources & (sources - 1) == 0 else sources - k, sources) for k in ahead]
 
@@ -205,7 +202,7 @@
             base_ref[rows, head_cols(h)] = (fade * share) * text_ref[rows, head_cols(h)]
 
 
-def mix_kernel(sources, reach, place, *refs):
+def mix_kernel(sources, reach, k_target, *refs):
     v_refs = refs[:sources]
     weight_ref, base_ref, scale_ref, wt_ref, out_ref, v_all = refs[sources:]
     tok_dev, local = v_refs[0].shape[1:]
@@ -215,7 +212,7 @@
     for k in range(sources):
         v_all[source_rows(sources, k, tok_dev), :] = v_refs[k][2 if k < NEAR else 0]
     count = out_ref.shape[1]
-    first = pl.multiple_of(place(lax.axis_index("seq")) * tok_dev, tok_dev)
+    first = pl.multiple_of(partner(lax.axis_index("seq"), k_target, sources) * tok_dev, tok_dev)
     rows = pl.ds(first, count)
     span = pl.ds(pl.multiple_of(reach_of(first, reach, group_rows), HEAD_DIM), reach[1])
     mixed = [
@@ -244,35 +241,15 @@
     return part[:channels], stat[0:1] + stat[1:2] + stat[2:3], stat[3:4] + stat[4:5] + stat[5:6]
 
 
-def merge_kernel(near_ref, far_ref, keep_ref, send_ref):
-    tok_dev = keep_ref.shape[1]
-    channels = near_ref.shape[0] - STAT_ROWS
-    mine = lax.axis_index("seq") & 1
-    for ref, half in ((send_ref, 1 - mine), (keep_ref, mine)):
-        cols = pl.ds(pl.multiple_of(half * tok_dev, HEAD_DIM), tok_dev)
-        near, near_sum, near_square = read_part(near_ref[:, cols], channels)
-        far, far_sum, far_square = read_part(far_ref[:, cols].astype(F32), channels)
-        ref[:channels, :] = near + far
-        row = lax.broadcasted_iota(jnp.int32, (MERGED_ROWS, tok_dev), 0)
-        stats = jnp.where(row == 0, near_sum, jnp.where(row == 1, far_sum, near_square + far_square))
-        ref[channels:, :] = stats
-
-
-def loss_kernel(count, merged, width, *refs):
-    part_refs = refs[:count]
-    slope_ref, offset_ref, share_ref, out_ref = refs[count:]
-    sources, channels = slope_ref.shape[:2]
+def loss_kernel(sources, width, *refs):
+    part_refs = refs[:sources]
+    slope_ref, offset_ref, share_ref, out_ref = refs[sources:]
+    channels = slope_ref.shape[1]
     clips = share_ref.shape[0]
     projected, sums, squares = [], [], []
     for ref in part_refs:
-        part = ref[...].astype(F32)
-        if merged:
-            projected.append(part[:channels])
-            sums += [part[channels : channels + 1], part[channels + 1 : channels + 2]]
-            squares.append(part[channels + 2 : channels + 3])
-        else:
-            for place, value in zip((projected, sums, squares), read_part(part, channels)):
-                place.append(value)
+        for place, value in zip((projected, sums, squares), read_part(ref[...].astype(F32), channels)):
+            place.append(value)
     center = sum(sums[1:], sums[0]) * (1.0 / width)
     spread = sum(squares[1:], squares[0]) * (1.0 / width) - center * center
     total = sum(projected[1:], projected[0])
@@ -391,26 +368,18 @@
         [pltpu.VMEM((group_rows, local), BF16)] * 2, scalars=[info],
     )
 
-    def mix(place, tiles=1, dtype=BF16):
-        return call(
-            functools.partial(mix_kernel, sources, reach, place), "mix",
+    parts = []
+    for k in reversed(range(sources)):
+        (part,) = call(
+            functools.partial(mix_kernel, sources, reach, k), "mix",
             [*near_blocks, *v_blocks, weights, base, scale_tok, weight_local],
-            [((channels + STAT_ROWS, tiles * tok_dev), dtype)],
+            [((channels + STAT_ROWS, tok_dev), BF16)],
             [pltpu.VMEM((group_rows, local), BF16)], flops=4 * tok_dev * reach[1] * local, traffic=2**20,
-        )[0]
-
-    if sources == 4:
-        arrived = onward(mix(lambda rank: (rank ^ 2) // 2 * 2, 2), 2)
-        keep, send = call(
-            merge_kernel, "merge", [mix(lambda rank: rank // 2 * 2, 2, F32), arrived],
-            [((channels + MERGED_ROWS, tok_dev), F32)] * 2,
         )
-        parts = [keep, onward(send, 1)]
-    else:
-        parts = [onward(mix(lambda rank, k=k: partner(rank, k, sources)), k) for k in reversed(range(sources))]
+        parts.append(onward(part, k))
 
     (shares,) = call(
-        functools.partial(loss_kernel, len(parts), sources == 4, width), "loss", [*parts, slope, offset, share],
+        functools.partial(loss_kernel, sources, width), "loss", [*parts, slope, offset, share],
         [((groups * sources, 1, HEAD_DIM), F32)],
     )
     everyone = lax.all_to_all(shares, ("dp", "seq"), split_axis=0, concat_axis=0, tiled=True)

time: 61.7 us -> 60.7 us (0.984)
  starting transfers between devices: 18.1 us -> 17.2 us
  Pallas kernels: 25.4 us -> 26.1 us
    ppermute x9 -> x10, starting transfers between devices: 18.1 us -> 17.2 us  [onward(): lax.ppermute(x, 'seq', [(i, partner(i, k, sources)) for i in range(source...]
    pallas_call x9 -> x10, Pallas kernels: 25.4 us -> 26.1 us  [call(): pl.pallas_call(kernel, in_specs=[smem()] * len(scalars) + [hbm() if i in...]
    ppermute x9 -> x10, waiting for transfers between devices: 4.9 us -> 4.38 us  [onward(): lax.ppermute(x, 'seq', [(i, partner(i, k, sources)) for i in range(source...]
  transfers between devices with their start and end apart: 9 -> 10, of which waited for: 3 -> 3; matrix products, arithmetic and copies ran while one was open for 0% -> 0% of each run, Pallas kernels for 38% -> 40%
where the time goes in v7:
time: 60.7 us; the launch traced here: 60.5 us
  Pallas kernels  26.1 us (43%)
  starting transfers between devices  17.2 us (28%)
  blocking collectives  11.6 us (19%)
  waiting for transfers between devices  4.38 us (7%)
  other arithmetic  0.92 us (2%)
    pallas_call x10, Pallas kernels, call(): pl.pallas_call(kernel, in_specs=[smem()] * len(scalars) + [hbm() if i in...  26.1 us
    ppermute x10, starting transfers between devices, onward(): lax.ppermute(x, 'seq', [(i, partner(i, k, sources)) for i in range(source...  17.2 us
    all_to_all x1, blocking collectives, per_device(): lax.all_to_all(shares, ('dp', 'seq'), split_axis=0, concat_axis=0, tiled=...  11.6 us
    ppermute x10, waiting for transfers between devices, onward(): lax.ppermute(x, 'seq', [(i, partner(i, k, sources)) for i in range(source...  4.38 us
  transfers between devices with their start and end apart: 10, of which 3 were waited for; matrix products, arithmetic and copies ran while one was open for 0% of the time, Pallas kernels for 40%

profile of v7, /device:TPU:0, one launch (start us, length us, event | category | flops | bytes accessed | tf_op | source)
XLA Modules:
  0.0 60.5 jit_solution(12748820092634022661)
XLA Ops:
  0.0 1.0 %cut_first.1 = (bf16[1,128,512]{2,1,0:T(8,128)(2,1)S(1)}, bf16[1,128,512]{2,1,0:T(8,128)(2,1)S(1)}) custom-call(bf16[128,2048]{1,0:T(8,128)(2,1)} %refs_0_.3), custom_call_target="tpu_custom_call" | custom-call | bytes 524288 | tf_op jit(solution)/shard_map/cut_first/pallas_call | solution.py:280
  1.0 5.1 %collective-permute-start.4 = (bf16[1,128,512]{2,1,0:T(8,128)(2,1)S(1)}, bf16[1,128,512]{2,1,0:T(8,128)(2,1)S(1)}, u32[]{:S(2)}, u32[]{:S(2)}) collective-permute-start(bf16[1,128,512]{2,1,0:T(8,128)(2,1)S(1)} %get-tuple-element.37), channel_id=1, source_target_pairs={{0,3},{1,2},{2,1},{3,0},{4,7},{5,6},{6,5},{7,4},{8,11},{9,10},{10,... | collective-permute-start | bytes 393224 | tf_op jit(solution)/shard_map/ppermute | solution.py:322
  6.2 0.0 collective-permute-start.3
  6.2 1.5 %cut_rest.1 = (bf16[3,128,512]{2,1,0:T(8,128)(2,1)S(1)}, bf16[3,128,512]{2,1,0:T(8,128)(2,1)S(1)}, bf16[1,128,512]{2,1,0:T(8,128)(2,1)S(1)}, bf16[1,128,512]{2,1...) custom-call(bf16[128,2048]{1,0:T(8,128)(2,1)} %refs_0_.3, ...), custom_call_target="tpu_custom_call" | custom-call | bytes 2621440 | tf_op jit(solution)/shard_map/cut_rest/pallas_call | solution.py:280
  7.6 3.0 %collective-permute-start.5 = (bf16[1,128,512]{2,1,0:T(8,128)(2,1)S(1)}, bf16[1,128,512]{2,1,0:T(8,128)(2,1)S(1)}, u32[]{:S(2)}, u32[]{:S(2)}) collective-permute-start(bf16[1,128,512]{2,1,0:T(8,128)(2,1)S(1)} %get-tuple-element.38), channel_id=1, source_target_pairs={{0,2},{1,3},{2,0},{3,1},{4,6},{5,7},{6,4},{7,5},{8,10},{9,11},{10,... | collective-permute-start | bytes 393224 | tf_op jit(solution)/shard_map/ppermute | solution.py:322
  10.6 0.1 collective-permute-start.6
  10.7 0.6 collective-permute-start
  11.3 0.1 multiply_cosine_fusion
  11.4 0.1 pad_add_fusion.info_ref
  11.5 14.1 %prep.1 = (f32[512,512]{1,0:T(8,128)S(1)}, f32[4,64,128]{2,1,0:T(8,128)S(1)}, f32[64,128]{1,0:T(8,128)S(1)}, f32[8,128]{1,0:T(8,128)S(1)}, bf16[64,512]{1,0:T(8,...) custom-call(s32[16]{0:T(128)S(1)} %pad_add_fusion.info_ref, ...), custom_call_target="tpu_custom_call" | custom-call | tf_op jit(solution)/shard_map/prep/pallas_call | solution.py:280
  25.6 0.0 collective-permute-done.4.refs_3_
  25.6 3.8 %collective-permute-start.1 = (bf16[1,128,512]{2,1,0:T(8,128)(2,1)S(1)}, bf16[1,128,512]{2,1,0:T(8,128)(2,1)S(1)}, u32[]{:S(2)}, u32[]{:S(2)}) collective-permute-start(bf16[1,128,512]{2,1,0:T(8,128)(2,1)S(1)} %get-tuple-element.35), channel_id=1, source_target_pairs={{0,2},{1,3},{2,0},{3,1},{4,6},{5,7},{6,4},{7,5},{8,10},{9,11},{10,... | collective-permute-start | bytes 393224 | tf_op jit(solution)/shard_map/ppermute | solution.py:322
  29.4 0.0 collective-permute-done.3.refs_2_
  29.4 0.1 collective-permute-start.2
  29.5 4.5 %text.1 = (f32[656,512]{1,0:T(8,128)S(1)}, f32[4,656,128]{2,1,0:T(8,128)S(1)}) custom-call(s32[16]{0:T(128)S(1)} %pad_add_fusion.info_ref, bf16[3,128,512]{2,1,0:T(8,128)(2,1)S(1)} %get-tuple-element.30.refs_0_, bf16[3,128,512]{2,1,0:T(8,128)(2,1)S(1)} %collective-permute-done.refs_1_, bf16[1,128,512]{2,1,0:T(8,128)(2,1)S(1)} %collective-permute-done.3.refs_2_, ...), custom_call_target="tpu_custom_call" | custom-call | tf_op jit(solution)/shard_map/text/pallas_call | solution.py:280
  34.0 0.0 collective-permute-done.6.refs_5_
  34.0 2.3 %weigh.1 = (bf16[4,512,384]{2,1,0:T(8,128)(2,1)S(1)}, f32[512,512]{1,0:T(8,128)S(1)}) custom-call(s32[16]{0:T(128)S(1)} %pad_add_fusion.info_ref, bf16[3,128,512]{2,1,0:T(8,128)(2,1)S(1)} %get-tuple-element.30.refs_0_, bf16[3,128,512]{2,1,0:T(8,128)(2,1)S(1)} %collective-permute-done.refs_1_, bf16[1,128,512]{2,1,0:T(8,128)(2,1)S(1)} %collective-permute-done.3.refs_2_, ...), custom_call_target="tpu_custom_call" | custom-call | tf_op jit(solution)/shard_map/weigh/pallas_call | solution.py:280
  36.3 1.7 %collective-permute-done.1.refs_2_ = bf16[1,128,512]{2,1,0:T(8,128)(2,1)S(1)} collective-permute-done((bf16[1,128,512]{2,1,0:T(8,128)(2,1)S(1)}, bf16[1,128,512]{2,1,0:T(8,128)(2,1)S(1)}, u32[]{:S(2)}, u32[]{:S(2)}) %collective-permute-start.1) | collective-permute-done | bytes 131104 | tf_op jit(solution)/shard_map/ppermute | solution.py:322
  38.0 0.7 %mix.4 = bf16[80,128]{1,0:T(8,128)(2,1)S(1)} custom-call(bf16[3,128,512]{2,1,0:T(8,128)(2,1)S(1)} %get-tuple-element.30.refs_0_, bf16[3,128,512]{2,1,0:T(8,128)(2,1)S(1)} %collective-permute-done.refs_1_, bf16[1,128,512]{2,1,0:T(8,128)(2,1)S(1)} %collective-permute-done.1.refs_2_, bf16[1,128,512]{2,1,0:T(8,128)(2,1)S(1)} %collective-permute-done.2.refs_3_, ...), custom_call_target="tpu_custom_call" | custom-call | flops 100663296 | bytes 1048576 | tf_op jit(solution)/shard_map/mix/pallas_call | solution.py:280
  38.7 2.9 %collective-permute-start.7 = (bf16[80,128]{1,0:T(8,128)(2,1)S(1)}, bf16[80,128]{1,0:T(8,128)(2,1)S(1)}, u32[]{:S(2)}, u32[]{:S(2)}) collective-permute-start(bf16[80,128]{1,0:T(8,128)(2,1)S(1)} %mix.4), channel_id=1, source_target_pairs={{0,3},{1,2},{2,1},{3,0},{4,7},{5,6},{6,5},{7,4},{8,11},{9,10},{10,... | collective-permute-start | bytes 61448 | tf_op jit(solution)/shard_map/ppermute | solution.py:322
  41.5 0.7 %mix.5 = bf16[80,128]{1,0:T(8,128)(2,1)S(1)} custom-call(bf16[3,128,512]{2,1,0:T(8,128)(2,1)S(1)} %get-tuple-element.30.refs_0_, bf16[3,128,512]{2,1,0:T(8,128)(2,1)S(1)} %collective-permute-done.refs_1_, bf16[1,128,512]{2,1,0:T(8,128)(2,1)S(1)} %collective-permute-done.1.refs_2_, bf16[1,128,512]{2,1,0:T(8,128)(2,1)S(1)} %collective-permute-done.2.refs_3_, ...), custom_call_target="tpu_custom_call" | custom-call | flops 100663296 | bytes 1048576 | tf_op jit(solution)/shard_map/mix/pallas_call | solution.py:280
  42.2 1.2 %collective-permute-start.8 = (bf16[80,128]{1,0:T(8,128)(2,1)S(1)}, bf16[80,128]{1,0:T(8,128)(2,1)S(1)}, u32[]{:S(2)}, u32[]{:S(2)}) collective-permute-start(bf16[80,128]{1,0:T(8,128)(2,1)S(1)} %mix.5), channel_id=1, source_target_pairs={{0,2},{1,3},{2,0},{3,1},{4,6},{5,7},{6,4},{7,5},{8,10},{9,11},{10,... | collective-permute-start | bytes 61448 | tf_op jit(solution)/shard_map/ppermute | solution.py:322
  43.4 0.7 %mix.6 = bf16[80,128]{1,0:T(8,128)(2,1)S(1)} custom-call(bf16[3,128,512]{2,1,0:T(8,128)(2,1)S(1)} %get-tuple-element.30.refs_0_, bf16[3,128,512]{2,1,0:T(8,128)(2,1)S(1)} %collective-permute-done.refs_1_, bf16[1,128,512]{2,1,0:T(8,128)(2,1)S(1)} %collective-permute-done.1.refs_2_, bf16[1,128,512]{2,1,0:T(8,128)(2,1)S(1)} %collective-permute-done.2.refs_3_, ...), custom_call_target="tpu_custom_call" | custom-call | flops 100663296 | bytes 1048576 | tf_op jit(solution)/shard_map/mix/pallas_call | solution.py:280
  44.1 0.0 copy-start.3
  44.1 0.5 collective-permute-start.9
  44.6 0.7 %mix.7.refs_3_ = bf16[80,128]{1,0:T(8,128)(2,1)S(1)} custom-call(bf16[3,128,512]{2,1,0:T(8,128)(2,1)S(1)} %get-tuple-element.30.refs_0_, bf16[3,128,512]{2,1,0:T(8,128)(2,1)S(1)} %collective-permute-done.refs_1_, bf16[1,128,512]{2,1,0:T(8,128)(2,1)S(1)} %collective-permute-done.1.refs_2_, bf16[1,128,512]{2,1,0:T(8,128)(2,1)S(1)} %collective-permute-done.2.refs_3_, ...), custom_call_target="tpu_custom_call" | custom-call | flops 100663296 | bytes 1048576 | tf_op jit(solution)/shard_map/mix/pallas_call | solution.py:280
  45.3 1.7 %collective-permute-done.8.refs_1_ = bf16[80,128]{1,0:T(8,128)(2,1)S(1)} collective-permute-done((bf16[80,128]{1,0:T(8,128)(2,1)S(1)}, bf16[80,128]{1,0:T(8,128)(2,1)S(1)}, u32[]{:S(2)}, u32[]{:S(2)}) %collective-permute-start.8) | collective-permute-done | bytes 20512 | tf_op jit(solution)/shard_map/ppermute | solution.py:322
  47.0 1.0 %collective-permute-done.9.refs_2_ = bf16[80,128]{1,0:T(8,128)(2,1)S(1)} collective-permute-done((bf16[80,128]{1,0:T(8,128)(2,1)S(1)}, bf16[80,128]{1,0:T(8,128)(2,1)S(1)}, u32[]{:S(2)}, u32[]{:S(2)}) %collective-permute-start.9) | collective-permute-done | bytes 20512 | tf_op jit(solution)/shard_map/ppermute | solution.py:322
  47.9 0.1 loss.1
  48.1 11.6 %all_to_all.5 = f32[32,1,128]{2,1,0:T(1,128)S(1)} all-to-all(f32[32,1,128]{2,1,0:T(1,128)S(1)} %loss.1), channel_id=1, replica_groups=mesh['dp'=8,'seq'=4] {'dp','seq'}, dimensions={0} | all-to-all | bytes 32768 | tf_op jit(solution)/shard_map/all_to_all | solution.py:385
  59.7 0.1 broadcast_in_dim.18
  59.8 0.7 %select_reduce_fusion = f32[8]{0:T(128)} fusion(f32[64]{0:T(128)S(1)} %broadcast_in_dim.18, s32[8]{0:T(128)S(1)} %copy-done.3), kind=kLoop, calls=%fused_computation.4 | loop fusion | flops 1528 | bytes 320 | tf_op jit(solution)/shard_map/reduce_sum | solution.py:388
  (15 shorter events, 0.1 us)
Async XLA Ops:
  0.0 11.3 %copy-start = (s32[8]{0:T(128)S(1)}, s32[8]{0:T(128)}, u32[]{:S(2)}) copy-start(s32[8]{0:T(128)} %param.18) | copy-start | bytes 100
  0.0 11.4 %copy-start.2 = (s32[1,8]{1,0:T(1,128)S(1)}, s32[1,8]{1,0:T(1,128)}, u32[]{:S(2)}) copy-start(s32[1,8]{1,0:T(1,128)} %param.17) | copy-start | bytes 100
  0.0 11.4 %copy-start.1 = (s32[8]{0:T(128)S(1)}, s32[8]{0:T(128)}, u32[]{:S(2)}) copy-start(s32[8]{0:T(128)} %param.16) | copy-start | bytes 100
  1.0 24.5 %collective-permute-start.4 = (bf16[1,128,512]{2,1,0:T(8,128)(2,1)S(1)}, bf16[1,128,512]{2,1,0:T(8,128)(2,1)S(1)}, u32[]{:S(2)}, u32[]{:S(2)}) collective-permute-start(bf16[1,128,512]{2,1,0:T(8,128)(2,1)S(1)} %get-tuple-element.37), channel_id=1, source_target_pairs={{0,3},{1,2},{2,1},{3,0},{4,7},{5,6},{6,5},{7,4},{8,11},{9,10},{10,... | collective-permute-start | bytes 393224 | tf_op jit(solution)/shard_map/ppermute | solution.py:322
  6.2 23.2 %collective-permute-start.3 = (bf16[1,128,512]{2,1,0:T(8,128)(2,1)S(1)}, bf16[1,128,512]{2,1,0:T(8,128)(2,1)S(1)}, u32[]{:S(2)}, u32[]{:S(2)}) collective-permute-start(bf16[1,128,512]{2,1,0:T(8,128)(2,1)S(1)} %get-tuple-element.28), channel_id=1, source_target_pairs={{0,2},{1,3},{2,0},{3,1},{4,6},{5,7},{6,4},{7,5},{8,10},{9,11},{10,... | collective-permute-start | bytes 393224 | tf_op jit(solution)/shard_map/ppermute | solution.py:322
  7.6 26.3 %collective-permute-start.5 = (bf16[1,128,512]{2,1,0:T(8,128)(2,1)S(1)}, bf16[1,128,512]{2,1,0:T(8,128)(2,1)S(1)}, u32[]{:S(2)}, u32[]{:S(2)}) collective-permute-start(bf16[1,128,512]{2,1,0:T(8,128)(2,1)S(1)} %get-tuple-element.38), channel_id=1, source_target_pairs={{0,2},{1,3},{2,0},{3,1},{4,6},{5,7},{6,4},{7,5},{8,10},{9,11},{10,... | collective-permute-start | bytes 393224 | tf_op jit(solution)/shard_map/ppermute | solution.py:322
  10.6 23.4 %collective-permute-start.6 = (bf16[1,128,512]{2,1,0:T(8,128)(2,1)S(1)}, bf16[1,128,512]{2,1,0:T(8,128)(2,1)S(1)}, u32[]{:S(2)}, u32[]{:S(2)}) collective-permute-start(bf16[1,128,512]{2,1,0:T(8,128)(2,1)S(1)} %get-tuple-element.39), channel_id=1, source_target_pairs={{0,3},{1,2},{2,1},{3,0},{4,7},{5,6},{6,5},{7,4},{8,11},{9,10},{10,... | collective-permute-start | bytes 393224 | tf_op jit(solution)/shard_map/ppermute | solution.py:322
  10.7 18.8 %collective-permute-start = (bf16[3,128,512]{2,1,0:T(8,128)(2,1)S(1)}, bf16[3,128,512]{2,1,0:T(8,128)(2,1)S(1)}, u32[]{:S(2)}, u32[]{:S(2)}) collective-permute-start(bf16[3,128,512]{2,1,0:T(8,128)(2,1)S(1)} %get-tuple-element.31), channel_id=1, source_target_pairs={{0,1},{1,0},{2,3},{3,2},{4,5},{5,4},{6,7},{7,6},{8,9},{9,8},{10,11... | collective-permute-start | bytes 1179656 | tf_op jit(solution)/shard_map/ppermute | solution.py:322
  25.6 12.4 %collective-permute-start.1 = (bf16[1,128,512]{2,1,0:T(8,128)(2,1)S(1)}, bf16[1,128,512]{2,1,0:T(8,128)(2,1)S(1)}, u32[]{:S(2)}, u32[]{:S(2)}) collective-permute-start(bf16[1,128,512]{2,1,0:T(8,128)(2,1)S(1)} %get-tuple-element.35), channel_id=1, source_target_pairs={{0,2},{1,3},{2,0},{3,1},{4,6},{5,7},{6,4},{7,5},{8,10},{9,11},{10,... | collective-permute-start | bytes 393224 | tf_op jit(solution)/shard_map/ppermute | solution.py:322
  29.4 8.6 %collective-permute-start.2 = (bf16[1,128,512]{2,1,0:T(8,128)(2,1)S(1)}, bf16[1,128,512]{2,1,0:T(8,128)(2,1)S(1)}, u32[]{:S(2)}, u32[]{:S(2)}) collective-permute-start(bf16[1,128,512]{2,1,0:T(8,128)(2,1)S(1)} %get-tuple-element.36), channel_id=1, source_target_pairs={{0,3},{1,2},{2,1},{3,0},{4,7},{5,6},{6,5},{7,4},{8,11},{9,10},{10,... | collective-permute-start | bytes 393224 | tf_op jit(solution)/shard_map/ppermute | solution.py:322
  38.7 6.6 %collective-permute-start.7 = (bf16[80,128]{1,0:T(8,128)(2,1)S(1)}, bf16[80,128]{1,0:T(8,128)(2,1)S(1)}, u32[]{:S(2)}, u32[]{:S(2)}) collective-permute-start(bf16[80,128]{1,0:T(8,128)(2,1)S(1)} %mix.4), channel_id=1, source_target_pairs={{0,3},{1,2},{2,1},{3,0},{4,7},{5,6},{6,5},{7,4},{8,11},{9,10},{10,... | collective-permute-start | bytes 61448 | tf_op jit(solution)/shard_map/ppermute | solution.py:322
  42.2 4.7 %collective-permute-start.8 = (bf16[80,128]{1,0:T(8,128)(2,1)S(1)}, bf16[80,128]{1,0:T(8,128)(2,1)S(1)}, u32[]{:S(2)}, u32[]{:S(2)}) collective-permute-start(bf16[80,128]{1,0:T(8,128)(2,1)S(1)} %mix.5), channel_id=1, source_target_pairs={{0,2},{1,3},{2,0},{3,1},{4,6},{5,7},{6,4},{7,5},{8,10},{9,11},{10,... | collective-permute-start | bytes 61448 | tf_op jit(solution)/shard_map/ppermute | solution.py:322
  44.1 15.7 %copy-start.3 = (s32[8]{0:T(128)S(1)}, s32[8]{0:T(128)}, u32[]{:S(2)}) copy-start(s32[8]{0:T(128)} %param.23) | copy-start | bytes 100
  44.1 3.8 %collective-permute-start.9 = (bf16[80,128]{1,0:T(8,128)(2,1)S(1)}, bf16[80,128]{1,0:T(8,128)(2,1)S(1)}, u32[]{:S(2)}, u32[]{:S(2)}) collective-permute-start(bf16[80,128]{1,0:T(8,128)(2,1)S(1)} %mix.6), channel_id=1, source_target_pairs={{0,1},{1,0},{2,3},{3,2},{4,5},{5,4},{6,7},{7,6},{8,9},{9,8},{10,11... | collective-permute-start | bytes 61448 | tf_op jit(solution)/shard_map/ppermute | solution.py:322

commit v8 on v7

--- a/solution.py
+++ b/solution.py
@@ -24,11 +24,6 @@
 
 def nt_dot(a, b, precision=None):
     return lax.dot_general(a, b, (((1,), (1,)), ((), ())), precision=precision, preferred_element_type=F32)
-
-
-def two_parts(x):
-    high = x.astype(BF16)
-    return high, (x - high.astype(F32)).astype(BF16)
 
 
 def head_cols(h):
@@ -221,19 +216,18 @@
     attended = jnp.concatenate([(mixed[h] + base_ref[rows, head_cols(h)]).astype(BF16) for h in range(heads)], axis=1)
     attended_full = attended.astype(F32)
     local_mean = jnp.sum(attended_full, axis=1, keepdims=True) * (1.0 / local)
-    y_high, y_low = two_parts((attended_full - local_mean) * scale_ref[rows, :])
-    s_high, s_low = two_parts(attended_full * attended_full)
+    centred = attended_full - local_mean
     weight = wt_ref[...]
     every = jnp.ones((STAT_ROWS, local), BF16)
-    out_ref[:channels, :] = (nt_dot(weight, y_high) + nt_dot(weight, y_low)).astype(out_ref.dtype)
+    out_ref[:channels, :] = nt_dot(weight, (centred * scale_ref[rows, :]).astype(BF16)).astype(BF16)
     row = lax.broadcasted_iota(jnp.int32, (STAT_ROWS, count), 0)
-    rest = jnp.where(row < 3, nt_dot(every, attended), nt_dot(every, s_high) + nt_dot(every, s_low))
+    rest = jnp.where(row < 3, nt_dot(every, attended), nt_dot(every, (centred * centred).astype(BF16)))
     terms = jnp.zeros((STAT_ROWS, count), F32)
     for place in range(3):
-        term = rest.astype(out_ref.dtype).astype(F32)
+        term = rest.astype(BF16).astype(F32)
         terms = jnp.where((row == place) | (row == place + 3), term, terms)
         rest = rest - term
-    out_ref[channels:, :] = terms.astype(out_ref.dtype)
+    out_ref[channels:, :] = terms.astype(BF16)
 
 
 def read_part(part, channels):
@@ -251,10 +245,11 @@
         for place, value in zip((projected, sums, squares), read_part(ref[...].astype(F32), channels)):
             place.append(value)
     center = sum(sums[1:], sums[0]) * (1.0 / width)
-    spread = sum(squares[1:], squares[0]) * (1.0 / width) - center * center
+    strays = [value * (sources / width) - center for value in sums]
+    spread = sum(squares[1:], squares[0]) * (1.0 / width) + sum(stray * stray for stray in strays) * (1.0 / sources)
     total = sum(projected[1:], projected[0])
     for place in range(sources):
-        total = total + (sums[place] * (sources / width) - center) * slope_ref[place]
+        total = total + strays[place] * slope_ref[place]
     diff = total * lax.rsqrt(spread + EPS) + offset_ref[...]
     error = jnp.sum(diff * diff, axis=0, keepdims=True) * (1.0 / channels)
     sums = jnp.sum(share_ref[...] * error, axis=1, keepdims=True)
@@ -262,6 +257,16 @@
     mine = lanes == lax.broadcasted_iota(jnp.int32, lanes.shape, 0)
     row = jnp.sum(jnp.where(mine, sums, 0.0), axis=0, keepdims=True)
     out_ref[...] = jnp.broadcast_to(row[None], out_ref.shape)
+
+
+def pick_kernel(clips, losses_ref, order_ref, out_ref):
+    losses = jnp.sum(losses_ref[...], axis=1)
+    order = order_ref[...]
+    column = lax.broadcasted_iota(jnp.int32, (losses.shape[1], order.shape[1]), 0)
+    chosen = (column == lax.rem(order, clips)).astype(F32)
+    by_group = jnp.dot(losses, chosen, precision=EXACT, preferred_element_type=F32)
+    group = lax.broadcasted_iota(jnp.int32, by_group.shape, 0)
+    out_ref[...] = jnp.sum(jnp.where(group == lax.div(order, clips), by_group, 0.0), axis=0, keepdims=True)
 
 
 def smem():
@@ -383,9 +388,12 @@
         [((groups * sources, 1, HEAD_DIM), F32)],
     )
     everyone = lax.all_to_all(shares, ("dp", "seq"), split_axis=0, concat_axis=0, tiled=True)
-    losses = jnp.sum(everyone.reshape(groups, sources, HEAD_DIM), axis=1)[:, :clips].reshape(1, -1)
-    slots = jnp.arange(groups * clips, dtype=jnp.int32)
-    return jnp.sum(jnp.where(report_order[:, None] == slots[None, :], losses, 0.0), axis=1)
+    (scores,) = call(
+        functools.partial(pick_kernel, clips), "pick",
+        [everyone.reshape(groups, sources, HEAD_DIM), report_order.reshape(1, -1)],
+        [((1, report_order.shape[0]), F32)], pinned=False,
+    )
+    return scores.reshape(-1)
 
 
 def solution(mesh):

time: 60.7 us -> 60.4 us (level)
  other arithmetic: 0.92 us -> 0.21 us
  Pallas kernels: 26.1 us -> 26.8 us
    reduce_sum x2 -> x0, other arithmetic: 0.71 us -> none  [the longest x1 0.7 us: per_device(): jnp.sum(jnp.where(report_order[:, None] == slots[None, :], losses, 0.0),...]
    pallas_call x10 -> x11, Pallas kernels: 26.1 us -> 26.8 us  [call(): pl.pallas_call(kernel, in_specs=[smem()] * len(scalars) + [hbm() if i in...]
where the time goes in v8:
time: 60.4 us; the launch traced here: 60.2 us
  Pallas kernels  26.8 us (44%)
  starting transfers between devices  17.1 us (28%)
  blocking collectives  11.6 us (19%)
  waiting for transfers between devices  4.4 us (7%)
    pallas_call x11, Pallas kernels, call(): pl.pallas_call(kernel, in_specs=[smem()] * len(scalars) + [hbm() if i in...  26.8 us
    ppermute x10, starting transfers between devices, onward(): lax.ppermute(x, 'seq', [(i, partner(i, k, sources)) for i in range(source...  17.1 us
    all_to_all x1, blocking collectives, per_device(): lax.all_to_all(shares, ('dp', 'seq'), split_axis=0, concat_axis=0, tiled=...  11.6 us
    ppermute x10, waiting for transfers between devices, onward(): lax.ppermute(x, 'seq', [(i, partner(i, k, sources)) for i in range(source...  4.4 us
  transfers between devices with their start and end apart: 10, of which 3 were waited for; matrix products, arithmetic and copies ran while one was open for 0% of the time, Pallas kernels for 40%

profile of v8, /device:TPU:0, one launch (start us, length us, event | category | flops | bytes accessed | tf_op | source)
XLA Modules:
  0.0 60.2 jit_solution(12734888034425808972)
XLA Ops:
  0.0 1.0 %cut_first.1 = (bf16[1,128,512]{2,1,0:T(8,128)(2,1)S(1)}, bf16[1,128,512]{2,1,0:T(8,128)(2,1)S(1)}) custom-call(bf16[128,2048]{1,0:T(8,128)(2,1)} %refs_0_.3), custom_call_target="tpu_custom_call" | custom-call | bytes 524288 | tf_op jit(solution)/shard_map/cut_first/pallas_call | solution.py:285
  1.0 5.1 %collective-permute-start.4 = (bf16[1,128,512]{2,1,0:T(8,128)(2,1)S(1)}, bf16[1,128,512]{2,1,0:T(8,128)(2,1)S(1)}, u32[]{:S(2)}, u32[]{:S(2)}) collective-permute-start(bf16[1,128,512]{2,1,0:T(8,128)(2,1)S(1)} %get-tuple-element.37), channel_id=1, source_target_pairs={{0,3},{1,2},{2,1},{3,0},{4,7},{5,6},{6,5},{7,4},{8,11},{9,10},{10,... | collective-permute-start | bytes 393224 | tf_op jit(solution)/shard_map/ppermute | solution.py:327
  6.2 0.0 collective-permute-start.3
  6.2 1.5 %cut_rest.1 = (bf16[3,128,512]{2,1,0:T(8,128)(2,1)S(1)}, bf16[3,128,512]{2,1,0:T(8,128)(2,1)S(1)}, bf16[1,128,512]{2,1,0:T(8,128)(2,1)S(1)}, bf16[1,128,512]{2,1...) custom-call(bf16[128,2048]{1,0:T(8,128)(2,1)} %refs_0_.3, ...), custom_call_target="tpu_custom_call" | custom-call | bytes 2621440 | tf_op jit(solution)/shard_map/cut_rest/pallas_call | solution.py:285
  7.6 3.0 %collective-permute-start.5 = (bf16[1,128,512]{2,1,0:T(8,128)(2,1)S(1)}, bf16[1,128,512]{2,1,0:T(8,128)(2,1)S(1)}, u32[]{:S(2)}, u32[]{:S(2)}) collective-permute-start(bf16[1,128,512]{2,1,0:T(8,128)(2,1)S(1)} %get-tuple-element.38), channel_id=1, source_target_pairs={{0,2},{1,3},{2,0},{3,1},{4,6},{5,7},{6,4},{7,5},{8,10},{9,11},{10,... | collective-permute-start | bytes 393224 | tf_op jit(solution)/shard_map/ppermute | solution.py:327
  10.6 0.1 collective-permute-start.6
  10.7 0.6 collective-permute-start
  11.3 0.1 multiply_cosine_fusion
  11.4 0.1 pad_add_fusion.info_ref
  11.5 14.1 %prep.1 = (f32[512,512]{1,0:T(8,128)S(1)}, f32[4,64,128]{2,1,0:T(8,128)S(1)}, f32[64,128]{1,0:T(8,128)S(1)}, f32[8,128]{1,0:T(8,128)S(1)}, bf16[64,512]{1,0:T(8,...) custom-call(s32[16]{0:T(128)S(1)} %pad_add_fusion.info_ref, ...), custom_call_target="tpu_custom_call" | custom-call | tf_op jit(solution)/shard_map/prep/pallas_call | solution.py:285
  25.6 0.0 collective-permute-done.4.refs_3_
  25.6 3.8 %collective-permute-start.1 = (bf16[1,128,512]{2,1,0:T(8,128)(2,1)S(1)}, bf16[1,128,512]{2,1,0:T(8,128)(2,1)S(1)}, u32[]{:S(2)}, u32[]{:S(2)}) collective-permute-start(bf16[1,128,512]{2,1,0:T(8,128)(2,1)S(1)} %get-tuple-element.35), channel_id=1, source_target_pairs={{0,2},{1,3},{2,0},{3,1},{4,6},{5,7},{6,4},{7,5},{8,10},{9,11},{10,... | collective-permute-start | bytes 393224 | tf_op jit(solution)/shard_map/ppermute | solution.py:327
  29.4 0.0 collective-permute-done.3.refs_2_
  29.4 0.1 collective-permute-start.2
  29.5 0.0 collective-permute-done.refs_1_
  29.5 4.5 %text.1 = (f32[656,512]{1,0:T(8,128)S(1)}, f32[4,656,128]{2,1,0:T(8,128)S(1)}) custom-call(s32[16]{0:T(128)S(1)} %pad_add_fusion.info_ref, bf16[3,128,512]{2,1,0:T(8,128)(2,1)S(1)} %get-tuple-element.30.refs_0_, bf16[3,128,512]{2,1,0:T(8,128)(2,1)S(1)} %collective-permute-done.refs_1_, bf16[1,128,512]{2,1,0:T(8,128)(2,1)S(1)} %collective-permute-done.3.refs_2_, ...), custom_call_target="tpu_custom_call" | custom-call | tf_op jit(solution)/shard_map/text/pallas_call | solution.py:285
  34.0 0.0 collective-permute-done.6.refs_5_
  34.0 2.3 %weigh.1 = (bf16[4,512,384]{2,1,0:T(8,128)(2,1)S(1)}, f32[512,512]{1,0:T(8,128)S(1)}) custom-call(s32[16]{0:T(128)S(1)} %pad_add_fusion.info_ref, bf16[3,128,512]{2,1,0:T(8,128)(2,1)S(1)} %get-tuple-element.30.refs_0_, bf16[3,128,512]{2,1,0:T(8,128)(2,1)S(1)} %collective-permute-done.refs_1_, bf16[1,128,512]{2,1,0:T(8,128)(2,1)S(1)} %collective-permute-done.3.refs_2_, ...), custom_call_target="tpu_custom_call" | custom-call | tf_op jit(solution)/shard_map/weigh/pallas_call | solution.py:285
  36.3 1.7 %collective-permute-done.1.refs_2_ = bf16[1,128,512]{2,1,0:T(8,128)(2,1)S(1)} collective-permute-done((bf16[1,128,512]{2,1,0:T(8,128)(2,1)S(1)}, bf16[1,128,512]{2,1,0:T(8,128)(2,1)S(1)}, u32[]{:S(2)}, u32[]{:S(2)}) %collective-permute-start.1) | collective-permute-done | bytes 131104 | tf_op jit(solution)/shard_map/ppermute | solution.py:327
  38.0 0.7 %mix.4 = bf16[80,128]{1,0:T(8,128)(2,1)S(1)} custom-call(bf16[3,128,512]{2,1,0:T(8,128)(2,1)S(1)} %get-tuple-element.30.refs_0_, bf16[3,128,512]{2,1,0:T(8,128)(2,1)S(1)} %collective-permute-done.refs_1_, bf16[1,128,512]{2,1,0:T(8,128)(2,1)S(1)} %collective-permute-done.1.refs_2_, bf16[1,128,512]{2,1,0:T(8,128)(2,1)S(1)} %collective-permute-done.2.refs_3_, ...), custom_call_target="tpu_custom_call" | custom-call | flops 100663296 | bytes 1048576 | tf_op jit(solution)/shard_map/mix/pallas_call | solution.py:285
  38.7 2.8 %collective-permute-start.7 = (bf16[80,128]{1,0:T(8,128)(2,1)S(1)}, bf16[80,128]{1,0:T(8,128)(2,1)S(1)}, u32[]{:S(2)}, u32[]{:S(2)}) collective-permute-start(bf16[80,128]{1,0:T(8,128)(2,1)S(1)} %mix.4), channel_id=1, source_target_pairs={{0,3},{1,2},{2,1},{3,0},{4,7},{5,6},{6,5},{7,4},{8,11},{9,10},{10,... | collective-permute-start | bytes 61448 | tf_op jit(solution)/shard_map/ppermute | solution.py:327
  41.5 0.7 %mix.5 = bf16[80,128]{1,0:T(8,128)(2,1)S(1)} custom-call(bf16[3,128,512]{2,1,0:T(8,128)(2,1)S(1)} %get-tuple-element.30.refs_0_, bf16[3,128,512]{2,1,0:T(8,128)(2,1)S(1)} %collective-permute-done.refs_1_, bf16[1,128,512]{2,1,0:T(8,128)(2,1)S(1)} %collective-permute-done.1.refs_2_, bf16[1,128,512]{2,1,0:T(8,128)(2,1)S(1)} %collective-permute-done.2.refs_3_, ...), custom_call_target="tpu_custom_call" | custom-call | flops 100663296 | bytes 1048576 | tf_op jit(solution)/shard_map/mix/pallas_call | solution.py:285
  42.1 1.2 %collective-permute-start.8 = (bf16[80,128]{1,0:T(8,128)(2,1)S(1)}, bf16[80,128]{1,0:T(8,128)(2,1)S(1)}, u32[]{:S(2)}, u32[]{:S(2)}) collective-permute-start(bf16[80,128]{1,0:T(8,128)(2,1)S(1)} %mix.5), channel_id=1, source_target_pairs={{0,2},{1,3},{2,0},{3,1},{4,6},{5,7},{6,4},{7,5},{8,10},{9,11},{10,... | collective-permute-start | bytes 61448 | tf_op jit(solution)/shard_map/ppermute | solution.py:327
  43.3 0.7 %mix.6 = bf16[80,128]{1,0:T(8,128)(2,1)S(1)} custom-call(bf16[3,128,512]{2,1,0:T(8,128)(2,1)S(1)} %get-tuple-element.30.refs_0_, bf16[3,128,512]{2,1,0:T(8,128)(2,1)S(1)} %collective-permute-done.refs_1_, bf16[1,128,512]{2,1,0:T(8,128)(2,1)S(1)} %collective-permute-done.1.refs_2_, bf16[1,128,512]{2,1,0:T(8,128)(2,1)S(1)} %collective-permute-done.2.refs_3_, ...), custom_call_target="tpu_custom_call" | custom-call | flops 100663296 | bytes 1048576 | tf_op jit(solution)/shard_map/mix/pallas_call | solution.py:285
  43.9 0.5 collective-permute-start.9
  44.5 0.7 %mix.7.refs_3_ = bf16[80,128]{1,0:T(8,128)(2,1)S(1)} custom-call(bf16[3,128,512]{2,1,0:T(8,128)(2,1)S(1)} %get-tuple-element.30.refs_0_, bf16[3,128,512]{2,1,0:T(8,128)(2,1)S(1)} %collective-permute-done.refs_1_, bf16[1,128,512]{2,1,0:T(8,128)(2,1)S(1)} %collective-permute-done.1.refs_2_, bf16[1,128,512]{2,1,0:T(8,128)(2,1)S(1)} %collective-permute-done.2.refs_3_, ...), custom_call_target="tpu_custom_call" | custom-call | flops 100663296 | bytes 1048576 | tf_op jit(solution)/shard_map/mix/pallas_call | solution.py:285
  45.1 0.0 collective-permute-done.7.refs_0_
  45.1 1.7 %collective-permute-done.8.refs_1_ = bf16[80,128]{1,0:T(8,128)(2,1)S(1)} collective-permute-done((bf16[80,128]{1,0:T(8,128)(2,1)S(1)}, bf16[80,128]{1,0:T(8,128)(2,1)S(1)}, u32[]{:S(2)}, u32[]{:S(2)}) %collective-permute-start.8) | collective-permute-done | bytes 20512 | tf_op jit(solution)/shard_map/ppermute | solution.py:327
  46.8 0.9 %collective-permute-done.9.refs_2_ = bf16[80,128]{1,0:T(8,128)(2,1)S(1)} collective-permute-done((bf16[80,128]{1,0:T(8,128)(2,1)S(1)}, bf16[80,128]{1,0:T(8,128)(2,1)S(1)}, u32[]{:S(2)}, u32[]{:S(2)}) %collective-permute-start.9) | collective-permute-done | bytes 20512 | tf_op jit(solution)/shard_map/ppermute | solution.py:327
  47.8 0.1 loss.1
  47.9 11.6 %all_to_all.5 = f32[32,1,128]{2,1,0:T(1,128)S(1)} all-to-all(f32[32,1,128]{2,1,0:T(1,128)S(1)} %loss.1), channel_id=1, replica_groups=mesh['dp'=8,'seq'=4] {'dp','seq'}, dimensions={0} | all-to-all | bytes 32768 | tf_op jit(solution)/shard_map/all_to_all | solution.py:390
  59.5 0.7 %pick.1 = f32[1,8]{1,0:T(1,128)} custom-call(f32[8,4,128]{2,1,0:T(4,128)S(1)} %bitcast.7, s32[1,8]{1,0:T(1,128)S(1)} %bitcast.8), custom_call_target="tpu_custom_call" | custom-call | tf_op jit(solution)/shard_map/pick/pallas_call | solution.py:285
  (13 shorter events, 0.0 us)
Async XLA Ops:
  0.0 11.3 %copy-start.1 = (s32[8]{0:T(128)S(1)}, s32[8]{0:T(128)}, u32[]{:S(2)}) copy-start(s32[8]{0:T(128)} %param.18) | copy-start | bytes 100
  0.0 11.4 %copy-start.3 = (s32[1,8]{1,0:T(1,128)S(1)}, s32[1,8]{1,0:T(1,128)}, u32[]{:S(2)}) copy-start(s32[1,8]{1,0:T(1,128)} %param.17) | copy-start | bytes 100
  0.0 11.4 %copy-start.2 = (s32[8]{0:T(128)S(1)}, s32[8]{0:T(128)}, u32[]{:S(2)}) copy-start(s32[8]{0:T(128)} %param.16) | copy-start | bytes 100
  1.0 24.5 %collective-permute-start.4 = (bf16[1,128,512]{2,1,0:T(8,128)(2,1)S(1)}, bf16[1,128,512]{2,1,0:T(8,128)(2,1)S(1)}, u32[]{:S(2)}, u32[]{:S(2)}) collective-permute-start(bf16[1,128,512]{2,1,0:T(8,128)(2,1)S(1)} %get-tuple-element.37), channel_id=1, source_target_pairs={{0,3},{1,2},{2,1},{3,0},{4,7},{5,6},{6,5},{7,4},{8,11},{9,10},{10,... | collective-permute-start | bytes 393224 | tf_op jit(solution)/shard_map/ppermute | solution.py:327
  6.2 23.2 %collective-permute-start.3 = (bf16[1,128,512]{2,1,0:T(8,128)(2,1)S(1)}, bf16[1,128,512]{2,1,0:T(8,128)(2,1)S(1)}, u32[]{:S(2)}, u32[]{:S(2)}) collective-permute-start(bf16[1,128,512]{2,1,0:T(8,128)(2,1)S(1)} %get-tuple-element.28), channel_id=1, source_target_pairs={{0,2},{1,3},{2,0},{3,1},{4,6},{5,7},{6,4},{7,5},{8,10},{9,11},{10,... | collective-permute-start | bytes 393224 | tf_op jit(solution)/shard_map/ppermute | solution.py:327
  7.6 26.3 %collective-permute-start.5 = (bf16[1,128,512]{2,1,0:T(8,128)(2,1)S(1)}, bf16[1,128,512]{2,1,0:T(8,128)(2,1)S(1)}, u32[]{:S(2)}, u32[]{:S(2)}) collective-permute-start(bf16[1,128,512]{2,1,0:T(8,128)(2,1)S(1)} %get-tuple-element.38), channel_id=1, source_target_pairs={{0,2},{1,3},{2,0},{3,1},{4,6},{5,7},{6,4},{7,5},{8,10},{9,11},{10,... | collective-permute-start | bytes 393224 | tf_op jit(solution)/shard_map/ppermute | solution.py:327
  10.6 23.4 %collective-permute-start.6 = (bf16[1,128,512]{2,1,0:T(8,128)(2,1)S(1)}, bf16[1,128,512]{2,1,0:T(8,128)(2,1)S(1)}, u32[]{:S(2)}, u32[]{:S(2)}) collective-permute-start(bf16[1,128,512]{2,1,0:T(8,128)(2,1)S(1)} %get-tuple-element.39), channel_id=1, source_target_pairs={{0,3},{1,2},{2,1},{3,0},{4,7},{5,6},{6,5},{7,4},{8,11},{9,10},{10,... | collective-permute-start | bytes 393224 | tf_op jit(solution)/shard_map/ppermute | solution.py:327
  10.7 18.8 %collective-permute-start = (bf16[3,128,512]{2,1,0:T(8,128)(2,1)S(1)}, bf16[3,128,512]{2,1,0:T(8,128)(2,1)S(1)}, u32[]{:S(2)}, u32[]{:S(2)}) collective-permute-start(bf16[3,128,512]{2,1,0:T(8,128)(2,1)S(1)} %get-tuple-element.31), channel_id=1, source_target_pairs={{0,1},{1,0},{2,3},{3,2},{4,5},{5,4},{6,7},{7,6},{8,9},{9,8},{10,11... | collective-permute-start | bytes 1179656 | tf_op jit(solution)/shard_map/ppermute | solution.py:327
  25.6 12.4 %collective-permute-start.1 = (bf16[1,128,512]{2,1,0:T(8,128)(2,1)S(1)}, bf16[1,128,512]{2,1,0:T(8,128)(2,1)S(1)}, u32[]{:S(2)}, u32[]{:S(2)}) collective-permute-start(bf16[1,128,512]{2,1,0:T(8,128)(2,1)S(1)} %get-tuple-element.35), channel_id=1, source_target_pairs={{0,2},{1,3},{2,0},{3,1},{4,6},{5,7},{6,4},{7,5},{8,10},{9,11},{10,... | collective-permute-start | bytes 393224 | tf_op jit(solution)/shard_map/ppermute | solution.py:327
  29.4 8.6 %collective-permute-start.2 = (bf16[1,128,512]{2,1,0:T(8,128)(2,1)S(1)}, bf16[1,128,512]{2,1,0:T(8,128)(2,1)S(1)}, u32[]{:S(2)}, u32[]{:S(2)}) collective-permute-start(bf16[1,128,512]{2,1,0:T(8,128)(2,1)S(1)} %get-tuple-element.36), channel_id=1, source_target_pairs={{0,3},{1,2},{2,1},{3,0},{4,7},{5,6},{6,5},{7,4},{8,11},{9,10},{10,... | collective-permute-start | bytes 393224 | tf_op jit(solution)/shard_map/ppermute | solution.py:327
  38.7 6.4 %collective-permute-start.7 = (bf16[80,128]{1,0:T(8,128)(2,1)S(1)}, bf16[80,128]{1,0:T(8,128)(2,1)S(1)}, u32[]{:S(2)}, u32[]{:S(2)}) collective-permute-start(bf16[80,128]{1,0:T(8,128)(2,1)S(1)} %mix.4), channel_id=1, source_target_pairs={{0,3},{1,2},{2,1},{3,0},{4,7},{5,6},{6,5},{7,4},{8,11},{9,10},{10,... | collective-permute-start | bytes 61448 | tf_op jit(solution)/shard_map/ppermute | solution.py:327
  42.1 4.7 %collective-permute-start.8 = (bf16[80,128]{1,0:T(8,128)(2,1)S(1)}, bf16[80,128]{1,0:T(8,128)(2,1)S(1)}, u32[]{:S(2)}, u32[]{:S(2)}) collective-permute-start(bf16[80,128]{1,0:T(8,128)(2,1)S(1)} %mix.5), channel_id=1, source_target_pairs={{0,2},{1,3},{2,0},{3,1},{4,6},{5,7},{6,4},{7,5},{8,10},{9,11},{10,... | collective-permute-start | bytes 61448 | tf_op jit(solution)/shard_map/ppermute | solution.py:327
  43.9 15.6 %copy-start = (s32[8]{0:T(128)S(1)}, s32[8]{0:T(128)}, u32[]{:S(2)}) copy-start(s32[8]{0:T(128)} %param.23) | copy-start | bytes 100
  43.9 3.8 %collective-permute-start.9 = (bf16[80,128]{1,0:T(8,128)(2,1)S(1)}, bf16[80,128]{1,0:T(8,128)(2,1)S(1)}, u32[]{:S(2)}, u32[]{:S(2)}) collective-permute-start(bf16[80,128]{1,0:T(8,128)(2,1)S(1)} %mix.6), channel_id=1, source_target_pairs={{0,1},{1,0},{2,3},{3,2},{4,5},{5,4},{6,7},{7,6},{8,9},{9,8},{10,11... | collective-permute-start | bytes 61448 | tf_op jit(solution)/shard_map/ppermute | solution.py:327

commit v9 on v8

--- a/solution.py
+++ b/solution.py
@@ -197,15 +197,16 @@
             base_ref[rows, head_cols(h)] = (fade * share) * text_ref[rows, head_cols(h)]
 
 
-def mix_kernel(sources, reach, k_target, *refs):
-    v_refs = refs[:sources]
-    weight_ref, base_ref, scale_ref, wt_ref, out_ref, v_all = refs[sources:]
+def mix_kernel(sources, reach, k_target, have, *refs):
+    v_refs = refs[:have]
+    weight_ref, base_ref, scale_ref, wt_ref, out_ref, v_all = refs[have:]
     tok_dev, local = v_refs[0].shape[1:]
     group_rows = scale_ref.shape[0]
     heads = local // HEAD_DIM
     channels = wt_ref.shape[0]
     for k in range(sources):
-        v_all[source_rows(sources, k, tok_dev), :] = v_refs[k][2 if k < NEAR else 0]
+        block = v_refs[k][2 if k < NEAR else 0] if k < have else jnp.zeros((tok_dev, local), BF16)
+        v_all[source_rows(sources, k, tok_dev), :] = block
     count = out_ref.shape[1]
     first = pl.multiple_of(partner(lax.axis_index("seq"), k_target, sources) * tok_dev, tok_dev)
     rows = pl.ds(first, count)
@@ -373,15 +374,25 @@
         [pltpu.VMEM((group_rows, local), BF16)] * 2, scalars=[info],
     )
 
-    parts = []
-    for k in reversed(range(sources)):
-        (part,) = call(
-            functools.partial(mix_kernel, sources, reach, k), "mix",
-            [*near_blocks, *v_blocks, weights, base, scale_tok, weight_local],
+    def mix(k, have):
+        return call(
+            functools.partial(mix_kernel, sources, reach, k, have), "mix",
+            [*[*near_blocks, *v_blocks][:have], weights, base, scale_tok, weight_local],
             [((channels + STAT_ROWS, tok_dev), BF16)],
             [pltpu.VMEM((group_rows, local), BF16)], flops=4 * tok_dev * reach[1] * local, traffic=2**20,
-        )
-        parts.append(onward(part, k))
+        )[0]
+
+    parts = [None] * sources
+    if sources == 4 and clip_most <= tok_dev:
+        first = mix(1, 3)
+        parts[1] = onward(first, 1)
+        v_blocks[-1], _ = lax.optimization_barrier((v_blocks[-1], first))
+    for k in reversed(range(sources)):
+        if parts[k] is None:
+            parts[k] = onward(mix(k, sources), k)
+        if k == 3 and parts[1] is not None:
+            weights, parts[1] = lax.optimization_barrier((weights, parts[1]))
+    parts = parts[::-1]
 
     (shares,) = call(
         functools.partial(loss_kernel, sources, width), "loss", [*parts, slope, offset, share],

time: 60.4 us -> 60.9 us (level)
  transfers between devices with their start and end apart: 10 -> 10, of which waited for: 3 -> 3; matrix products, arithmetic and copies ran while one was open for 0% -> 0% of each run, Pallas kernels for 40% -> 41%
where the time goes in v9:
time: 60.9 us; the launch traced here: 60.7 us
  Pallas kernels  26.8 us (44%)
  starting transfers between devices  16.8 us (28%)
  blocking collectives  12 us (20%)
  waiting for transfers between devices  4.74 us (8%)
    pallas_call x11, Pallas kernels, call(): pl.pallas_call(kernel, in_specs=[smem()] * len(scalars) + [hbm() if i in...  26.8 us
    ppermute x10, starting transfers between devices, onward(): lax.ppermute(x, 'seq', [(i, partner(i, k, sources)) for i in range(source...  16.8 us
    all_to_all x1, blocking collectives, per_device(): lax.all_to_all(shares, ('dp', 'seq'), split_axis=0, concat_axis=0, tiled=...  12 us
    ppermute x10, waiting for transfers between devices, onward(): lax.ppermute(x, 'seq', [(i, partner(i, k, sources)) for i in range(source...  4.74 us
  transfers between devices with their start and end apart: 10, of which 3 were waited for; matrix products, arithmetic and copies ran while one was open for 0% of the time, Pallas kernels for 41%

profile of v9, /device:TPU:0, one launch (start us, length us, event | category | flops | bytes accessed | tf_op | source)
XLA Modules:
  0.0 60.7 jit_solution(18241363134730396397)
XLA Ops:
  0.0 1.0 %cut_first.1 = (bf16[1,128,512]{2,1,0:T(8,128)(2,1)S(1)}, bf16[1,128,512]{2,1,0:T(8,128)(2,1)S(1)}) custom-call(bf16[128,2048]{1,0:T(8,128)(2,1)} %refs_0_.3), custom_call_target="tpu_custom_call" | custom-call | bytes 524288 | tf_op jit(solution)/shard_map/cut_first/pallas_call | solution.py:286
  1.0 5.1 %collective-permute-start.4 = (bf16[1,128,512]{2,1,0:T(8,128)(2,1)S(1)}, bf16[1,128,512]{2,1,0:T(8,128)(2,1)S(1)}, u32[]{:S(2)}, u32[]{:S(2)}) collective-permute-start(bf16[1,128,512]{2,1,0:T(8,128)(2,1)S(1)} %get-tuple-element.40), channel_id=1, source_target_pairs={{0,3},{1,2},{2,1},{3,0},{4,7},{5,6},{6,5},{7,4},{8,11},{9,10},{10,... | collective-permute-start | bytes 393224 | tf_op jit(solution)/shard_map/ppermute | solution.py:328
  6.2 0.0 collective-permute-start.3
  6.2 1.5 %cut_rest.1 = (bf16[3,128,512]{2,1,0:T(8,128)(2,1)S(1)}, bf16[3,128,512]{2,1,0:T(8,128)(2,1)S(1)}, bf16[1,128,512]{2,1,0:T(8,128)(2,1)S(1)}, bf16[1,128,512]{2,1...) custom-call(bf16[128,2048]{1,0:T(8,128)(2,1)} %refs_0_.3, ...), custom_call_target="tpu_custom_call" | custom-call | bytes 2621440 | tf_op jit(solution)/shard_map/cut_rest/pallas_call | solution.py:286
  7.6 3.0 %collective-permute-start.5 = (bf16[1,128,512]{2,1,0:T(8,128)(2,1)S(1)}, bf16[1,128,512]{2,1,0:T(8,128)(2,1)S(1)}, u32[]{:S(2)}, u32[]{:S(2)}) collective-permute-start(bf16[1,128,512]{2,1,0:T(8,128)(2,1)S(1)} %get-tuple-element.41), channel_id=1, source_target_pairs={{0,2},{1,3},{2,0},{3,1},{4,6},{5,7},{6,4},{7,5},{8,10},{9,11},{10,... | collective-permute-start | bytes 393224 | tf_op jit(solution)/shard_map/ppermute | solution.py:328
  10.6 0.1 collective-permute-start.6
  10.7 0.6 collective-permute-start
  11.3 0.1 multiply_cosine_fusion
  11.4 0.1 pad_add_fusion.info_ref
  11.5 14.1 %prep.1 = (f32[512,512]{1,0:T(8,128)S(1)}, f32[4,64,128]{2,1,0:T(8,128)S(1)}, f32[64,128]{1,0:T(8,128)S(1)}, f32[8,128]{1,0:T(8,128)S(1)}, bf16[64,512]{1,0:T(8,...) custom-call(s32[16]{0:T(128)S(1)} %pad_add_fusion.info_ref, ...), custom_call_target="tpu_custom_call" | custom-call | tf_op jit(solution)/shard_map/prep/pallas_call | solution.py:286
  25.6 0.0 collective-permute-done.4.refs_3_
  25.6 3.8 %collective-permute-start.1 = (bf16[1,128,512]{2,1,0:T(8,128)(2,1)S(1)}, bf16[1,128,512]{2,1,0:T(8,128)(2,1)S(1)}, u32[]{:S(2)}, u32[]{:S(2)}) collective-permute-start(bf16[1,128,512]{2,1,0:T(8,128)(2,1)S(1)} %get-tuple-element.38), channel_id=1, source_target_pairs={{0,2},{1,3},{2,0},{3,1},{4,6},{5,7},{6,4},{7,5},{8,10},{9,11},{10,... | collective-permute-start | bytes 393224 | tf_op jit(solution)/shard_map/ppermute | solution.py:328
  29.4 0.0 collective-permute-done.3.refs_2_
  29.4 0.1 collective-permute-start.2
  29.5 0.0 collective-permute-done.refs_1_
  29.5 4.5 %text.1 = (f32[656,512]{1,0:T(8,128)S(1)}, f32[4,656,128]{2,1,0:T(8,128)S(1)}) custom-call(s32[16]{0:T(128)S(1)} %pad_add_fusion.info_ref, bf16[3,128,512]{2,1,0:T(8,128)(2,1)S(1)} %get-tuple-element.33.refs_0_, bf16[3,128,512]{2,1,0:T(8,128)(2,1)S(1)} %collective-permute-done.refs_1_, bf16[1,128,512]{2,1,0:T(8,128)(2,1)S(1)} %collective-permute-done.3.refs_2_, ...), custom_call_target="tpu_custom_call" | custom-call | tf_op jit(solution)/shard_map/text/pallas_call | solution.py:286
  34.0 0.0 collective-permute-done.5.refs_4_
  34.0 0.0 collective-permute-done.6.refs_5_
  34.0 2.3 %weigh.1 = (bf16[4,512,384]{2,1,0:T(8,128)(2,1)S(1)}, f32[512,512]{1,0:T(8,128)S(1)}) custom-call(s32[16]{0:T(128)S(1)} %pad_add_fusion.info_ref, bf16[3,128,512]{2,1,0:T(8,128)(2,1)S(1)} %get-tuple-element.33.refs_0_, bf16[3,128,512]{2,1,0:T(8,128)(2,1)S(1)} %collective-permute-done.refs_1_, bf16[1,128,512]{2,1,0:T(8,128)(2,1)S(1)} %collective-permute-done.3.refs_2_, ...), custom_call_target="tpu_custom_call" | custom-call | tf_op jit(solution)/shard_map/weigh/pallas_call | solution.py:286
  36.3 1.7 %collective-permute-done.1.refs_2_ = bf16[1,128,512]{2,1,0:T(8,128)(2,1)S(1)} collective-permute-done((bf16[1,128,512]{2,1,0:T(8,128)(2,1)S(1)}, bf16[1,128,512]{2,1,0:T(8,128)(2,1)S(1)}, u32[]{:S(2)}, u32[]{:S(2)}) %collective-permute-start.1) | collective-permute-done | bytes 131104 | tf_op jit(solution)/shard_map/ppermute | solution.py:328
  38.0 0.7 %mix.4 = bf16[80,128]{1,0:T(8,128)(2,1)S(1)} custom-call(bf16[3,128,512]{2,1,0:T(8,128)(2,1)S(1)} %get-tuple-element.33.refs_0_, bf16[3,128,512]{2,1,0:T(8,128)(2,1)S(1)} %collective-permute-done.refs_1_, bf16[1,128,512]{2,1,0:T(8,128)(2,1)S(1)} %collective-permute-done.1.refs_2_, bf16[4,512,384]{2,1,0:T(8,128)(2,1)S(1)} %get-tuple-element.52.refs_3_.refs_4_, ...), custom_call_target="tpu_custom_call" | custom-call | flops 100663296 | bytes 1048576 | tf_op jit(solution)/shard_map/mix/pallas_call | solution.py:286
  38.7 0.0 collective-permute-start.8
  38.7 0.7 %mix.5 = bf16[80,128]{1,0:T(8,128)(2,1)S(1)} custom-call(bf16[3,128,512]{2,1,0:T(8,128)(2,1)S(1)} %get-tuple-element.33.refs_0_, bf16[3,128,512]{2,1,0:T(8,128)(2,1)S(1)} %collective-permute-done.refs_1_, bf16[1,128,512]{2,1,0:T(8,128)(2,1)S(1)} %collective-permute-done.1.refs_2_, bf16[1,128,512]{2,1,0:T(8,128)(2,1)S(1)} %collective-permute-done.2.refs_3_, ...), custom_call_target="tpu_custom_call" | custom-call | flops 100663296 | bytes 1048576 | tf_op jit(solution)/shard_map/mix/pallas_call | solution.py:286
  39.4 2.8 %collective-permute-start.7 = (bf16[80,128]{1,0:T(8,128)(2,1)S(1)}, bf16[80,128]{1,0:T(8,128)(2,1)S(1)}, u32[]{:S(2)}, u32[]{:S(2)}) collective-permute-start(bf16[80,128]{1,0:T(8,128)(2,1)S(1)} %mix.5), channel_id=1, source_target_pairs={{0,3},{1,2},{2,1},{3,0},{4,7},{5,6},{6,5},{7,4},{8,11},{9,10},{10,... | collective-permute-start | bytes 61448 | tf_op jit(solution)/shard_map/ppermute | solution.py:328
  42.2 0.3 collective-permute-done.8.refs_2_
  42.5 0.7 %mix.6 = bf16[80,128]{1,0:T(8,128)(2,1)S(1)} custom-call(bf16[3,128,512]{2,1,0:T(8,128)(2,1)S(1)} %get-tuple-element.33.refs_0_, bf16[3,128,512]{2,1,0:T(8,128)(2,1)S(1)} %collective-permute-done.refs_1_, bf16[1,128,512]{2,1,0:T(8,128)(2,1)S(1)} %collective-permute-done.1.refs_2_, bf16[1,128,512]{2,1,0:T(8,128)(2,1)S(1)} %collective-permute-done.2.refs_3_, ...), custom_call_target="tpu_custom_call" | custom-call | flops 100663296 | bytes 1048576 | tf_op jit(solution)/shard_map/mix/pallas_call | solution.py:286
  43.1 1.4 %collective-permute-start.9 = (bf16[80,128]{1,0:T(8,128)(2,1)S(1)}, bf16[80,128]{1,0:T(8,128)(2,1)S(1)}, u32[]{:S(2)}, u32[]{:S(2)}) collective-permute-start(bf16[80,128]{1,0:T(8,128)(2,1)S(1)} %mix.6), channel_id=1, source_target_pairs={{0,2},{1,3},{2,0},{3,1},{4,6},{5,7},{6,4},{7,5},{8,10},{9,11},{10,... | collective-permute-start | bytes 61448 | tf_op jit(solution)/shard_map/ppermute | solution.py:328
  44.5 0.7 %mix.7.refs_3_ = bf16[80,128]{1,0:T(8,128)(2,1)S(1)} custom-call(bf16[3,128,512]{2,1,0:T(8,128)(2,1)S(1)} %get-tuple-element.33.refs_0_, bf16[3,128,512]{2,1,0:T(8,128)(2,1)S(1)} %collective-permute-done.refs_1_, bf16[1,128,512]{2,1,0:T(8,128)(2,1)S(1)} %collective-permute-done.1.refs_2_, bf16[1,128,512]{2,1,0:T(8,128)(2,1)S(1)} %collective-permute-done.2.refs_3_, ...), custom_call_target="tpu_custom_call" | custom-call | flops 100663296 | bytes 1048576 | tf_op jit(solution)/shard_map/mix/pallas_call | solution.py:286
  45.2 2.7 %collective-permute-done.9.refs_1_ = bf16[80,128]{1,0:T(8,128)(2,1)S(1)} collective-permute-done((bf16[80,128]{1,0:T(8,128)(2,1)S(1)}, bf16[80,128]{1,0:T(8,128)(2,1)S(1)}, u32[]{:S(2)}, u32[]{:S(2)}) %collective-permute-start.9) | collective-permute-done | bytes 20512 | tf_op jit(solution)/shard_map/ppermute | solution.py:328
  47.9 0.1 loss.1
  48.0 12.0 %all_to_all.5 = f32[32,1,128]{2,1,0:T(1,128)S(1)} all-to-all(f32[32,1,128]{2,1,0:T(1,128)S(1)} %loss.1), channel_id=1, replica_groups=mesh['dp'=8,'seq'=4] {'dp','seq'}, dimensions={0} | all-to-all | bytes 32768 | tf_op jit(solution)/shard_map/all_to_all | solution.py:401
  60.0 0.7 %pick.1 = f32[1,8]{1,0:T(1,128)} custom-call(f32[8,4,128]{2,1,0:T(4,128)S(1)} %bitcast.7, s32[1,8]{1,0:T(1,128)S(1)} %bitcast.8), custom_call_target="tpu_custom_call" | custom-call | tf_op jit(solution)/shard_map/pick/pallas_call | solution.py:286
  (13 shorter events, 0.0 us)
Async XLA Ops:
  0.0 11.3 %copy-start.1 = (s32[8]{0:T(128)S(1)}, s32[8]{0:T(128)}, u32[]{:S(2)}) copy-start(s32[8]{0:T(128)} %param.18) | copy-start | bytes 100
  0.0 11.4 %copy-start.3 = (s32[1,8]{1,0:T(1,128)S(1)}, s32[1,8]{1,0:T(1,128)}, u32[]{:S(2)}) copy-start(s32[1,8]{1,0:T(1,128)} %param.17) | copy-start | bytes 100
  0.0 11.4 %copy-start.2 = (s32[8]{0:T(128)S(1)}, s32[8]{0:T(128)}, u32[]{:S(2)}) copy-start(s32[8]{0:T(128)} %param.16) | copy-start | bytes 100
  1.0 24.5 %collective-permute-start.4 = (bf16[1,128,512]{2,1,0:T(8,128)(2,1)S(1)}, bf16[1,128,512]{2,1,0:T(8,128)(2,1)S(1)}, u32[]{:S(2)}, u32[]{:S(2)}) collective-permute-start(bf16[1,128,512]{2,1,0:T(8,128)(2,1)S(1)} %get-tuple-element.40), channel_id=1, source_target_pairs={{0,3},{1,2},{2,1},{3,0},{4,7},{5,6},{6,5},{7,4},{8,11},{9,10},{10,... | collective-permute-start | bytes 393224 | tf_op jit(solution)/shard_map/ppermute | solution.py:328
  6.2 23.2 %collective-permute-start.3 = (bf16[1,128,512]{2,1,0:T(8,128)(2,1)S(1)}, bf16[1,128,512]{2,1,0:T(8,128)(2,1)S(1)}, u32[]{:S(2)}, u32[]{:S(2)}) collective-permute-start(bf16[1,128,512]{2,1,0:T(8,128)(2,1)S(1)} %get-tuple-element.31), channel_id=1, source_target_pairs={{0,2},{1,3},{2,0},{3,1},{4,6},{5,7},{6,4},{7,5},{8,10},{9,11},{10,... | collective-permute-start | bytes 393224 | tf_op jit(solution)/shard_map/ppermute | solution.py:328
  7.6 26.3 %collective-permute-start.5 = (bf16[1,128,512]{2,1,0:T(8,128)(2,1)S(1)}, bf16[1,128,512]{2,1,0:T(8,128)(2,1)S(1)}, u32[]{:S(2)}, u32[]{:S(2)}) collective-permute-start(bf16[1,128,512]{2,1,0:T(8,128)(2,1)S(1)} %get-tuple-element.41), channel_id=1, source_target_pairs={{0,2},{1,3},{2,0},{3,1},{4,6},{5,7},{6,4},{7,5},{8,10},{9,11},{10,... | collective-permute-start | bytes 393224 | tf_op jit(solution)/shard_map/ppermute | solution.py:328
  10.6 23.4 %collective-permute-start.6 = (bf16[1,128,512]{2,1,0:T(8,128)(2,1)S(1)}, bf16[1,128,512]{2,1,0:T(8,128)(2,1)S(1)}, u32[]{:S(2)}, u32[]{:S(2)}) collective-permute-start(bf16[1,128,512]{2,1,0:T(8,128)(2,1)S(1)} %get-tuple-element.42), channel_id=1, source_target_pairs={{0,3},{1,2},{2,1},{3,0},{4,7},{5,6},{6,5},{7,4},{8,11},{9,10},{10,... | collective-permute-start | bytes 393224 | tf_op jit(solution)/shard_map/ppermute | solution.py:328
  10.7 18.8 %collective-permute-start = (bf16[3,128,512]{2,1,0:T(8,128)(2,1)S(1)}, bf16[3,128,512]{2,1,0:T(8,128)(2,1)S(1)}, u32[]{:S(2)}, u32[]{:S(2)}) collective-permute-start(bf16[3,128,512]{2,1,0:T(8,128)(2,1)S(1)} %get-tuple-element.34), channel_id=1, source_target_pairs={{0,1},{1,0},{2,3},{3,2},{4,5},{5,4},{6,7},{7,6},{8,9},{9,8},{10,11... | collective-permute-start | bytes 1179656 | tf_op jit(solution)/shard_map/ppermute | solution.py:328
  25.6 12.4 %collective-permute-start.1 = (bf16[1,128,512]{2,1,0:T(8,128)(2,1)S(1)}, bf16[1,128,512]{2,1,0:T(8,128)(2,1)S(1)}, u32[]{:S(2)}, u32[]{:S(2)}) collective-permute-start(bf16[1,128,512]{2,1,0:T(8,128)(2,1)S(1)} %get-tuple-element.38), channel_id=1, source_target_pairs={{0,2},{1,3},{2,0},{3,1},{4,6},{5,7},{6,4},{7,5},{8,10},{9,11},{10,... | collective-permute-start | bytes 393224 | tf_op jit(solution)/shard_map/ppermute | solution.py:328
  29.4 9.3 %collective-permute-start.2 = (bf16[1,128,512]{2,1,0:T(8,128)(2,1)S(1)}, bf16[1,128,512]{2,1,0:T(8,128)(2,1)S(1)}, u32[]{:S(2)}, u32[]{:S(2)}) collective-permute-start(bf16[1,128,512]{2,1,0:T(8,128)(2,1)S(1)} %get-tuple-element.39), channel_id=1, source_target_pairs={{0,3},{1,2},{2,1},{3,0},{4,7},{5,6},{6,5},{7,4},{8,11},{9,10},{10,... | collective-permute-start | bytes 393224 | tf_op jit(solution)/shard_map/ppermute | solution.py:328
  38.7 3.8 %collective-permute-start.8 = (bf16[80,128]{1,0:T(8,128)(2,1)S(1)}, bf16[80,128]{1,0:T(8,128)(2,1)S(1)}, u32[]{:S(2)}, u32[]{:S(2)}) collective-permute-start(bf16[80,128]{1,0:T(8,128)(2,1)S(1)} %mix.4), channel_id=1, source_target_pairs={{0,1},{1,0},{2,3},{3,2},{4,5},{5,4},{6,7},{7,6},{8,9},{9,8},{10,11... | collective-permute-start | bytes 61448 | tf_op jit(solution)/shard_map/ppermute | solution.py:328
  39.4 5.8 %collective-permute-start.7 = (bf16[80,128]{1,0:T(8,128)(2,1)S(1)}, bf16[80,128]{1,0:T(8,128)(2,1)S(1)}, u32[]{:S(2)}, u32[]{:S(2)}) collective-permute-start(bf16[80,128]{1,0:T(8,128)(2,1)S(1)} %mix.5), channel_id=1, source_target_pairs={{0,3},{1,2},{2,1},{3,0},{4,7},{5,6},{6,5},{7,4},{8,11},{9,10},{10,... | collective-permute-start | bytes 61448 | tf_op jit(solution)/shard_map/ppermute | solution.py:328
  43.1 16.9 %copy-start = (s32[8]{0:T(128)S(1)}, s32[8]{0:T(128)}, u32[]{:S(2)}) copy-start(s32[8]{0:T(128)} %param.23) | copy-start | bytes 100
  43.1 4.7 %collective-permute-start.9 = (bf16[80,128]{1,0:T(8,128)(2,1)S(1)}, bf16[80,128]{1,0:T(8,128)(2,1)S(1)}, u32[]{:S(2)}, u32[]{:S(2)}) collective-permute-start(bf16[80,128]{1,0:T(8,128)(2,1)S(1)} %mix.6), channel_id=1, source_target_pairs={{0,2},{1,3},{2,0},{3,1},{4,6},{5,7},{6,4},{7,5},{8,10},{9,11},{10,... | collective-permute-start | bytes 61448 | tf_op jit(solution)/shard_map/ppermute | solution.py:328

commit v10 on v9

--- a/solution.py
+++ b/solution.py
@@ -390,7 +390,7 @@
     for k in reversed(range(sources)):
         if parts[k] is None:
             parts[k] = onward(mix(k, sources), k)
-        if k == 3 and parts[1] is not None:
+        if k == 2 and parts[1] is not None:
             weights, parts[1] = lax.optimization_barrier((weights, parts[1]))
     parts = parts[::-1]
 

time: 60.9 us -> 58.9 us (0.967)
  blocking collectives: 12 us -> 10.3 us
    all_to_all x1, blocking collectives: 12 us -> 10.3 us  [per_device(): lax.all_to_all(shares, ('dp', 'seq'), split_axis=0, concat_axis=0, tiled=...]
    ppermute x10, starting transfers between devices: 16.8 us -> 16.2 us  [onward(): lax.ppermute(x, 'seq', [(i, partner(i, k, sources)) for i in range(source...]
  transfers between devices with their start and end apart: 10 -> 10, of which waited for: 3 -> 3; matrix products, arithmetic and copies ran while one was open for 0% -> 0% of each run, Pallas kernels for 41% -> 42%
where the time goes in v10:
time: 58.9 us; the launch traced here: 58.7 us
  Pallas kernels  26.8 us (46%)
  starting transfers between devices  16.2 us (28%)
  blocking collectives  10.3 us (17%)
  waiting for transfers between devices  5.11 us (9%)
    pallas_call x11, Pallas kernels, call(): pl.pallas_call(kernel, in_specs=[smem()] * len(scalars) + [hbm() if i in...  26.8 us
    ppermute x10, starting transfers between devices, onward(): lax.ppermute(x, 'seq', [(i, partner(i, k, sources)) for i in range(source...  16.2 us
    all_to_all x1, blocking collectives, per_device(): lax.all_to_all(shares, ('dp', 'seq'), split_axis=0, concat_axis=0, tiled=...  10.3 us
    ppermute x10, waiting for transfers between devices, onward(): lax.ppermute(x, 'seq', [(i, partner(i, k, sources)) for i in range(source...  5.11 us
  transfers between devices with their start and end apart: 10, of which 3 were waited for; matrix products, arithmetic and copies ran while one was open for 0% of the time, Pallas kernels for 42%

profile of v10, /device:TPU:0, one launch (start us, length us, event | category | flops | bytes accessed | tf_op | source)
XLA Modules:
  0.0 58.7 jit_solution(93407061051646590)
XLA Ops:
  0.0 1.0 %cut_first.1 = (bf16[1,128,512]{2,1,0:T(8,128)(2,1)S(1)}, bf16[1,128,512]{2,1,0:T(8,128)(2,1)S(1)}) custom-call(bf16[128,2048]{1,0:T(8,128)(2,1)} %refs_0_.3), custom_call_target="tpu_custom_call" | custom-call | bytes 524288 | tf_op jit(solution)/shard_map/cut_first/pallas_call | solution.py:286
  1.0 5.1 %collective-permute-start.4 = (bf16[1,128,512]{2,1,0:T(8,128)(2,1)S(1)}, bf16[1,128,512]{2,1,0:T(8,128)(2,1)S(1)}, u32[]{:S(2)}, u32[]{:S(2)}) collective-permute-start(bf16[1,128,512]{2,1,0:T(8,128)(2,1)S(1)} %get-tuple-element.40), channel_id=1, source_target_pairs={{0,3},{1,2},{2,1},{3,0},{4,7},{5,6},{6,5},{7,4},{8,11},{9,10},{10,... | collective-permute-start | bytes 393224 | tf_op jit(solution)/shard_map/ppermute | solution.py:328
  6.2 0.0 collective-permute-start.3
  6.2 1.5 %cut_rest.1 = (bf16[3,128,512]{2,1,0:T(8,128)(2,1)S(1)}, bf16[3,128,512]{2,1,0:T(8,128)(2,1)S(1)}, bf16[1,128,512]{2,1,0:T(8,128)(2,1)S(1)}, bf16[1,128,512]{2,1...) custom-call(bf16[128,2048]{1,0:T(8,128)(2,1)} %refs_0_.3, ...), custom_call_target="tpu_custom_call" | custom-call | bytes 2621440 | tf_op jit(solution)/shard_map/cut_rest/pallas_call | solution.py:286
  7.6 3.0 %collective-permute-start.5 = (bf16[1,128,512]{2,1,0:T(8,128)(2,1)S(1)}, bf16[1,128,512]{2,1,0:T(8,128)(2,1)S(1)}, u32[]{:S(2)}, u32[]{:S(2)}) collective-permute-start(bf16[1,128,512]{2,1,0:T(8,128)(2,1)S(1)} %get-tuple-element.41), channel_id=1, source_target_pairs={{0,2},{1,3},{2,0},{3,1},{4,6},{5,7},{6,4},{7,5},{8,10},{9,11},{10,... | collective-permute-start | bytes 393224 | tf_op jit(solution)/shard_map/ppermute | solution.py:328
  10.6 0.1 collective-permute-start.6
  10.7 0.6 collective-permute-start
  11.3 0.1 multiply_cosine_fusion
  11.4 0.1 pad_add_fusion.info_ref
  11.5 14.1 %prep.1 = (f32[512,512]{1,0:T(8,128)S(1)}, f32[4,64,128]{2,1,0:T(8,128)S(1)}, f32[64,128]{1,0:T(8,128)S(1)}, f32[8,128]{1,0:T(8,128)S(1)}, bf16[64,512]{1,0:T(8,...) custom-call(s32[16]{0:T(128)S(1)} %pad_add_fusion.info_ref, ...), custom_call_target="tpu_custom_call" | custom-call | tf_op jit(solution)/shard_map/prep/pallas_call | solution.py:286
  25.6 0.0 collective-permute-done.4.refs_3_
  25.6 3.8 %collective-permute-start.1 = (bf16[1,128,512]{2,1,0:T(8,128)(2,1)S(1)}, bf16[1,128,512]{2,1,0:T(8,128)(2,1)S(1)}, u32[]{:S(2)}, u32[]{:S(2)}) collective-permute-start(bf16[1,128,512]{2,1,0:T(8,128)(2,1)S(1)} %get-tuple-element.38), channel_id=1, source_target_pairs={{0,2},{1,3},{2,0},{3,1},{4,6},{5,7},{6,4},{7,5},{8,10},{9,11},{10,... | collective-permute-start | bytes 393224 | tf_op jit(solution)/shard_map/ppermute | solution.py:328
  29.4 0.0 collective-permute-done.3.refs_2_
  29.4 0.1 collective-permute-start.2
  29.5 4.5 %text.1 = (f32[656,512]{1,0:T(8,128)S(1)}, f32[4,656,128]{2,1,0:T(8,128)S(1)}) custom-call(s32[16]{0:T(128)S(1)} %pad_add_fusion.info_ref, bf16[3,128,512]{2,1,0:T(8,128)(2,1)S(1)} %get-tuple-element.33.refs_0_, bf16[3,128,512]{2,1,0:T(8,128)(2,1)S(1)} %collective-permute-done.refs_1_, bf16[1,128,512]{2,1,0:T(8,128)(2,1)S(1)} %collective-permute-done.3.refs_2_, ...), custom_call_target="tpu_custom_call" | custom-call | tf_op jit(solution)/shard_map/text/pallas_call | solution.py:286
  34.0 0.0 collective-permute-done.5.refs_4_
  34.0 0.0 collective-permute-done.6.refs_5_
  34.0 2.3 %weigh.1 = (bf16[4,512,384]{2,1,0:T(8,128)(2,1)S(1)}, f32[512,512]{1,0:T(8,128)S(1)}) custom-call(s32[16]{0:T(128)S(1)} %pad_add_fusion.info_ref, bf16[3,128,512]{2,1,0:T(8,128)(2,1)S(1)} %get-tuple-element.33.refs_0_, bf16[3,128,512]{2,1,0:T(8,128)(2,1)S(1)} %collective-permute-done.refs_1_, bf16[1,128,512]{2,1,0:T(8,128)(2,1)S(1)} %collective-permute-done.3.refs_2_, ...), custom_call_target="tpu_custom_call" | custom-call | tf_op jit(solution)/shard_map/weigh/pallas_call | solution.py:286
  36.3 1.7 %collective-permute-done.1.refs_2_ = bf16[1,128,512]{2,1,0:T(8,128)(2,1)S(1)} collective-permute-done((bf16[1,128,512]{2,1,0:T(8,128)(2,1)S(1)}, bf16[1,128,512]{2,1,0:T(8,128)(2,1)S(1)}, u32[]{:S(2)}, u32[]{:S(2)}) %collective-permute-start.1) | collective-permute-done | bytes 131104 | tf_op jit(solution)/shard_map/ppermute | solution.py:328
  38.0 0.7 %mix.4 = bf16[80,128]{1,0:T(8,128)(2,1)S(1)} custom-call(bf16[3,128,512]{2,1,0:T(8,128)(2,1)S(1)} %get-tuple-element.33.refs_0_, bf16[3,128,512]{2,1,0:T(8,128)(2,1)S(1)} %collective-permute-done.refs_1_, bf16[1,128,512]{2,1,0:T(8,128)(2,1)S(1)} %collective-permute-done.1.refs_2_, bf16[4,512,384]{2,1,0:T(8,128)(2,1)S(1)} %get-tuple-element.53.refs_3_.refs_4_, ...), custom_call_target="tpu_custom_call" | custom-call | flops 100663296 | bytes 1048576 | tf_op jit(solution)/shard_map/mix/pallas_call | solution.py:286
  38.7 0.0 collective-permute-start.9
  38.7 0.7 %mix.5 = bf16[80,128]{1,0:T(8,128)(2,1)S(1)} custom-call(bf16[3,128,512]{2,1,0:T(8,128)(2,1)S(1)} %get-tuple-element.33.refs_0_, bf16[3,128,512]{2,1,0:T(8,128)(2,1)S(1)} %collective-permute-done.refs_1_, bf16[1,128,512]{2,1,0:T(8,128)(2,1)S(1)} %collective-permute-done.1.refs_2_, bf16[1,128,512]{2,1,0:T(8,128)(2,1)S(1)} %collective-permute-done.2.refs_3_, ...), custom_call_target="tpu_custom_call" | custom-call | flops 100663296 | bytes 1048576 | tf_op jit(solution)/shard_map/mix/pallas_call | solution.py:286
  39.4 2.8 %collective-permute-start.7 = (bf16[80,128]{1,0:T(8,128)(2,1)S(1)}, bf16[80,128]{1,0:T(8,128)(2,1)S(1)}, u32[]{:S(2)}, u32[]{:S(2)}) collective-permute-start(bf16[80,128]{1,0:T(8,128)(2,1)S(1)} %mix.5), channel_id=1, source_target_pairs={{0,3},{1,2},{2,1},{3,0},{4,7},{5,6},{6,5},{7,4},{8,11},{9,10},{10,... | collective-permute-start | bytes 61448 | tf_op jit(solution)/shard_map/ppermute | solution.py:328
  42.2 0.7 %mix.6 = bf16[80,128]{1,0:T(8,128)(2,1)S(1)} custom-call(bf16[3,128,512]{2,1,0:T(8,128)(2,1)S(1)} %get-tuple-element.33.refs_0_, bf16[3,128,512]{2,1,0:T(8,128)(2,1)S(1)} %collective-permute-done.refs_1_, bf16[1,128,512]{2,1,0:T(8,128)(2,1)S(1)} %collective-permute-done.1.refs_2_, bf16[1,128,512]{2,1,0:T(8,128)(2,1)S(1)} %collective-permute-done.2.refs_3_, ...), custom_call_target="tpu_custom_call" | custom-call | flops 100663296 | bytes 1048576 | tf_op jit(solution)/shard_map/mix/pallas_call | solution.py:286
  42.8 0.7 %collective-permute-start.8 = (bf16[80,128]{1,0:T(8,128)(2,1)S(1)}, bf16[80,128]{1,0:T(8,128)(2,1)S(1)}, u32[]{:S(2)}, u32[]{:S(2)}) collective-permute-start(bf16[80,128]{1,0:T(8,128)(2,1)S(1)} %mix.6), channel_id=1, source_target_pairs={{0,2},{1,3},{2,0},{3,1},{4,6},{5,7},{6,4},{7,5},{8,10},{9,11},{10,... | collective-permute-start | bytes 61448 | tf_op jit(solution)/shard_map/ppermute | solution.py:328
  43.6 0.0 collective-permute-done.9.refs_2_
  43.6 0.7 %mix.7.refs_3_ = bf16[80,128]{1,0:T(8,128)(2,1)S(1)} custom-call(bf16[3,128,512]{2,1,0:T(8,128)(2,1)S(1)} %get-tuple-element.33.refs_0_, bf16[3,128,512]{2,1,0:T(8,128)(2,1)S(1)} %collective-permute-done.refs_1_, bf16[1,128,512]{2,1,0:T(8,128)(2,1)S(1)} %collective-permute-done.1.refs_2_, bf16[1,128,512]{2,1,0:T(8,128)(2,1)S(1)} %collective-permute-done.2.refs_3_, ...), custom_call_target="tpu_custom_call" | custom-call | flops 100663296 | bytes 1048576 | tf_op jit(solution)/shard_map/mix/pallas_call | solution.py:286
  44.2 0.9 %collective-permute-done.7.refs_0_ = bf16[80,128]{1,0:T(8,128)(2,1)S(1)} collective-permute-done((bf16[80,128]{1,0:T(8,128)(2,1)S(1)}, bf16[80,128]{1,0:T(8,128)(2,1)S(1)}, u32[]{:S(2)}, u32[]{:S(2)}) %collective-permute-start.7) | collective-permute-done | bytes 20512 | tf_op jit(solution)/shard_map/ppermute | solution.py:328
  45.1 2.5 %collective-permute-done.8.refs_1_ = bf16[80,128]{1,0:T(8,128)(2,1)S(1)} collective-permute-done((bf16[80,128]{1,0:T(8,128)(2,1)S(1)}, bf16[80,128]{1,0:T(8,128)(2,1)S(1)}, u32[]{:S(2)}, u32[]{:S(2)}) %collective-permute-start.8) | collective-permute-done | bytes 20512 | tf_op jit(solution)/shard_map/ppermute | solution.py:328
  47.6 0.1 loss.1
  47.7 10.3 %all_to_all.5 = f32[32,1,128]{2,1,0:T(1,128)S(1)} all-to-all(f32[32,1,128]{2,1,0:T(1,128)S(1)} %loss.1), channel_id=1, replica_groups=mesh['dp'=8,'seq'=4] {'dp','seq'}, dimensions={0} | all-to-all | bytes 32768 | tf_op jit(solution)/shard_map/all_to_all | solution.py:401
  58.0 0.7 %pick.1 = f32[1,8]{1,0:T(1,128)} custom-call(f32[8,4,128]{2,1,0:T(4,128)S(1)} %bitcast.7, s32[1,8]{1,0:T(1,128)S(1)} %bitcast.8), custom_call_target="tpu_custom_call" | custom-call | tf_op jit(solution)/shard_map/pick/pallas_call | solution.py:286
  (13 shorter events, 0.0 us)
Async XLA Ops:
  0.0 11.3 %copy-start.1 = (s32[8]{0:T(128)S(1)}, s32[8]{0:T(128)}, u32[]{:S(2)}) copy-start(s32[8]{0:T(128)} %param.18) | copy-start | bytes 100
  0.0 11.4 %copy-start.3 = (s32[1,8]{1,0:T(1,128)S(1)}, s32[1,8]{1,0:T(1,128)}, u32[]{:S(2)}) copy-start(s32[1,8]{1,0:T(1,128)} %param.17) | copy-start | bytes 100
  0.0 11.4 %copy-start.2 = (s32[8]{0:T(128)S(1)}, s32[8]{0:T(128)}, u32[]{:S(2)}) copy-start(s32[8]{0:T(128)} %param.16) | copy-start | bytes 100
  1.0 24.5 %collective-permute-start.4 = (bf16[1,128,512]{2,1,0:T(8,128)(2,1)S(1)}, bf16[1,128,512]{2,1,0:T(8,128)(2,1)S(1)}, u32[]{:S(2)}, u32[]{:S(2)}) collective-permute-start(bf16[1,128,512]{2,1,0:T(8,128)(2,1)S(1)} %get-tuple-element.40), channel_id=1, source_target_pairs={{0,3},{1,2},{2,1},{3,0},{4,7},{5,6},{6,5},{7,4},{8,11},{9,10},{10,... | collective-permute-start | bytes 393224 | tf_op jit(solution)/shard_map/ppermute | solution.py:328
  6.2 23.2 %collective-permute-start.3 = (bf16[1,128,512]{2,1,0:T(8,128)(2,1)S(1)}, bf16[1,128,512]{2,1,0:T(8,128)(2,1)S(1)}, u32[]{:S(2)}, u32[]{:S(2)}) collective-permute-start(bf16[1,128,512]{2,1,0:T(8,128)(2,1)S(1)} %get-tuple-element.31), channel_id=1, source_target_pairs={{0,2},{1,3},{2,0},{3,1},{4,6},{5,7},{6,4},{7,5},{8,10},{9,11},{10,... | collective-permute-start | bytes 393224 | tf_op jit(solution)/shard_map/ppermute | solution.py:328
  7.6 26.3 %collective-permute-start.5 = (bf16[1,128,512]{2,1,0:T(8,128)(2,1)S(1)}, bf16[1,128,512]{2,1,0:T(8,128)(2,1)S(1)}, u32[]{:S(2)}, u32[]{:S(2)}) collective-permute-start(bf16[1,128,512]{2,1,0:T(8,128)(2,1)S(1)} %get-tuple-element.41), channel_id=1, source_target_pairs={{0,2},{1,3},{2,0},{3,1},{4,6},{5,7},{6,4},{7,5},{8,10},{9,11},{10,... | collective-permute-start | bytes 393224 | tf_op jit(solution)/shard_map/ppermute | solution.py:328
  10.6 23.4 %collective-permute-start.6 = (bf16[1,128,512]{2,1,0:T(8,128)(2,1)S(1)}, bf16[1,128,512]{2,1,0:T(8,128)(2,1)S(1)}, u32[]{:S(2)}, u32[]{:S(2)}) collective-permute-start(bf16[1,128,512]{2,1,0:T(8,128)(2,1)S(1)} %get-tuple-element.42), channel_id=1, source_target_pairs={{0,3},{1,2},{2,1},{3,0},{4,7},{5,6},{6,5},{7,4},{8,11},{9,10},{10,... | collective-permute-start | bytes 393224 | tf_op jit(solution)/shard_map/ppermute | solution.py:328
  10.7 18.8 %collective-permute-start = (bf16[3,128,512]{2,1,0:T(8,128)(2,1)S(1)}, bf16[3,128,512]{2,1,0:T(8,128)(2,1)S(1)}, u32[]{:S(2)}, u32[]{:S(2)}) collective-permute-start(bf16[3,128,512]{2,1,0:T(8,128)(2,1)S(1)} %get-tuple-element.34), channel_id=1, source_target_pairs={{0,1},{1,0},{2,3},{3,2},{4,5},{5,4},{6,7},{7,6},{8,9},{9,8},{10,11... | collective-permute-start | bytes 1179656 | tf_op jit(solution)/shard_map/ppermute | solution.py:328
  25.6 12.4 %collective-permute-start.1 = (bf16[1,128,512]{2,1,0:T(8,128)(2,1)S(1)}, bf16[1,128,512]{2,1,0:T(8,128)(2,1)S(1)}, u32[]{:S(2)}, u32[]{:S(2)}) collective-permute-start(bf16[1,128,512]{2,1,0:T(8,128)(2,1)S(1)} %get-tuple-element.38), channel_id=1, source_target_pairs={{0,2},{1,3},{2,0},{3,1},{4,6},{5,7},{6,4},{7,5},{8,10},{9,11},{10,... | collective-permute-start | bytes 393224 | tf_op jit(solution)/shard_map/ppermute | solution.py:328
  29.4 9.3 %collective-permute-start.2 = (bf16[1,128,512]{2,1,0:T(8,128)(2,1)S(1)}, bf16[1,128,512]{2,1,0:T(8,128)(2,1)S(1)}, u32[]{:S(2)}, u32[]{:S(2)}) collective-permute-start(bf16[1,128,512]{2,1,0:T(8,128)(2,1)S(1)} %get-tuple-element.39), channel_id=1, source_target_pairs={{0,3},{1,2},{2,1},{3,0},{4,7},{5,6},{6,5},{7,4},{8,11},{9,10},{10,... | collective-permute-start | bytes 393224 | tf_op jit(solution)/shard_map/ppermute | solution.py:328
  38.7 4.9 %collective-permute-start.9 = (bf16[80,128]{1,0:T(8,128)(2,1)S(1)}, bf16[80,128]{1,0:T(8,128)(2,1)S(1)}, u32[]{:S(2)}, u32[]{:S(2)}) collective-permute-start(bf16[80,128]{1,0:T(8,128)(2,1)S(1)} %mix.4), channel_id=1, source_target_pairs={{0,1},{1,0},{2,3},{3,2},{4,5},{5,4},{6,7},{7,6},{8,9},{9,8},{10,11... | collective-permute-start | bytes 61448 | tf_op jit(solution)/shard_map/ppermute | solution.py:328
  39.4 5.7 %collective-permute-start.7 = (bf16[80,128]{1,0:T(8,128)(2,1)S(1)}, bf16[80,128]{1,0:T(8,128)(2,1)S(1)}, u32[]{:S(2)}, u32[]{:S(2)}) collective-permute-start(bf16[80,128]{1,0:T(8,128)(2,1)S(1)} %mix.5), channel_id=1, source_target_pairs={{0,3},{1,2},{2,1},{3,0},{4,7},{5,6},{6,5},{7,4},{8,11},{9,10},{10,... | collective-permute-start | bytes 61448 | tf_op jit(solution)/shard_map/ppermute | solution.py:328
  42.8 15.2 %copy-start = (s32[8]{0:T(128)S(1)}, s32[8]{0:T(128)}, u32[]{:S(2)}) copy-start(s32[8]{0:T(128)} %param.23) | copy-start | bytes 100
  42.8 4.7 %collective-permute-start.8 = (bf16[80,128]{1,0:T(8,128)(2,1)S(1)}, bf16[80,128]{1,0:T(8,128)(2,1)S(1)}, u32[]{:S(2)}, u32[]{:S(2)}) collective-permute-start(bf16[80,128]{1,0:T(8,128)(2,1)S(1)} %mix.6), channel_id=1, source_target_pairs={{0,2},{1,3},{2,0},{3,1},{4,6},{5,7},{6,4},{7,5},{8,10},{9,11},{10,... | collective-permute-start | bytes 61448 | tf_op jit(solution)/shard_map/ppermute | solution.py:328
